TPU v7x, 256 devices: a whole 4x4x8 slice. The times are simulated.
256 devices in a mesh: blk: 8 (over y, core), kvh: 4 (over z_lo), dec: 8 (over x, z_hi).
Axes of the slice: x: 4, y: 4, z: 8 (z_hi: 2, z_lo: 4; z = z_hi * 4 + z_lo), core: 2. Of those that a mesh axis runs over, the one named last changes fastest.
Arguments:
- queries: bfloat16 [8192, 8192], P('blk', ('kvh', 'dec')), may hold values from -6 to 6
- keys: bfloat16 [8192, 1024], P(('blk', 'dec'), 'kvh'), may hold values from -6 to 6
- values: bfloat16 [8192, 1024], P(('blk', 'dec'), 'kvh'), may hold values from -6 to 6
- page_slot: int32 [64], replicated, may hold values from 0 to 127, as said below
Outputs:
- attended: bfloat16 [8192, 8192], P('blk', ('kvh', 'dec'))
- cache_keys: bfloat16 [16384, 1024], P(('blk', 'dec'), 'kvh')
- cache_values: bfloat16 [16384, 1024], P(('blk', 'dec'), 'kvh')
- key_scales: float32 [128, 8], P(('blk', 'dec'), 'kvh')
- value_scales: float32 [128, 8], P(('blk', 'dec'), 'kvh')
Inputs may be any that keep to these rules, and one draw needn't show every extreme that they name: `page_slot`: the values are distinct; slot s belongs to decode owner s // 2 (its index along blk+dec) as its slot s % 2.
All inputs are finite; a program needn't handle non-finite values. Where the computation divides by a largest or mean magnitude, that divisor is 1e-20 or more.
Results may differ from a plain program's by a relative error of at most 0.0045.
Values may be sent and summed in bfloat16 or wider, within the bound.
No kernel may reach another device: no remote copies, remote signals or barrier semaphores. Data moves between devices by JAX's collectives and lax.ppermute only.
A program may use at most 256 MiB of HBM per device.

v0:
```python
import jax
import jax.numpy as jnp
from jax import lax
from jax.sharding import PartitionSpec as P

HEADS = 64
KVH = 8
HD = 128
PAGE = 128


def normalize_pages(rows):
    count = rows.shape[0] // PAGE
    local_heads = rows.shape[1] // HD
    pages = rows.reshape(count, PAGE, local_heads, HD).astype(jnp.float32)
    scale = jnp.max(jnp.abs(pages), axis=(1, 3)) + 1e-06
    normed = (pages / scale[:, None, :, None]).astype(jnp.bfloat16)
    return (normed.reshape(count, PAGE * local_heads * HD), scale)


def body(queries, keys, values, page_slot):
    group = HEADS // KVH
    tok_rows = queries.shape[0]
    head_count = queries.shape[1] // HD
    local_heads = keys.shape[1] // HD
    slots = 2 * keys.shape[0] // PAGE
    q_heads = queries.reshape(tok_rows, head_count, HD)
    q_first = lax.axis_index("blk") * tok_rows
    q_pos = q_first + jnp.arange(tok_rows)
    head_groups = (lax.axis_index("dec") * head_count + jnp.arange(head_count)) // group
    slot_base = lax.axis_index(("blk", "dec")) * slots + jnp.arange(slots)
    page_width = PAGE * local_heads * HD
    empty_cache = (
        jnp.zeros((slots, page_width), jnp.float32),
        jnp.zeros((slots, page_width), jnp.float32),
        jnp.zeros((slots, local_heads), jnp.float32),
        jnp.zeros((slots, local_heads), jnp.float32),
    )
    empty_state = (
        jnp.full((head_count, tok_rows), -1e30, jnp.float32),
        jnp.zeros((head_count, tok_rows), jnp.float32),
        jnp.zeros((head_count, tok_rows, HD), jnp.float32),
    )
    k_rows = lax.all_gather(keys, ("blk", "dec"), axis=0, tiled=True)
    v_rows = lax.all_gather(values, ("blk", "dec"), axis=0, tiled=True)
    count = k_rows.shape[0]
    width = k_rows.shape[1] // HD

    def compute(inner):
        running, total, accum = inner
        k_sel = jnp.take(k_rows.reshape(count, width, HD), head_groups, axis=1)
        v_sel = jnp.take(v_rows.reshape(count, width, HD), head_groups, axis=1)
        scores = jnp.einsum(
            "thd,nhd->htn", q_heads, k_sel, preferred_element_type=jnp.float32
        ) * HD ** (-0.5)
        allowed = jnp.arange(count)[None, :] <= q_pos[:, None]
        scores = jnp.where(allowed[None], scores, -1e30)
        newmax = jnp.maximum(running, jnp.max(scores, axis=2))
        expd = jnp.where(allowed[None], jnp.exp(scores - newmax[:, :, None]), 0.0)
        total = jnp.sum(expd, axis=2)
        mixed = jnp.einsum(
            "htn,nhd->htd", expd.astype(jnp.bfloat16), v_sel, preferred_element_type=jnp.float32
        )
        return (newmax, total, mixed)

    attention = lax.cond(
        jnp.int32(0) <= q_first + tok_rows - 1, compute, lambda inner: inner, empty_state
    )
    own_k, own_ks = normalize_pages(keys)
    own_v, own_vs = normalize_pages(values)
    own_k, own_v, own_ks, own_vs = (own_k, own_v, own_ks, own_vs)
    normed_k = lax.all_gather(own_k, ("blk", "dec"), axis=0, tiled=True)
    picked = page_slot[None, :] == slot_base[:, None]
    pick_half = picked.astype(jnp.bfloat16)
    pick_full = picked.astype(jnp.float32)
    accum = attention[2] / attention[1][:, :, None]
    attended = (
        jnp.transpose(accum, (1, 0, 2)).reshape(tok_rows, head_count * HD).astype(jnp.bfloat16)
    )
    cache_keys = (
        jnp.dot(pick_half, normed_k, preferred_element_type=jnp.float32)
        .astype(jnp.bfloat16)
        .reshape(slots * PAGE, local_heads * HD)
    )
    cache_values = (
        jnp.dot(
            pick_half,
            lax.all_gather(own_v, ("blk", "dec"), axis=0, tiled=True),
            preferred_element_type=jnp.float32,
        )
        .astype(jnp.bfloat16)
        .reshape(slots * PAGE, local_heads * HD)
    )
    return (
        attended,
        cache_keys,
        cache_values,
        empty_cache[2]
        + jnp.dot(
            pick_full,
            lax.all_gather(own_ks.astype(jnp.bfloat16), ("blk", "dec"), axis=0, tiled=True).astype(
                jnp.float32
            ),
            precision=lax.Precision.HIGHEST,
        ),
        empty_cache[3]
        + jnp.dot(
            pick_full,
            lax.all_gather(own_vs.astype(jnp.bfloat16), ("blk", "dec"), axis=0, tiled=True).astype(
                jnp.float32
            ),
            precision=lax.Precision.HIGHEST,
        ),
    )


def solution(mesh):
    return jax.shard_map(
        body,
        mesh=mesh,
        in_specs=(
            P("blk", ("kvh", "dec")),
            P(("blk", "dec"), "kvh"),
            P(("blk", "dec"), "kvh"),
            P(),
        ),
        out_specs=(
            P("blk", ("kvh", "dec")),
            P(("blk", "dec"), "kvh"),
            P(("blk", "dec"), "kvh"),
            P(("blk", "dec"), "kvh"),
            P(("blk", "dec"), "kvh"),
        ),
        check_vma=False,
    )
```

profile of v0, /device:TPU:17, one launch (start us, length us, event | category | flops | bytes accessed | tf_op | source)
XLA Modules:
  0.0 564.4 jit_solution(9185042878105522672)
XLA Ops:
  7.2 0.9 fusion.29
  13.2 1.6 copy.33
  14.8 1.6 copy.32
  16.4 1.3 dynamic-slice
  18.8 192.1 %all-reduce.2 = (bf16[128]{0:T(256)(128)(2,1)S(1)}, bf16[128]{0:T(256)(128)(2,1)S(1)}) all-reduce(bf16[128]{0:T(256)(128)(2,1)S(1)} %dynamic-update-slice, bf16[128]{0:T(256)(128)(2,1)S(1)} %dynamic-update-slice.1), channel_id=2, replica_groups=mesh['blk'=8,'kvh'=4,'dec'=8] {'blk','dec'}, use_global_device_ids=true, to_apply=%add | all-reduce | flops 256 | bytes 1024
  211.2 1.4 fusion.31
  212.6 1.4 fusion.33
  214.0 7.9 %convolution_convert_fusion.1 = bf16[2,32768]{1,0:T(2,128)(2,1)S(1)} fusion(bf16[64,1,32768]{2,1,0:T(2,128)(2,1)} %all-gather.13.cloned.1.call-done, s32[64]{0:T(128)} %param.11, s32[2]{0:T(128)S(1)} %iota_add_fusion), kind=kOutput, calls=%fused_computation.42 | convolution fusion | flops 8454272 | bytes 4325640 | tf_op jit(solution)/shard_map/dot_general | solution.py:81
  222.7 19.5 %all-gather.15.cloned.1.call-done = bf16[64,1,32768]{2,1,0:T(2,128)(2,1)} async-done(((bf16[1,1,32768]{2,1,0:T(2,128)(2,1)}), bf16[64,1,32768]{2,1,0:T(2,128)(2,1)}) %all-gather.15.cloned.1.call-update) | async-done | bytes 4194320 | tf_op jit(solution)/shard_map/all_gather | solution.py:88
  242.2 7.9 %convolution_convert_fusion = bf16[2,32768]{1,0:T(2,128)(2,1)S(1)} fusion(bf16[64,1,32768]{2,1,0:T(2,128)(2,1)} %all-gather.15.cloned.1.call-done, s32[64]{0:T(128)S(1)} %copy-done.1, s32[2]{0:T(128)S(1)} %iota_add_fusion), kind=kOutput, calls=%fused_computation.41 | convolution fusion | flops 8454272 | bytes 4325640 | tf_op jit(solution)/shard_map/dot_general | solution.py:86
  250.8 90.7 %all-gather.11.cloned.1.call-done = bf16[8192,256]{0,1:T(8,128)(2,1)} async-done(((bf16[128,256]{0,1:T(8,128)(2,1)}), bf16[8192,256]{0,1:T(8,128)(2,1)}) %all-gather.11.cloned.1.call-update) | async-done | bytes 4194320 | tf_op jit(solution)/shard_map/all_gather | solution.py:45
  341.5 99.7 %all-gather.9.cloned.1.call-done = bf16[8192,256]{0,1:T(8,128)(2,1)} async-done(((bf16[128,256]{0,1:T(8,128)(2,1)}), bf16[8192,256]{0,1:T(8,128)(2,1)}) %all-gather.9.cloned.1.call-update) | async-done | bytes 4194320 | tf_op jit(solution)/shard_map/all_gather | solution.py:44
  441.3 115.5 %conditional.1 = (f32[2,1024]{1,0:T(2,128)S(1)}, f32[2,1024,128]{2,1,0:T(8,128)S(1)}) conditional(s32[]{:T(128)} %convert_element_type.119, () %tuple.34, (s32[]{:T(128)}, s32[1024]{0:T(1024)S(1)}, bf16[8192,256]{0,1:T(8,128)(2,1)}, s32[]{:T(128)}, s32[2]{0:T(128)S(1)}, /*index=5*/s32[]{:T(128)}, bf16[1024,256]{1,0:T(8,128)(2,1)}, ...), branch_computations={%region_0.1_spmd, %region_1.5_spmd.clone} | conditional | flops 8837398528 | bytes 288948352 | solution.py:66
  441.3 3.9 fusion.48
  445.2 3.6 gather_fusion.1
  448.8 2.0 gather_fusion
  450.8 11.1 %iota_compare_fusion = pred[1024,8192]{0,1:T(8,128)(4,1)} fusion(s32[1024]{0:T(1024)S(1)} %broadcast_add_fusion), kind=kLoop, calls=%fused_computation.9 | loop fusion | flops 8388608 | bytes 8392704 | tf_op jit(solution)/shard_map/cond/branch_1_fun/le | solution.py:56
  461.9 27.8 %fusion = (f32[2,1024]{1,0:T(2,128)S(1)}, f32[2,8192,1024]{2,1,0:T(8,128)}) fusion(pred[1024,8192]{0,1:T(8,128)(4,1)} %iota_compare_fusion, bf16[4096,2,128]{0,2,1:T(8,128)(2,1)S(1)} %bitcast.61, bf16[4096,2,128]{0,2,1:T(8,128)(2,1)} %bitcast.62, pred[2]{0:T(512)(128)(4,1)S(1)} %get-tuple-element.190, bf16[1024,256]{1,0:T(8,128)(2,1)S(1)} %copy-done.2), kind=kOutput, calls=%fused_computation.6 | convolution fusion | flops 4355782656 | bytes 80224256 | tf_op jit(solution)/shard_map/cond/branch_1_fun/thd,nhd->htn/dot_general | solution.py:53
  489.7 4.0 fusion.47
  493.7 3.6 gather_fusion.2
  497.3 2.0 gather_fusion.3
  499.3 33.1 %fusion.3 = f32[2,1024,128]{2,1,0:T(8,128)S(1)} fusion(f32[2,8192,1024]{2,1,0:T(8,128)} %get-tuple-element.197, f32[2,1024]{1,0:T(2,128)S(1)} %broadcast_maximum_fusion, pred[1024,8192]{0,1:T(8,128)(4,1)} %iota_compare_fusion, bf16[4096,2,128]{0,2,1:T(8,128)(2,1)} %bitcast.64, bf16[4096,2,128]{0,2,1:T(8,128)(2,1)} %bitcast.63, ...), kind=kOutput, calls=%fused_computation.10 | convolution fusion | flops 4389339136 | bytes 80748544 | tf_op jit(solution)/shard_map/cond/branch_1_fun/htn,nhd->htd/dot_general | solution.py:61
  532.4 24.3 %fusion.2 = f32[2,1024]{1,0:T(2,128)S(1)} fusion(f32[2,8192,1024]{2,1,0:T(8,128)} %get-tuple-element.197, f32[2,1024]{1,0:T(2,128)S(1)} %broadcast_maximum_fusion, pred[1024,8192]{0,1:T(8,128)(4,1)} %iota_compare_fusion), kind=kLoop, calls=%fused_computation.8 | loop fusion | flops 83884032 | bytes 75513856 | tf_op jit(solution)/shard_map/cond/branch_1_fun/reduce_sum | solution.py:60
  556.7 1.1 copy_bitcast_fusion
  (43 shorter events, 7.4 us)
Async XLA Ops:
  7.2 235.0 %copy-start.1 = (s32[64]{0:T(128)S(1)}, s32[64]{0:T(128)}, u32[]{:S(2)}) copy-start(s32[64]{0:T(128)} %param.11) | copy-start | bytes 772
  7.2 206.9 %all-gather.13.cloned.1.call-start = ((), (), s32[]{:S(2)}) async-start(), calls=%async_computation.2 | async-start | bytes 8519680 | tf_op jit(solution)/shard_map/all_gather | solution.py:72
  10.1 232.1 %all-gather.15.cloned.1.call-start = ((), (), s32[]{:S(2)}) async-start(), calls=%async_computation.3 | async-start | bytes 8519680 | tf_op jit(solution)/shard_map/all_gather | solution.py:88
  13.1 328.4 %all-gather.11.cloned.1.call-start = ((), (), s32[]{:S(2)}) async-start(), calls=%async_computation.1 | async-start | bytes 4259840 | tf_op jit(solution)/shard_map/all_gather | solution.py:45
  14.7 426.5 %all-gather.9.cloned.1.call-start = ((), (), s32[]{:S(2)}) async-start(), calls=%async_computation | async-start | bytes 4259840 | tf_op jit(solution)/shard_map/all_gather | solution.py:44
  450.8 11.1 %copy-start = (bf16[2,4096,128]{1,2,0:T(8,128)(2,1)S(1)}, bf16[2,4096,128]{1,2,0:T(8,128)(2,1)}, u32[]{:S(2)}) copy-start(bf16[2,4096,128]{1,2,0:T(8,128)(2,1)} %gather_fusion.1) | copy-start | bytes 6291460 | tf_op jit(solution)/shard_map/cond
  450.8 11.1 %copy-start.2 = (bf16[1024,256]{1,0:T(8,128)(2,1)S(1)}, bf16[1024,256]{1,0:T(8,128)(2,1)}, u32[]{:S(2)}) copy-start(bf16[1024,256]{1,0:T(8,128)(2,1)} %get-tuple-element.174) | copy-start | bytes 1572868 | tf_op jit(solution)/shard_map/cond
Sparse Core Ops, SparseCore 0:
  12.2 116.8 all-gather.12
  133.2 108.9 all-gather.14
  245.5 95.9 all-gather.10
  344.7 96.4 all-gather.8
where the time goes:
time: 566 us; the launch traced here: 564 us
  waiting for transfers between devices  210 us (37%)
  blocking collectives  192 us (34%)
  matrix products  79.5 us (14%)
  other arithmetic  41.8 us (7%)
  local copies, waits for them, and re-layouts  26.2 us (5%)
  between operations  14.5 us (3%)
    unnamed x1, blocking collectives  192 us
    all_gather x1, waiting for transfers between devices, body(): k_rows = lax.all_gather(keys, ('blk', 'dec'), axis=0, tiled=True)  99.7 us
    all_gather x1, waiting for transfers between devices, body(): v_rows = lax.all_gather(values, ('blk', 'dec'), axis=0, tiled=True)  90.7 us
    dot_general x1, matrix products, compute(): jnp.einsum('htn,nhd->htd', expd.astype(jnp.bfloat16), v_sel, preferred_el...  33.1 us
    dot_general x1, matrix products, compute(): jnp.einsum('thd,nhd->htn', q_heads, k_sel, preferred_element_type=jnp.flo...  27.8 us
    reduce_sum x1, other arithmetic, compute(): total = jnp.sum(expd, axis=2)  24.3 us
    all_gather x1, waiting for transfers between devices, body(): lax.all_gather(own_v, ('blk', 'dec'), axis=0, tiled=True)  19.5 us
  transfers between devices with their start and end apart: 4, of which 3 were waited for; matrix products, arithmetic and copies ran while one was open for 5% of the time, Pallas kernels for 0%

commit v1 on v0

v1 whole, which is shorter than its diff:
```python
import functools

import jax
import jax.numpy as jnp
import numpy as np
from jax import lax
from jax.experimental import pallas as pl
from jax.experimental.pallas import tpu as pltpu
from jax.sharding import PartitionSpec as P

HEADS = 64
KVH = 8
HD = 128
PAGE = 128
TQ = 256
SEG = 512
C = float(np.log2(np.e) / np.sqrt(HD))
NEG = -1e30
LIMIT = 80.0
NT = (((1,), (1,)), ((), ()))


def row_norm(x):
    x = x.astype(jnp.float32)
    return jnp.sqrt(jnp.sum(x * x, axis=1, keepdims=True))


def first_kernel(meta, q_ref, e0, e1, acc_ref, stat_ref):
    rows = q_ref.shape[0]
    core, dec = meta[0], meta[1]
    half = rows // 2
    acc_ref[...] = jnp.zeros_like(acc_ref)
    stat_ref[...] = jnp.zeros_like(stat_ref)
    for h in range(2):
        stat_ref[:, h : h + 1] = jnp.full((rows, 1), NEG, jnp.float32)
        stat_ref[:, 4 + h : 5 + h] = row_norm(q_ref[:, h * HD : (h + 1) * HD])

    def tile(i, _):
        r = pl.ds(pl.multiple_of(i * TQ, TQ), TQ)
        q_pos = i * TQ + lax.broadcasted_iota(jnp.int32, (TQ, 1), 0)
        lane = lax.broadcasted_iota(jnp.int32, (1, SEG), 1)
        ok = []
        for z in range(2):
            page = jnp.bitwise_xor(2 * (lane // PAGE) + z, dec)
            ok.append(core * half + page * PAGE + lane % PAGE <= q_pos)
        allowed = jnp.concatenate(ok, axis=1)
        k = jnp.concatenate([e0[:, :HD], e1[:, :HD]], axis=0)
        v = jnp.concatenate([e0[:, HD:], e1[:, HD:]], axis=0)
        for h in range(2):
            q = q_ref[r, h * HD : (h + 1) * HD]
            s = lax.dot_general(q, k, NT, preferred_element_type=jnp.float32) * C
            s = jnp.where(allowed, s, NEG)
            m = jnp.max(s, axis=1, keepdims=True)
            p = jnp.where(allowed, jnp.exp2(s - m), 0.0)
            acc_ref[r, h * HD : (h + 1) * HD] = jnp.dot(
                p.astype(jnp.bfloat16), v, preferred_element_type=jnp.float32
            )
            stat_ref[r, h : h + 1] = m
            stat_ref[r, 2 + h : 3 + h] = jnp.sum(p, axis=1, keepdims=True)
        return 0

    lax.fori_loop(core * (half // TQ), rows // TQ, tile, 0)


def next_kernel(n, meta, q_ref, *refs):
    segs, acc_in, stat_in, acc_ref, stat_ref = refs[:n], *refs[n:]
    del acc_in, stat_in
    rows = q_ref.shape[0]

    def fast(seg):
        def tile(i, _):
            r = pl.ds(pl.multiple_of(i * TQ, TQ), TQ)
            for h in range(2):
                cols = slice(h * HD, (h + 1) * HD)
                s = lax.dot_general(
                    q_ref[r, cols], seg[:, :HD], NT, preferred_element_type=jnp.float32
                )
                p = jnp.exp2(s * C - stat_ref[r, h : h + 1])
                stat_ref[r, 2 + h : 3 + h] += jnp.sum(p, axis=1, keepdims=True)
                acc_ref[r, cols] += jnp.dot(
                    p.astype(jnp.bfloat16), seg[:, HD:], preferred_element_type=jnp.float32
                )
            return 0

        lax.fori_loop(0, rows // TQ, tile, 0)

    def slow(seg):
        def tile(i, _):
            r = pl.ds(pl.multiple_of(i * TQ, TQ), TQ)
            for h in range(2):
                cols = slice(h * HD, (h + 1) * HD)
                s = C * lax.dot_general(
                    q_ref[r, cols], seg[:, :HD], NT, preferred_element_type=jnp.float32
                )
                old = stat_ref[r, h : h + 1]
                m = jnp.maximum(old, jnp.max(s, axis=1, keepdims=True))
                p = jnp.exp2(s - m)
                a = jnp.exp2(old - m)
                stat_ref[r, h : h + 1] = m
                stat_ref[r, 2 + h : 3 + h] = a * stat_ref[r, 2 + h : 3 + h] + jnp.sum(
                    p, axis=1, keepdims=True
                )
                acc_ref[r, cols] = a * acc_ref[r, cols] + jnp.dot(
                    p.astype(jnp.bfloat16), seg[:, HD:], preferred_element_type=jnp.float32
                )
            return 0

        lax.fori_loop(0, rows // TQ, tile, 0)

    for j, seg in enumerate(segs):

        @pl.when(meta[j] > 0)
        def _():
            longest = jnp.max(row_norm(seg[:, :HD])) * (1.01 * C)
            st = stat_ref[...]
            top = jnp.max(st[:, 4:6] * longest - st[:, 0:2])

            @pl.when(top <= LIMIT)
            def _():
                fast(seg)

            @pl.when(jnp.logical_not(top <= LIMIT))
            def _():
                slow(seg)


def merge_kernel(mine, theirs, ml_mine, ml_theirs, out_ref):
    for h in range(2):
        cols = slice(h * HD, (h + 1) * HD)
        m0, m1 = ml_mine[:, h : h + 1], ml_theirs[:, h : h + 1]
        m = jnp.maximum(m0, m1)
        a0, a1 = jnp.exp2(m0 - m), jnp.exp2(m1 - m)
        total = a0 * ml_mine[:, 2 + h : 3 + h] + a1 * ml_theirs[:, 2 + h : 3 + h]
        mixed = a0 * mine[:, cols] + a1 * theirs[:, cols]
        out_ref[:, cols] = (mixed / total).astype(jnp.bfloat16)


def pick_kernel(meta, *refs):
    pages, outs = refs[:8], refs[8:]
    for d in range(4):
        for j in range(2):
            at = meta[2 * d + j]
            for b in range(8):

                @pl.when(at // 4 == b)
                def _():
                    rows = pl.ds(pl.multiple_of((at % 4) * PAGE, PAGE), PAGE)
                    outs[d][j * PAGE : (j + 1) * PAGE] = pages[b][rows]


def cache_kernel(meta, own, own_c, oth, oth_c, ck, cv, ks, vs):
    col = meta[0]
    scales = [jnp.zeros((2, 2), jnp.float32)] * 2
    row_at = lax.broadcasted_iota(jnp.int32, (2, 2), 0)
    col_at = lax.broadcasted_iota(jnp.int32, (2, 2), 1)
    for j in range(2):
        filled, same = meta[1 + j] > 0, meta[3 + j] > 0
        rows = slice(j * PAGE, (j + 1) * PAGE)
        blocks = [
            jnp.where(same, own[rows], own_c[rows]),
            jnp.where(same, oth[rows], oth_c[rows]),
        ]
        for kind, out in enumerate((ck, cv)):
            normed = []
            for b in range(2):
                x = blocks[b][:, kind * HD : (kind + 1) * HD].astype(jnp.float32)
                x = jnp.where(filled, x, 0.0)
                scale = jnp.max(jnp.abs(x)) + 1e-6
                normed.append((x / scale).astype(jnp.bfloat16))
                here = jnp.logical_and(row_at == j, col_at == (col if b == 0 else 1 - col))
                scales[kind] = jnp.where(jnp.logical_and(here, filled), scale, scales[kind])
            out[rows, :HD] = jnp.where(col == 0, normed[0], normed[1])
            out[rows, HD:] = jnp.where(col == 0, normed[1], normed[0])
    ks[...] = scales[0]
    vs[...] = scales[1]


VMEM = pl.BlockSpec(memory_space=pltpu.VMEM)
SMEM = pl.BlockSpec(memory_space=pltpu.SMEM)
PARAMS = pltpu.CompilerParams(vmem_limit_bytes=48 * 2**20)


def call(kernel, meta, arrays, outs, **more):
    return pl.pallas_call(
        kernel,
        in_specs=[SMEM] + [VMEM] * len(arrays),
        out_specs=[VMEM] * len(outs),
        out_shape=[jax.ShapeDtypeStruct(s, t) for s, t in outs],
        compiler_params=PARAMS,
        **more,
    )(meta, *arrays)


def body(queries, keys, values, page_slot):
    blk, dec = lax.axis_index("blk"), lax.axis_index("dec")
    y, core, head = blk // 2, blk % 2, dec // 4
    tok = queries.shape[0]
    i32 = jnp.int32

    def over_dec(x, m):
        return lax.ppermute(x, "dec", [(i, i ^ m) for i in range(8)])

    def over_core(x):
        return lax.ppermute(x, "blk", [(i, i ^ 1) for i in range(8)])

    def over_y(x, d):
        return lax.ppermute(x, "blk", [(i, (i + 2 * d) % 8) for i in range(8)])

    first = jnp.concatenate([keys[:, :HD], values[:, :HD]], axis=1)
    second = jnp.concatenate([keys[:, HD:], values[:, HD:]], axis=1)
    own = jnp.where(head == 0, first, second)
    other = jnp.where(head == 0, second, first)

    def spread(own, other):
        return jnp.concatenate(
            [own, over_dec(own, 2), over_dec(other, 4), over_dec(other, 6)], axis=0
        )

    across = over_dec(jnp.concatenate([own, other], axis=0), 1)
    e0 = spread(own, other)
    e1 = spread(across[:PAGE], across[PAGE:])
    parts = []
    for e in (e0, e1):
        parts.append((over_y(e, 1), over_y(e, 3), over_y(e, 2)))
    (a0, b0, c0), (a1, b1, c1) = parts

    q_there = over_core(queries)
    q = jnp.where(
        core == 0,
        jnp.concatenate([queries, q_there], axis=0),
        jnp.concatenate([q_there, queries], axis=0),
    )
    state = [((2 * tok, 2 * HD), jnp.float32), ((2 * tok, 8), jnp.float32)]
    acc, stat = call(first_kernel, jnp.stack([core, dec]).astype(i32), [q, e0, e1], state)

    def more(flags, segs, acc, stat):
        n = len(segs)
        return call(
            functools.partial(next_kernel, n),
            jnp.stack(flags).astype(i32),
            [q, *segs, acc, stat],
            state,
            input_output_aliases={n + 2: 0, n + 3: 1},
        )

    below, above, far = y >= 1, y == 3, y >= 2
    acc, stat = more([below, above], [a0, b0], acc, stat)
    acc, stat = more([below, above, far], [a1, b1, c0], acc, stat)
    acc, stat = more([far], [c1], acc, stat)
    lo, hi = slice(0, tok), slice(tok, 2 * tok)
    acc_mine = jnp.where(core == 0, acc[lo], acc[hi])
    acc_theirs = over_core(jnp.where(core == 0, acc[hi], acc[lo]))
    stat_mine = jnp.where(core == 0, stat[lo], stat[hi])
    stat_theirs = over_core(jnp.where(core == 0, stat[hi], stat[lo]))
    attended = pl.pallas_call(
        merge_kernel,
        in_specs=[VMEM] * 4,
        out_specs=VMEM,
        out_shape=jax.ShapeDtypeStruct((tok, 2 * HD), jnp.bfloat16),
        compiler_params=PARAMS,
    )(acc_mine, acc_theirs, stat_mine, stat_theirs)

    owners = jnp.stack(
        [
            8 * (blk ^ dc) + (dec ^ dx)
            for dx in (0, 4)
            for dc in (0, 1)
        ]
    )
    slots = (2 * owners[:, None] + jnp.arange(2)[None, :]).reshape(8)
    hits = page_slot[None, :] == slots[:, None]
    filled = jnp.any(hits, axis=1)
    page = jnp.sum(jnp.where(hits, jnp.arange(64)[None, :], 0), axis=1)
    page_blk, page_dec = page // 8, page % 8
    same = page_blk % 2 == core
    gap = (page_blk // 2 - y) % 4
    rel = page_dec ^ dec
    buffer = 2 * gap + rel % 2
    at = jnp.where(filled & same, 4 * buffer + rel // 2, -1).astype(i32)
    block = ((2 * PAGE, 2 * HD), jnp.bfloat16)
    mine, to_core, to_head, to_both = call(
        pick_kernel, at, [e0, e1, b0, b1, c0, c1, a0, a1], [block] * 4
    )
    own_c = over_core(to_core)
    oth = over_dec(to_head, 4)
    oth_c = lax.ppermute(
        to_both,
        ("blk", "dec"),
        [(8 * b + d, 8 * (b ^ 1) + (d ^ 4)) for b in range(8) for d in range(8)],
    )
    flags = jnp.concatenate([head[None], filled[:2], same[:2]]).astype(i32)
    cache_keys, cache_values, key_scales, value_scales = call(
        cache_kernel,
        flags,
        [mine, own_c, oth, oth_c],
        [block, block, ((2, 2), jnp.float32), ((2, 2), jnp.float32)],
    )
    return attended, cache_keys, cache_values, key_scales, value_scales


def solution(mesh):
    return jax.shard_map(
        body,
        mesh=mesh,
        in_specs=(
            P("blk", ("kvh", "dec")),
            P(("blk", "dec"), "kvh"),
            P(("blk", "dec"), "kvh"),
            P(),
        ),
        out_specs=(
            P("blk", ("kvh", "dec")),
            P(("blk", "dec"), "kvh"),
            P(("blk", "dec"), "kvh"),
            P(("blk", "dec"), "kvh"),
            P(("blk", "dec"), "kvh"),
        ),
        check_vma=False,
    )
```

time: 566 us -> 107 us (0.19)
  the two profiles are of different devices: /device:TPU:17 before, /device:TPU:57 now
where the time goes in v1:
time: 107 us; the launch traced here: 106 us
  Pallas kernels  57.1 us (53%)
  starting transfers between devices  36.9 us (34%)
  waiting for transfers between devices  9.13 us (9%)
  other arithmetic  1.4 us (1%)
    pallas_call x6, Pallas kernels, call(): pl.pallas_call(kernel, in_specs=[SMEM] + [VMEM] * len(arrays), out_specs=...  54.8 us
    ppermute x8, starting transfers between devices, over_dec(): return lax.ppermute(x, 'dec', [(i, i ^ m) for i in range(8)])  15.2 us
    ppermute x4, starting transfers between devices, over_core(): return lax.ppermute(x, 'blk', [(i, i ^ 1) for i in range(8)])  14 us
    ppermute x6, starting transfers between devices, over_y(): return lax.ppermute(x, 'blk', [(i, (i + 2 * d) % 8) for i in range(8)])  6.97 us
    ppermute x8, waiting for transfers between devices, over_dec(): return lax.ppermute(x, 'dec', [(i, i ^ m) for i in range(8)])  6.03 us
    ppermute x1, waiting for transfers between devices, body(): lax.ppermute(to_both, ('blk', 'dec'), [(8 * b + d, 8 * (b ^ 1) + (d ^ 4))...  3.07 us
    pallas_call x1, Pallas kernels, body(): pl.pallas_call(merge_kernel, in_specs=[VMEM] * 4, out_specs=VMEM, out_sha...  2.3 us
  transfers between devices with their start and end apart: 19, of which 3 were waited for; matrix products, arithmetic and copies ran while one was open for 1% of the time, Pallas kernels for 46%

profile of v1, /device:TPU:57, one launch (start us, length us, event | category | flops | bytes accessed | tf_op | source)
XLA Modules:
  0.0 106.4 jit_solution(17555916173830685046)
XLA Ops:
  0.7 0.9 fusion.8
  1.6 2.6 %collective-permute-start.10 = (bf16[128,256]{1,0:T(8,128)(2,1)S(1)}, bf16[128,256]{1,0:T(8,128)(2,1)S(1)}, u32[]{:S(2)}, u32[]{:S(2)}) collective-permute-start(bf16[128,256]{1,0:T(8,128)(2,1)S(1)} %get-tuple-element.46), channel_id=1, source_target_pairs={{0,6},{1,7},{2,4},{3,5},{4,2},{5,3},{6,0},{7,1},{8,14},{9,15},{10,... | collective-permute-start | bytes 196616 | tf_op jit(solution)/shard_map/ppermute | solution.py:201
  4.1 0.5 collective-permute-start.9
  4.9 6.1 %collective-permute-start.1 = (bf16[256,256]{1,0:T(8,128)(2,1)S(1)}, bf16[256,256]{1,0:T(8,128)(2,1)S(1)}, u32[]{:S(2)}, u32[]{:S(2)}) collective-permute-start(bf16[256,256]{1,0:T(8,128)(2,1)S(1)} %pad_maximum_fusion.2), channel_id=1, source_target_pairs={{0,1},{1,0},{2,3},{3,2},{4,5},{5,4},{6,7},{7,6},{8,9},{9,8},{10,11... | collective-permute-start | bytes 393224 | tf_op jit(solution)/shard_map/ppermute | solution.py:201
  11.0 1.8 %collective-permute-start = (bf16[1024,256]{1,0:T(8,128)(2,1)}, bf16[1024,256]{1,0:T(8,128)(2,1)S(1)}, u32[]{:S(2)}, u32[]{:S(2)}) collective-permute-start(bf16[1024,256]{1,0:T(8,128)(2,1)} %param.4), channel_id=1, source_target_pairs={{0,32},{32,0},{64,96},{96,64},{128,160},{160,128},{192,224},{224,1... | collective-permute-start | bytes 1572872 | tf_op jit(solution)/shard_map/ppermute | solution.py:204
  13.1 0.5 collective-permute-start.13
  13.7 2.6 %collective-permute-start.4 = (bf16[128,256]{1,0:T(8,128)(2,1)S(1)}, bf16[128,256]{1,0:T(8,128)(2,1)S(1)}, u32[]{:S(2)}, u32[]{:S(2)}) collective-permute-start(bf16[128,256]{1,0:T(8,128)(2,1)S(1)} %get-tuple-element.44), channel_id=1, source_target_pairs={{0,6},{1,7},{2,4},{3,5},{4,2},{5,3},{6,0},{7,1},{8,14},{9,15},{10,... | collective-permute-start | bytes 196616 | tf_op jit(solution)/shard_map/ppermute | solution.py:201
  17.1 3.1 %collective-permute-done.2 = bf16[128,256]{1,0:T(8,128)(2,1)S(1)} collective-permute-done((bf16[128,256]{1,0:T(8,128)(2,1)S(1)}, bf16[128,256]{1,0:T(8,128)(2,1)S(1)}, u32[]{:S(2)}, u32[]{:S(2)}) %collective-permute-start.2) | collective-permute-done | bytes 65568 | tf_op jit(solution)/shard_map/ppermute | solution.py:201
  20.1 1.9 %collective-permute-start.12 = (bf16[512,256]{1,0:T(8,128)(2,1)S(1)}, bf16[512,256]{1,0:T(8,128)(2,1)S(1)}, u32[]{:S(2)}, u32[]{:S(2)}) collective-permute-start(bf16[512,256]{1,0:T(8,128)(2,1)S(1)} %pad_maximum_fusion.1.e0.refs_0_), channel_id=1, source_target_pairs={{0,64},{32,96},{64,128},{96,160},{128,192},{160,224},{192,0},{224,... | collective-permute-start | bytes 786440 | tf_op jit(solution)/shard_map/ppermute | solution.py:207
  22.2 0.6 collective-permute-start.7
  22.8 2.2 %collective-permute-start.6 = (bf16[512,256]{1,0:T(8,128)(2,1)S(1)}, bf16[512,256]{1,0:T(8,128)(2,1)S(1)}, u32[]{:S(2)}, u32[]{:S(2)}) collective-permute-start(bf16[512,256]{1,0:T(8,128)(2,1)S(1)} %pad_maximum_fusion.e1.refs_1_), channel_id=1, source_target_pairs={{0,64},{32,96},{64,128},{96,160},{128,192},{160,224},{192,0},{224,... | collective-permute-start | bytes 786440 | tf_op jit(solution)/shard_map/ppermute | solution.py:207
  25.0 1.7 %collective-permute-start.5 = (bf16[512,256]{1,0:T(8,128)(2,1)S(1)}, bf16[512,256]{1,0:T(8,128)(2,1)S(1)}, u32[]{:S(2)}, u32[]{:S(2)}) collective-permute-start(bf16[512,256]{1,0:T(8,128)(2,1)S(1)} %pad_maximum_fusion.e1.refs_1_), channel_id=1, source_target_pairs={{0,128},{32,160},{64,192},{96,224},{128,0},{160,32},{192,64},{224,... | collective-permute-start | bytes 786440 | tf_op jit(solution)/shard_map/ppermute | solution.py:207
  27.0 6.8 %shard_map.83 = (f32[2048,256]{1,0:T(8,128)S(1)}, f32[2048,8]{1,0:T(8,128)S(1)}) custom-call(s32[2]{0:T(128)S(1)} %pad_add_fusion.meta, bf16[2048,256]{1,0:T(8,128)(2,1)S(1)} %maximum_select_fusion.q_ref, bf16[512,256]{1,0:T(8,128)(2,1)S(1)} %pad_maximum_fusion.1.e0.refs_0_, bf16[512,256]{1,0:T(8,128)(2,1)S(1)} %pad_maximum_fusion.e1.refs_1_), custom_call_target="tpu_custom_call" | custom-call | tf_op jit(solution)/shard_map/pallas_call | solution.py:184
  33.8 18.4 %shard_map.84 = (f32[2048,256]{1,0:T(8,128)S(1)}, f32[2048,8]{1,0:T(8,128)S(1)}) custom-call(s32[2]{0:T(128)S(1)} %add_convert_fusion.1.meta, bf16[2048,256]{1,0:T(8,128)(2,1)S(1)} %maximum_select_fusion.q_ref, bf16[512,256]{1,0:T(8,128)(2,1)S(1)} %collective-permute-done.12.refs_0_.refs_6_, ...), custom_call_target="tpu_custom_call", output_to_operand_aliasing={{0}: (4, {}), {1}: (5, {})} | custom-call | tf_op jit(solution)/shard_map/pallas_call | solution.py:184
  52.3 21.3 %shard_map.85 = (f32[2048,256]{1,0:T(8,128)S(1)}, f32[2048,8]{1,0:T(8,128)S(1)}) custom-call(s32[3]{0:T(128)S(1)} %add_convert_fusion.meta, bf16[2048,256]{1,0:T(8,128)(2,1)S(1)} %maximum_select_fusion.q_ref, bf16[512,256]{1,0:T(8,128)(2,1)S(1)} %collective-permute-done.6.refs_0_.refs_7_, ...), custom_call_target="tpu_custom_call", output_to_operand_aliasing={{0}: (5, {}), {1}: (6, {})} | custom-call | tf_op jit(solution)/shard_map/pallas_call | solution.py:184
  73.6 5.9 %shard_map.86 = (f32[2048,256]{1,0:T(8,128)S(1)}, f32[2048,8]{1,0:T(8,128)S(1)}) custom-call(s32[1]{0:T(128)S(6)} %convert_element_type.15.meta, bf16[2048,256]{1,0:T(8,128)(2,1)S(1)} %maximum_select_fusion.q_ref, bf16[512,256]{1,0:T(8,128)(2,1)S(1)} %collective-permute-done.5.refs_0_.refs_5_, ...), custom_call_target="tpu_custom_call", output_to_operand_aliasing={{0}: (3, {}), {1}: (4, {})} | custom-call | tf_op jit(solution)/shard_map/pallas_call | solution.py:184
  79.7 11.4 %collective-permute-start.14 = (f32[1024,256]{1,0:T(8,128)S(1)}, f32[1024,256]{1,0:T(8,128)S(1)}, u32[]{:S(2)}, u32[]{:S(2)}) collective-permute-start(f32[1024,256]{1,0:T(8,128)S(1)} %get-tuple-element.39), channel_id=1, source_target_pairs={{0,32},{32,0},{64,96},{96,64},{128,160},{160,128},{192,224},{224,1... | collective-permute-start | bytes 3145736 | tf_op jit(solution)/shard_map/ppermute | solution.py:204
  91.5 1.0 shard_map.88
  93.0 2.5 %collective-permute-start.17 = (bf16[256,256]{1,0:T(8,128)(2,1)S(1)}, bf16[256,256]{1,0:T(8,128)(2,1)S(1)}, u32[]{:S(2)}, u32[]{:S(2)}) collective-permute-start(bf16[256,256]{1,0:T(8,128)(2,1)S(1)} %get-tuple-element.31), channel_id=1, source_target_pairs={{0,4},{1,5},{2,6},{3,7},{4,0},{5,1},{6,2},{7,3},{8,12},{9,13},{10,... | collective-permute-start | bytes 393224 | tf_op jit(solution)/shard_map/ppermute | solution.py:201
  95.5 0.8 collective-permute-start.18
  96.6 2.9 %collective-permute-done.17.oth = bf16[256,256]{1,0:T(8,128)(2,1)S(1)} collective-permute-done((bf16[256,256]{1,0:T(8,128)(2,1)S(1)}, bf16[256,256]{1,0:T(8,128)(2,1)S(1)}, u32[]{:S(2)}, u32[]{:S(2)}) %collective-permute-start.17) | collective-permute-done | bytes 131104 | tf_op jit(solution)/shard_map/ppermute | solution.py:201
  99.6 3.1 %collective-permute-done.18.oth_c = bf16[256,256]{1,0:T(8,128)(2,1)S(1)} collective-permute-done((bf16[256,256]{1,0:T(8,128)(2,1)S(1)}, bf16[256,256]{1,0:T(8,128)(2,1)S(1)}, u32[]{:S(2)}, u32[]{:S(2)}) %collective-permute-start.18) | collective-permute-done | bytes 131104 | tf_op jit(solution)/shard_map/ppermute | solution.py:286
  102.6 1.5 %shard_map.89 = (bf16[256,256]{1,0:T(8,128)(2,1)}, bf16[256,256]{1,0:T(8,128)(2,1)}, f32[2,2]{1,0:T(2,128)}, f32[2,2]{1,0:T(2,128)}) custom-call(s32[5]{0:T(128)S(1)} %pad_add_fusion.1.meta, bf16[256,256]{1,0:T(8,128)(2,1)S(1)} %get-tuple-element.29.own, bf16[256,256]{1,0:T(8,128)(2,1)S(1)} %collective-permute-done.16.own_c, ...), custom_call_target="tpu_custom_call" | custom-call | tf_op jit(solution)/shard_map/pallas_call | solution.py:184
  104.1 2.3 %shard_map.87 = bf16[1024,256]{1,0:T(8,128)(2,1)} custom-call(f32[1024,256]{1,0:T(8,128)S(1)} %get-tuple-element.40.mine, f32[1024,256]{1,0:T(8,128)S(1)} %collective-permute-done.14.theirs, f32[1024,8]{1,0:T(8,128)S(1)} %get-tuple-element.42.ml_mine, f32[1024,8]{1,0:T(8,128)S(1)} %collective-permute-done.15.ml_theirs), custom_call_target="tpu_custom_call" | custom-call | tf_op jit(solution)/shard_map/pallas_call | solution.py:255
  (45 shorter events, 3.4 us)
Async XLA Ops:
  0.6 26.1 %copy-start = (bf16[1024,256]{1,0:T(8,128)(2,1)S(1)}, bf16[1024,256]{1,0:T(8,128)(2,1)}, u32[]{:S(2)}) copy-start(bf16[1024,256]{1,0:T(8,128)(2,1)} %param.4) | copy-start | bytes 1572868
  1.6 11.5 %collective-permute-start.10 = (bf16[128,256]{1,0:T(8,128)(2,1)S(1)}, bf16[128,256]{1,0:T(8,128)(2,1)S(1)}, u32[]{:S(2)}, u32[]{:S(2)}) collective-permute-start(bf16[128,256]{1,0:T(8,128)(2,1)S(1)} %get-tuple-element.46), channel_id=1, source_target_pairs={{0,6},{1,7},{2,4},{3,5},{4,2},{5,3},{6,0},{7,1},{8,14},{9,15},{10,... | collective-permute-start | bytes 196616 | tf_op jit(solution)/shard_map/ppermute | solution.py:201
  4.1 8.9 %collective-permute-start.9 = (bf16[128,256]{1,0:T(8,128)(2,1)S(1)}, bf16[128,256]{1,0:T(8,128)(2,1)S(1)}, u32[]{:S(2)}, u32[]{:S(2)}) collective-permute-start(bf16[128,256]{1,0:T(8,128)(2,1)S(1)} %get-tuple-element.46), channel_id=1, source_target_pairs={{0,4},{1,5},{2,6},{3,7},{4,0},{5,1},{6,2},{7,3},{8,12},{9,13},{10,... | collective-permute-start | bytes 196616 | tf_op jit(solution)/shard_map/ppermute | solution.py:201
  4.7 8.4 %collective-permute-start.8 = (bf16[128,256]{1,0:T(8,128)(2,1)S(1)}, bf16[128,256]{1,0:T(8,128)(2,1)S(1)}, u32[]{:S(2)}, u32[]{:S(2)}) collective-permute-start(bf16[128,256]{1,0:T(8,128)(2,1)S(1)} %get-tuple-element.45), channel_id=1, source_target_pairs={{0,2},{1,3},{2,0},{3,1},{4,6},{5,7},{6,4},{7,5},{8,10},{9,11},{10,... | collective-permute-start | bytes 196616 | tf_op jit(solution)/shard_map/ppermute | solution.py:201
  4.9 8.7 %collective-permute-start.1 = (bf16[256,256]{1,0:T(8,128)(2,1)S(1)}, bf16[256,256]{1,0:T(8,128)(2,1)S(1)}, u32[]{:S(2)}, u32[]{:S(2)}) collective-permute-start(bf16[256,256]{1,0:T(8,128)(2,1)S(1)} %pad_maximum_fusion.2), channel_id=1, source_target_pairs={{0,1},{1,0},{2,3},{3,2},{4,5},{5,4},{6,7},{7,6},{8,9},{9,8},{10,11... | collective-permute-start | bytes 393224 | tf_op jit(solution)/shard_map/ppermute | solution.py:201
  11.0 13.9 %collective-permute-start = (bf16[1024,256]{1,0:T(8,128)(2,1)}, bf16[1024,256]{1,0:T(8,128)(2,1)S(1)}, u32[]{:S(2)}, u32[]{:S(2)}) collective-permute-start(bf16[1024,256]{1,0:T(8,128)(2,1)} %param.4), channel_id=1, source_target_pairs={{0,32},{32,0},{64,96},{96,64},{128,160},{160,128},{192,224},{224,1... | collective-permute-start | bytes 1572872 | tf_op jit(solution)/shard_map/ppermute | solution.py:204
  13.1 9.7 %collective-permute-start.13 = (bf16[512,256]{1,0:T(8,128)(2,1)S(1)}, bf16[512,256]{1,0:T(8,128)(2,1)S(1)}, u32[]{:S(2)}, u32[]{:S(2)}) collective-permute-start(bf16[512,256]{1,0:T(8,128)(2,1)S(1)} %pad_maximum_fusion.1.e0.refs_0_), channel_id=1, source_target_pairs={{0,192},{32,224},{64,0},{96,32},{128,64},{160,96},{192,128},{224,1... | collective-permute-start | bytes 786440 | tf_op jit(solution)/shard_map/ppermute | solution.py:207
  13.7 8.4 %collective-permute-start.4 = (bf16[128,256]{1,0:T(8,128)(2,1)S(1)}, bf16[128,256]{1,0:T(8,128)(2,1)S(1)}, u32[]{:S(2)}, u32[]{:S(2)}) collective-permute-start(bf16[128,256]{1,0:T(8,128)(2,1)S(1)} %get-tuple-element.44), channel_id=1, source_target_pairs={{0,6},{1,7},{2,4},{3,5},{4,2},{5,3},{6,0},{7,1},{8,14},{9,15},{10,... | collective-permute-start | bytes 196616 | tf_op jit(solution)/shard_map/ppermute | solution.py:201
  16.2 6.0 %collective-permute-start.3 = (bf16[128,256]{1,0:T(8,128)(2,1)S(1)}, bf16[128,256]{1,0:T(8,128)(2,1)S(1)}, u32[]{:S(2)}, u32[]{:S(2)}) collective-permute-start(bf16[128,256]{1,0:T(8,128)(2,1)S(1)} %get-tuple-element.44), channel_id=1, source_target_pairs={{0,4},{1,5},{2,6},{3,7},{4,0},{5,1},{6,2},{7,3},{8,12},{9,13},{10,... | collective-permute-start | bytes 196616 | tf_op jit(solution)/shard_map/ppermute | solution.py:201
  16.7 3.4 %collective-permute-start.2 = (bf16[128,256]{1,0:T(8,128)(2,1)S(1)}, bf16[128,256]{1,0:T(8,128)(2,1)S(1)}, u32[]{:S(2)}, u32[]{:S(2)}) collective-permute-start(bf16[128,256]{1,0:T(8,128)(2,1)S(1)} %get-tuple-element.43), channel_id=1, source_target_pairs={{0,2},{1,3},{2,0},{3,1},{4,6},{5,7},{6,4},{7,5},{8,10},{9,11},{10,... | collective-permute-start | bytes 196616 | tf_op jit(solution)/shard_map/ppermute | solution.py:201
  20.1 13.7 %collective-permute-start.12 = (bf16[512,256]{1,0:T(8,128)(2,1)S(1)}, bf16[512,256]{1,0:T(8,128)(2,1)S(1)}, u32[]{:S(2)}, u32[]{:S(2)}) collective-permute-start(bf16[512,256]{1,0:T(8,128)(2,1)S(1)} %pad_maximum_fusion.1.e0.refs_0_), channel_id=1, source_target_pairs={{0,64},{32,96},{64,128},{96,160},{128,192},{160,224},{192,0},{224,... | collective-permute-start | bytes 786440 | tf_op jit(solution)/shard_map/ppermute | solution.py:207
  22.1 30.2 %collective-permute-start.11 = (bf16[512,256]{1,0:T(8,128)(2,1)S(1)}, bf16[512,256]{1,0:T(8,128)(2,1)S(1)}, u32[]{:S(2)}, u32[]{:S(2)}) collective-permute-start(bf16[512,256]{1,0:T(8,128)(2,1)S(1)} %pad_maximum_fusion.1.e0.refs_0_), channel_id=1, source_target_pairs={{0,128},{32,160},{64,192},{96,224},{128,0},{160,32},{192,64},{224,... | collective-permute-start | bytes 786440 | tf_op jit(solution)/shard_map/ppermute | solution.py:207
  22.2 30.1 %collective-permute-start.7 = (bf16[512,256]{1,0:T(8,128)(2,1)S(1)}, bf16[512,256]{1,0:T(8,128)(2,1)S(1)}, u32[]{:S(2)}, u32[]{:S(2)}) collective-permute-start(bf16[512,256]{1,0:T(8,128)(2,1)S(1)} %pad_maximum_fusion.e1.refs_1_), channel_id=1, source_target_pairs={{0,192},{32,224},{64,0},{96,32},{128,64},{160,96},{192,128},{224,1... | collective-permute-start | bytes 786440 | tf_op jit(solution)/shard_map/ppermute | solution.py:207
  22.8 29.5 %collective-permute-start.6 = (bf16[512,256]{1,0:T(8,128)(2,1)S(1)}, bf16[512,256]{1,0:T(8,128)(2,1)S(1)}, u32[]{:S(2)}, u32[]{:S(2)}) collective-permute-start(bf16[512,256]{1,0:T(8,128)(2,1)S(1)} %pad_maximum_fusion.e1.refs_1_), channel_id=1, source_target_pairs={{0,64},{32,96},{64,128},{96,160},{128,192},{160,224},{192,0},{224,... | collective-permute-start | bytes 786440 | tf_op jit(solution)/shard_map/ppermute | solution.py:207
  25.0 48.6 %collective-permute-start.5 = (bf16[512,256]{1,0:T(8,128)(2,1)S(1)}, bf16[512,256]{1,0:T(8,128)(2,1)S(1)}, u32[]{:S(2)}, u32[]{:S(2)}) collective-permute-start(bf16[512,256]{1,0:T(8,128)(2,1)S(1)} %pad_maximum_fusion.e1.refs_1_), channel_id=1, source_target_pairs={{0,128},{32,160},{64,192},{96,224},{128,0},{160,32},{192,64},{224,... | collective-permute-start | bytes 786440 | tf_op jit(solution)/shard_map/ppermute | solution.py:207
  79.5 11.6 %copy-start.1 = (s32[64]{0:T(128)S(1)}, s32[64]{0:T(128)}, u32[]{:S(2)}) copy-start(s32[64]{0:T(128)} %param.7) | copy-start | bytes 772
  79.7 24.4 %collective-permute-start.14 = (f32[1024,256]{1,0:T(8,128)S(1)}, f32[1024,256]{1,0:T(8,128)S(1)}, u32[]{:S(2)}, u32[]{:S(2)}) collective-permute-start(f32[1024,256]{1,0:T(8,128)S(1)} %get-tuple-element.39), channel_id=1, source_target_pairs={{0,32},{32,0},{64,96},{96,64},{128,160},{160,128},{192,224},{224,1... | collective-permute-start | bytes 3145736 | tf_op jit(solution)/shard_map/ppermute | solution.py:204
  92.5 4.1 %collective-permute-start.16 = (bf16[256,256]{1,0:T(8,128)(2,1)S(1)}, bf16[256,256]{1,0:T(8,128)(2,1)S(1)}, u32[]{:S(2)}, u32[]{:S(2)}) collective-permute-start(bf16[256,256]{1,0:T(8,128)(2,1)S(1)} %get-tuple-element.30), channel_id=1, source_target_pairs={{0,32},{32,0},{64,96},{96,64},{128,160},{160,128},{192,224},{224,1... | collective-permute-start | bytes 393224 | tf_op jit(solution)/shard_map/ppermute | solution.py:204
  93.0 6.6 %collective-permute-start.17 = (bf16[256,256]{1,0:T(8,128)(2,1)S(1)}, bf16[256,256]{1,0:T(8,128)(2,1)S(1)}, u32[]{:S(2)}, u32[]{:S(2)}) collective-permute-start(bf16[256,256]{1,0:T(8,128)(2,1)S(1)} %get-tuple-element.31), channel_id=1, source_target_pairs={{0,4},{1,5},{2,6},{3,7},{4,0},{5,1},{6,2},{7,3},{8,12},{9,13},{10,... | collective-permute-start | bytes 393224 | tf_op jit(solution)/shard_map/ppermute | solution.py:201
  95.5 7.2 %collective-permute-start.18 = (bf16[256,256]{1,0:T(8,128)(2,1)S(1)}, bf16[256,256]{1,0:T(8,128)(2,1)S(1)}, u32[]{:S(2)}, u32[]{:S(2)}) collective-permute-start(bf16[256,256]{1,0:T(8,128)(2,1)S(1)} %get-tuple-element.32), channel_id=1, source_target_pairs={{0,36},{1,37},{2,38},{3,39},{4,32},{5,33},{6,34},{7,35},{32,4},{33... | collective-permute-start | bytes 393224 | tf_op jit(solution)/shard_map/ppermute | solution.py:286
  96.3 7.8 %collective-permute-start.15 = (f32[1024,8]{1,0:T(8,128)S(1)}, f32[1024,8]{1,0:T(8,128)S(1)}, u32[]{:S(2)}, u32[]{:S(2)}) collective-permute-start(f32[1024,8]{1,0:T(8,128)S(1)} %get-tuple-element.41), channel_id=1, source_target_pairs={{0,32},{32,0},{64,96},{96,64},{128,160},{160,128},{192,224},{224,1... | collective-permute-start | bytes 98312 | tf_op jit(solution)/shard_map/ppermute | solution.py:204

commit v2 on v0

v2 whole, which is shorter than its diff:
```python
import functools

import jax
import jax.numpy as jnp
import numpy as np
from jax import lax
from jax.experimental import pallas as pl
from jax.experimental.pallas import tpu as pltpu
from jax.sharding import PartitionSpec as P

HEADS = 64
KVH = 8
HD = 128
PAGE = 128
TQ = 512
TN = 256
TS = 128
SEG = 512
C = float(np.log2(np.e) / np.sqrt(HD))
NEG = -1e30
LIMIT = 80.0
NT = (((1,), (1,)), ((), ()))


def longest(x):
    x = x.astype(jnp.float32)
    squares = jnp.dot(
        (x * x).astype(jnp.bfloat16),
        jnp.ones((HD, HD), jnp.bfloat16),
        preferred_element_type=jnp.float32,
    )
    return jnp.sqrt(jnp.max(squares))


def fast(q_ref, state, h, row, size, k, v, allowed=None):
    acc_ref, shift_ref, total_ref = state[:3]
    q = q_ref[rows_at(row, size), h * HD : (h + 1) * HD]
    r = rows_at(h * q_ref.shape[0] + row, size)
    s = lax.dot_general(q, k, NT, preferred_element_type=jnp.float32)
    p = jnp.exp2(s * C - shift_ref[r])
    if allowed is not None:
        p = jnp.where(allowed, p, 0.0)
    total_ref[r] += jnp.sum(p, axis=1, keepdims=True)
    acc_ref[r] += jnp.dot(p.astype(jnp.bfloat16), v, preferred_element_type=jnp.float32)


def slow(q_ref, state, h, row, size, k, v, allowed=True):
    acc_ref, shift_ref, total_ref = state[:3]
    q = q_ref[rows_at(row, size), h * HD : (h + 1) * HD]
    r = rows_at(h * q_ref.shape[0] + row, size)
    s = C * lax.dot_general(q, k, NT, preferred_element_type=jnp.float32)
    s = jnp.where(allowed, s, NEG)
    total = total_ref[r]
    old = jnp.where(total > 0, shift_ref[r], NEG)
    shift = jnp.maximum(old, jnp.max(s, axis=1, keepdims=True))
    p = jnp.where(allowed, jnp.exp2(s - shift), 0.0)
    a = jnp.exp2(old - shift)
    total = a * total + jnp.sum(p, axis=1, keepdims=True)
    shift_ref[r] = jnp.where(total > 0, shift, 0.0)
    total_ref[r] = total
    acc_ref[r] = a * acc_ref[r] + jnp.dot(
        p.astype(jnp.bfloat16), v, preferred_element_type=jnp.float32
    )


def loop(begin, end, step):
    def one(i, _):
        step(i)
        return 0

    lax.fori_loop(begin, end, one, 0)


def rows_at(start, size):
    return pl.ds(start if isinstance(start, int) else pl.multiple_of(start, size), size)


def guarded(state, key_norm, quick, careful):
    shift_ref, bound_ref = state[1], state[3]
    top = jnp.max(bound_ref[:, 0:1]) * key_norm * (1.02 * C) - jnp.min(bound_ref[:, 1:2])

    @pl.when(top <= LIMIT)
    def _():
        quick()

    @pl.when(jnp.logical_not(top <= LIMIT))
    def _():
        careful()
        lowest = jnp.minimum(jnp.min(shift_ref[...]), 0.0)
        bound_ref[:, 1:2] = jnp.full((8, 1), lowest)


def near_kernel(z, meta, q_ref, e_ref, x_ref, *refs):
    state, page_ref = refs[-5:-1], refs[-1]
    acc_ref, shift_ref, total_ref, bound_ref = state
    rows = q_ref.shape[0]
    core, dec = meta[0], meta[1]
    if z == 0:
        refs[0][...] = q_ref[...]
        acc_ref[...] = jnp.zeros_like(acc_ref)
        shift_ref[...] = jnp.zeros_like(shift_ref)
        total_ref[...] = jnp.zeros_like(total_ref)
        bound_ref[...] = jnp.zeros_like(bound_ref)
        norm = jnp.maximum(longest(q_ref[:, :HD]), longest(q_ref[:, HD:]))
        bound_ref[:, 0:1] = jnp.full((8, 1), norm)
    parity = jnp.bitwise_xor(dec % 2, z)
    for i in range(SEG // PAGE):
        to = jnp.bitwise_xor(dec // 2, i) * PAGE
        page_ref[rows_at(to, PAGE)] = e_ref[i * PAGE : (i + 1) * PAGE]

    def quick():
        row = lax.broadcasted_iota(jnp.int32, (2 * PAGE, PAGE), 0)
        lane = lax.broadcasted_iota(jnp.int32, (2 * PAGE, PAGE), 1)
        last = parity * PAGE + lane <= row
        for t in range(SEG // PAGE):
            n = (t + 1) * PAGE
            allowed = last
            if t:
                allowed = jnp.concatenate([jnp.full((2 * PAGE, t * PAGE), True), last], axis=1)
            for h in range(2):
                fast(
                    q_ref,
                    state,
                    h,
                    t * 2 * PAGE,
                    2 * PAGE,
                    page_ref[:n, :HD],
                    page_ref[:n, HD:],
                    allowed,
                )

        def extra(i):
            for h in range(2):
                fast(q_ref, state, h, i * TQ, TQ, x_ref[:, :HD], x_ref[:, HD:])

        loop(0, jnp.where(core == 1, rows // TQ, 0), extra)

    def careful():
        lane = lax.broadcasted_iota(jnp.int32, (1, SEG), 1)
        key_at = (2 * (lane // PAGE) + parity) * PAGE + lane % PAGE

        def diagonal(i):
            allowed = key_at <= i * TS + lax.broadcasted_iota(jnp.int32, (TS, 1), 0)
            for h in range(2):
                slow(q_ref, state, h, i * TS, TS, page_ref[:, :HD], page_ref[:, HD:], allowed)

        def extra(i):
            for h in range(2):
                slow(q_ref, state, h, i * TS, TS, x_ref[:, :HD], x_ref[:, HD:])

        loop(0, rows // TS, diagonal)
        loop(0, jnp.where(core == 1, rows // TS, 0), extra)

    key_norm = jnp.maximum(longest(e_ref[:, :HD]), longest(x_ref[:, :HD]))
    guarded(state, key_norm, quick, careful)


def next_kernel(last, meta, q_ref, own0, own1, there, *refs):
    if last:
        state, out_ref, kv_ref = refs[-6:-2], *refs[-2:]
    else:
        state, kv_ref = refs[-5:-1], refs[-1]
    rows = q_ref.shape[0]
    count = meta[0]

    for j, own in enumerate((own0, own1)):

        @pl.when(count > j)
        def _():
            kv_ref[2 * j * SEG : (2 * j + 1) * SEG] = own[...]
            kv_ref[(2 * j + 1) * SEG : (2 * j + 2) * SEG] = there[j * SEG : (j + 1) * SEG]

    @pl.when(count > 0)
    def _():
        tiles = rows // TN

        def step(i):
            keys = rows_at((i // tiles) * 2 * SEG, 2 * SEG)
            for h in range(2):
                fast(q_ref, state, h, (i % tiles) * TN, TN, kv_ref[keys, :HD], kv_ref[keys, HD:])

        few = rows // TS

        def slow_step(i):
            keys = rows_at((i // few) * SEG, SEG)
            for h in range(2):
                slow(q_ref, state, h, (i % few) * TS, TS, kv_ref[keys, :HD], kv_ref[keys, HD:])

        norms = [longest(x[:, :HD]) for x in (own0, own1, there)]
        key_norm = jnp.maximum(jnp.maximum(norms[0], norms[1]), norms[2])
        guarded(
            state,
            key_norm,
            lambda: loop(0, count * tiles, step),
            lambda: loop(0, 2 * count * few, slow_step),
        )

    if last:
        acc_ref, _, total_ref, _ = state
        for h in range(2):
            r = slice(h * rows, (h + 1) * rows)
            out_ref[:, h * HD : (h + 1) * HD] = (acc_ref[r] * (1.0 / total_ref[r])).astype(
                jnp.bfloat16
            )


def pick_kernel(meta, *refs):
    pages, outs = refs[:-2], refs[-2:]
    own, (e0, e1, ab0, ab1, cc) = pages[:8], pages[8:]
    places = [(ref, 0) for ref in (*own, e0, e1)]
    places += [(ab0, SEG), (ab1, SEG), (cc, 0), (cc, SEG), (ab0, 0), (ab1, 0)]
    for d in range(2):
        for j in range(2):
            at = meta[2 * d + j]
            for b, (ref, start) in enumerate(places):

                @pl.when(at // 4 == b)
                def _():
                    rows = rows_at(start + (at % 4) * PAGE, PAGE)
                    outs[d][j * PAGE : (j + 1) * PAGE] = ref[rows]


def cache_kernel(meta, own, oth, ck, cv, ks, vs):
    col = meta[0]
    scales = [jnp.zeros((2, 2), jnp.float32)] * 2
    row_at = lax.broadcasted_iota(jnp.int32, (2, 2), 0)
    col_at = lax.broadcasted_iota(jnp.int32, (2, 2), 1)
    for j in range(2):
        filled = meta[1 + j] > 0
        rows = slice(j * PAGE, (j + 1) * PAGE)
        for kind, out in enumerate((ck, cv)):
            normed = []
            for b, block in enumerate((own, oth)):
                x = block[rows, kind * HD : (kind + 1) * HD].astype(jnp.float32)
                x = jnp.where(filled, x, 0.0)
                scale = jnp.max(jnp.abs(x)) + 1e-6
                normed.append((x / scale).astype(jnp.bfloat16))
                here = jnp.logical_and(row_at == j, col_at == (col if b == 0 else 1 - col))
                scales[kind] = jnp.where(jnp.logical_and(here, filled), scale, scales[kind])
            out[rows, :HD] = jnp.where(col == 0, normed[0], normed[1])
            out[rows, HD:] = jnp.where(col == 0, normed[1], normed[0])
    ks[...] = scales[0]
    vs[...] = scales[1]


VMEM = pl.BlockSpec(memory_space=pltpu.VMEM)
SMEM = pl.BlockSpec(memory_space=pltpu.SMEM)
PARAMS = pltpu.CompilerParams(vmem_limit_bytes=10 * 2**20)


def call(kernel, meta, arrays, outs, work=0, **more):
    return pl.pallas_call(
        kernel,
        in_specs=[SMEM] + [VMEM] * len(arrays),
        out_specs=[VMEM] * len(outs),
        out_shape=[jax.ShapeDtypeStruct(s, t) for s, t in outs],
        compiler_params=PARAMS,
        cost_estimate=pl.CostEstimate(flops=4 * HD * work, transcendentals=work, bytes_accessed=2**20),
        **more,
    )(meta, *arrays)


def body(queries, keys, values, page_slot):
    blk, dec = lax.axis_index("blk"), lax.axis_index("dec")
    y, core, head = blk // 2, blk % 2, dec // 4
    tok = queries.shape[0]
    i32 = jnp.int32

    def over_dec(x, m):
        return lax.ppermute(x, "dec", [(i, i ^ m) for i in range(8)])

    def over_core(x):
        return lax.ppermute(x, "blk", [(i, i ^ 1) for i in range(8)])

    def over_y(x, d):
        return lax.ppermute(x, "blk", [(i, (i + 2 * d) % 8) for i in range(8)])

    first = jnp.concatenate([keys[:, :HD], values[:, :HD]], axis=1)
    second = jnp.concatenate([keys[:, HD:], values[:, HD:]], axis=1)
    own = jnp.where(head == 0, first, second)
    other = jnp.where(head == 0, second, first)

    e0 = jnp.concatenate(
        [own, over_dec(own, 2), over_dec(other, 4), over_dec(other, 6)], axis=0
    )

    owners = jnp.stack([8 * blk + dec, 8 * blk + (dec ^ 4)])
    slots = (2 * owners[:, None] + jnp.arange(2)[None, :]).reshape(4)
    hits = page_slot[None, :] == slots[:, None]
    filled = jnp.any(hits, axis=1)
    page = jnp.sum(jnp.where(hits, jnp.arange(64)[None, :], 0), axis=1)
    page_blk, page_dec = page // 8, page % 8
    rel = page_dec ^ dec
    buffer = 8 * ((page_blk % 2) ^ core) + 2 * ((page_blk // 2 - y) % 4) + rel % 2
    at = jnp.where(filled, 4 * buffer + rel // 2, -1).astype(i32)
    flags = jnp.concatenate([head[None], filled[:2]]).astype(i32)

    state_types = [
        ((2 * tok, HD), jnp.float32),
        ((2 * tok, 1), jnp.float32),
        ((2 * tok, 1), jnp.float32),
        ((8, 2), jnp.float32),
    ]
    place = jnp.stack([core, dec]).astype(i32)
    near_by = jnp.where(y == 3, 2, jnp.where(y >= 1, 1, 0)).astype(i32).reshape(1)
    far = jnp.where(y >= 2, 2, 0).astype(i32).reshape(1)
    e0, at, flags, place, near_by, far = lax.optimization_barrier(
        (e0, at, flags, place, near_by, far)
    )
    e0_there = over_core(e0)
    e1 = over_dec(e0, 1)
    e0_y, e0_there = lax.optimization_barrier((e0, e0_there))
    a0, b0 = over_y(e0_y, 1), over_y(e0_y, 3)
    score_count = 2 * tok * SEG

    def near(z, q, e, x, state=()):
        return call(
            functools.partial(near_kernel, z),
            place,
            [q, e, x, *state],
            [((tok, 2 * HD), jnp.bfloat16)] * (z == 0) + state_types,
            2 * score_count,
            scratch_shapes=[pltpu.VMEM((SEG, 2 * HD), jnp.bfloat16)],
            input_output_aliases={4 + i: i for i in range(len(state))},
        )

    def more(count, own0, own1, there, state, last=False):
        return call(
            functools.partial(next_kernel, last),
            count,
            [q, own0, own1, there, *state],
            state_types + [((tok, 2 * HD), jnp.bfloat16)] * last,
            4 * score_count,
            scratch_shapes=[pltpu.VMEM((4 * SEG, 2 * HD), jnp.bfloat16)],
            input_output_aliases={5 + i: i for i in range(4)},
        )

    def both(first, second):
        return over_core(jnp.concatenate([first, second], axis=0))

    q, *state = near(0, queries, e0, e0_there)
    e0_far, state = lax.optimization_barrier((e0, state))
    c0 = over_y(e0_far, 2)
    a0, b0, e1, state = lax.optimization_barrier((a0, b0, e1, state))
    ab0_there = both(a0, b0)
    a1, b1 = over_y(e1, 1), over_y(e1, 3)
    e1_there = over_core(e1)
    state = more(near_by, a0, b0, ab0_there, state)
    e1_far, state = lax.optimization_barrier((e1, state))
    c1 = over_y(e1_far, 2)
    a1, b1, state = lax.optimization_barrier((a1, b1, state))
    ab1_there = both(a1, b1)
    state = near(1, q, e1, e1_there, state)
    state = more(near_by, a1, b1, ab1_there, state)
    c0, c1, state = lax.optimization_barrier((c0, c1, state))
    c_there = both(c0, c1)

    block = ((2 * PAGE, 2 * HD), jnp.bfloat16)
    at, state = lax.optimization_barrier((at, state))
    mine, to_head = call(
        pick_kernel,
        at,
        [e0, e1, b0, b1, c0, c1, a0, a1, e0_there, e1_there, ab0_there, ab1_there, c_there],
        [block] * 2,
    )
    state, mine = lax.optimization_barrier((state, mine))
    oth = over_dec(to_head, 4)
    *_, attended = more(far, c0, c1, c_there, state, True)
    cache_keys, cache_values, key_scales, value_scales = call(
        cache_kernel,
        flags,
        [mine, oth],
        [block, block, ((2, 2), jnp.float32), ((2, 2), jnp.float32)],
    )
    return attended, cache_keys, cache_values, key_scales, value_scales


def solution(mesh):
    return jax.shard_map(
        body,
        mesh=mesh,
        in_specs=(
            P("blk", ("kvh", "dec")),
            P(("blk", "dec"), "kvh"),
            P(("blk", "dec"), "kvh"),
            P(),
        ),
        out_specs=(
            P("blk", ("kvh", "dec")),
            P(("blk", "dec"), "kvh"),
            P(("blk", "dec"), "kvh"),
            P(("blk", "dec"), "kvh"),
            P(("blk", "dec"), "kvh"),
        ),
        check_vma=False,
    )
```

time: 566 us -> 122 us (0.22)
  the two profiles are of different devices: /device:TPU:17 before, /device:TPU:185 now
where the time goes in v2:
time: 122 us
  Pallas kernels  83.2 us (68%)
  starting transfers between devices  19.7 us (16%)
  waiting for transfers between devices  16.3 us (13%)
  local copies, waits for them, and re-layouts  1.53 us (1%)
    pallas_call x7, Pallas kernels, call(): pl.pallas_call(kernel, in_specs=[SMEM] + [VMEM] * len(arrays), out_specs=...  83.2 us
    ppermute x5, waiting for transfers between devices, over_dec(): return lax.ppermute(x, 'dec', [(i, i ^ m) for i in range(8)])  12.5 us
    ppermute x6, starting transfers between devices, over_y(): return lax.ppermute(x, 'blk', [(i, (i + 2 * d) % 8) for i in range(8)])  9.95 us
    ppermute x5, starting transfers between devices, over_dec(): return lax.ppermute(x, 'dec', [(i, i ^ m) for i in range(8)])  4.97 us
    ppermute x5, starting transfers between devices, over_core(): return lax.ppermute(x, 'blk', [(i, i ^ 1) for i in range(8)])  4.75 us
    ppermute x5, waiting for transfers between devices, over_core(): return lax.ppermute(x, 'blk', [(i, i ^ 1) for i in range(8)])  3.12 us
  transfers between devices with their start and end apart: 16, of which 7 were waited for; matrix products, arithmetic and copies ran while one was open for 1% of the time, Pallas kernels for 66%

profile of v2, /device:TPU:185, one launch (start us, length us, event | category | flops | bytes accessed | tf_op | source)
XLA Modules:
  0.0 122.3 jit_solution(8460064036353023656)
XLA Ops:
  0.7 0.9 fusion.8
  1.6 2.8 %collective-permute-start.1 = (bf16[128,256]{1,0:T(8,128)(2,1)S(1)}, bf16[128,256]{1,0:T(8,128)(2,1)S(1)}, u32[]{:S(2)}, u32[]{:S(2)}) collective-permute-start(bf16[128,256]{1,0:T(8,128)(2,1)S(1)} %get-tuple-element.148), channel_id=1, source_target_pairs={{0,4},{1,5},{2,6},{3,7},{4,0},{5,1},{6,2},{7,3},{8,12},{9,13},{10,... | collective-permute-start | bytes 196616 | tf_op jit(solution)/shard_map/ppermute | solution.py:270
  4.4 0.9 collective-permute-start.2
  5.5 0.6 copy-done.1
  6.7 1.7 %collective-permute-done = bf16[128,256]{1,0:T(8,128)(2,1)S(1)} collective-permute-done((bf16[128,256]{1,0:T(8,128)(2,1)S(1)}, bf16[128,256]{1,0:T(8,128)(2,1)S(1)}, u32[]{:S(2)}, u32[]{:S(2)}) %collective-permute-start) | collective-permute-done | bytes 65568 | tf_op jit(solution)/shard_map/ppermute | solution.py:270
  8.4 0.3 collective-permute-done.2
  8.8 2.2 %collective-permute-start.3 = (bf16[512,256]{1,0:T(8,128)(2,1)S(1)}, bf16[512,256]{1,0:T(8,128)(2,1)S(1)}, u32[]{:S(2)}, u32[]{:S(2)}) collective-permute-start(bf16[512,256]{1,0:T(8,128)(2,1)S(1)} %pad_maximum_fusion.3.e_ref.refs_0_), channel_id=1, source_target_pairs={{0,32},{32,0},{64,96},{96,64},{128,160},{160,128},{192,224},{224,1... | collective-permute-start | bytes 786440 | tf_op jit(solution)/shard_map/ppermute | solution.py:273
  11.0 1.2 collective-permute-done.3.x_ref.refs_8_
  12.1 1.5 %collective-permute-start.6 = (bf16[512,256]{1,0:T(8,128)(2,1)S(1)}, bf16[512,256]{1,0:T(8,128)(2,1)S(1)}, u32[]{:S(2)}, u32[]{:S(2)}) collective-permute-start(bf16[512,256]{1,0:T(8,128)(2,1)S(1)} %pad_maximum_fusion.3.e_ref.refs_0_), channel_id=1, source_target_pairs={{0,192},{32,224},{64,0},{96,32},{128,64},{160,96},{192,128},{224,1... | collective-permute-start | bytes 786440 | tf_op jit(solution)/shard_map/ppermute | solution.py:276
  13.6 4.3 %shard_map.83 = (bf16[1024,256]{1,0:T(8,128)(2,1)S(1)}, f32[2048,128]{1,0:T(8,128)S(1)}, f32[2048,1]{1,0:T(8,128)S(1)}, f32[2048,1]{1,0:T(8,128)S(1)}, f32[8,2]{1,0:T(8,128)S(1)}) custom-call(s32[2]{0:T(128)S(1)} %pad_add_fusion.1.meta, bf16[1024,256]{1,0:T(8,128)(2,1)S(1)} %copy-done, bf16[512,256]{1,0:T(8,128)(2,1)S(1)} %pad_maximum_fusion.3.e_ref.refs_0_, ...), custom_call_target="tpu_custom_call" | custom-call | flops 1073741824 | bytes 1048576 | tf_op jit(solution)/shard_map/pallas_call | solution.py:252
  17.8 10.5 %collective-permute-done.7.e_ref.refs_1_ = bf16[512,256]{1,0:T(8,128)(2,1)S(1)} collective-permute-done((bf16[512,256]{1,0:T(8,128)(2,1)S(1)}, bf16[512,256]{1,0:T(8,128)(2,1)S(1)}, u32[]{:S(2)}, u32[]{:S(2)}) %collective-permute-start.7) | collective-permute-done | bytes 262176 | tf_op jit(solution)/shard_map/ppermute | solution.py:270
  28.4 1.0 collective-permute-start.8
  29.4 1.5 %collective-permute-start.11 = (bf16[512,256]{1,0:T(8,128)(2,1)S(1)}, bf16[512,256]{1,0:T(8,128)(2,1)S(1)}, u32[]{:S(2)}, u32[]{:S(2)}) collective-permute-start(bf16[512,256]{1,0:T(8,128)(2,1)S(1)} %collective-permute-done.7.e_ref.refs_1_), channel_id=1, source_target_pairs={{0,192},{32,224},{64,0},{96,32},{128,64},{160,96},{192,128},{224,1... | collective-permute-start | bytes 786440 | tf_op jit(solution)/shard_map/ppermute | solution.py:276
  30.9 6.6 %shard_map.84 = (f32[2048,128]{1,0:T(8,128)S(1)}, f32[2048,1]{1,0:T(8,128)S(1)}, f32[2048,1]{1,0:T(8,128)S(1)}, f32[8,2]{1,0:T(8,128)S(1)}) custom-call(s32[1]{0:T(128)} %bitcast.5.meta, bf16[1024,256]{1,0:T(8,128)(2,1)S(1)} %get-tuple-element.80.q_ref, ...), custom_call_target="tpu_custom_call", output_to_operand_aliasing={{0}: (5, {}), {1}: (6, {}), {2}: (7, {}), {3}: (8, {})} | custom-call | flops 2147483648 | bytes 1048576 | tf_op jit(solution)/shard_map/pallas_call | solution.py:252
  37.5 0.6 collective-permute-done.11.own1.refs_3_
  38.2 1.4 %collective-permute-start.12 = (bf16[1024,256]{1,0:T(8,128)(2,1)S(1)}, bf16[1024,256]{1,0:T(8,128)(2,1)S(1)}, u32[]{:S(2)}, u32[]{:S(2)}) collective-permute-start(bf16[1024,256]{1,0:T(8,128)(2,1)S(1)} %pad_maximum_fusion.1), channel_id=1, source_target_pairs={{0,32},{32,0},{64,96},{96,64},{128,160},{160,128},{192,224},{224,1... | collective-permute-start | bytes 1572872 | tf_op jit(solution)/shard_map/ppermute | solution.py:273
  39.7 7.0 %collective-permute-start.4 = (bf16[512,256]{1,0:T(8,128)(2,1)S(1)}, bf16[512,256]{1,0:T(8,128)(2,1)S(1)}, u32[]{:S(2)}, u32[]{:S(2)}) collective-permute-start(bf16[512,256]{1,0:T(8,128)(2,1)S(1)} %pad_maximum_fusion.3.e_ref.refs_0_), channel_id=1, source_target_pairs={{0,128},{32,160},{64,192},{96,224},{128,0},{160,32},{192,64},{224,... | collective-permute-start | bytes 786440 | tf_op jit(solution)/shard_map/ppermute | solution.py:276
  46.7 14.4 %shard_map.85 = (f32[2048,128]{1,0:T(8,128)S(1)}, f32[2048,1]{1,0:T(8,128)S(1)}, f32[2048,1]{1,0:T(8,128)S(1)}, f32[8,2]{1,0:T(8,128)S(1)}) custom-call(s32[2]{0:T(128)S(1)} %pad_add_fusion.1.meta, bf16[1024,256]{1,0:T(8,128)(2,1)S(1)} %get-tuple-element.80.q_ref, ...), custom_call_target="tpu_custom_call", output_to_operand_aliasing={{0}: (4, {}), {1}: (5, {}), {2}: (6, {}), {3}: (7, {})} | custom-call | flops 1073741824 | bytes 1048576 | tf_op jit(solution)/shard_map/pallas_call | solution.py:252
  61.1 27.2 %shard_map.86 = (f32[2048,128]{1,0:T(8,128)S(1)}, f32[2048,1]{1,0:T(8,128)S(1)}, f32[2048,1]{1,0:T(8,128)S(1)}, f32[8,2]{1,0:T(8,128)S(1)}) custom-call(s32[1]{0:T(128)} %bitcast.5.meta, bf16[1024,256]{1,0:T(8,128)(2,1)S(1)} %get-tuple-element.80.q_ref, ...), custom_call_target="tpu_custom_call", output_to_operand_aliasing={{0}: (5, {}), {1}: (6, {}), {2}: (7, {}), {3}: (8, {})} | custom-call | flops 2147483648 | bytes 1048576 | tf_op jit(solution)/shard_map/pallas_call | solution.py:252
  88.5 1.9 %collective-permute-done.14.refs_12_.there = bf16[1024,256]{1,0:T(8,128)(2,1)S(1)} collective-permute-done((bf16[1024,256]{1,0:T(8,128)(2,1)S(1)}, bf16[1024,256]{1,0:T(8,128)(2,1)S(1)}, u32[]{:S(2)}, u32[]{:S(2)}) %collective-permute-start.14) | collective-permute-done | bytes 524320 | tf_op jit(solution)/shard_map/ppermute | solution.py:273
  90.4 0.9 shard_map.87
  91.3 1.3 %collective-permute-start.15 = (bf16[256,256]{1,0:T(8,128)(2,1)S(1)}, bf16[256,256]{1,0:T(8,128)(2,1)S(1)}, u32[]{:S(2)}, u32[]{:S(2)}) collective-permute-start(bf16[256,256]{1,0:T(8,128)(2,1)S(1)} %get-tuple-element.142), channel_id=1, source_target_pairs={{0,4},{1,5},{2,6},{3,7},{4,0},{5,1},{6,2},{7,3},{8,12},{9,13},{10,... | collective-permute-start | bytes 393224 | tf_op jit(solution)/shard_map/ppermute | solution.py:270
  92.6 28.3 %shard_map.88 = (f32[2048,128]{1,0:T(8,128)S(1)}, f32[2048,1]{1,0:T(8,128)S(1)}, f32[2048,1]{1,0:T(8,128)S(1)}, f32[8,2]{1,0:T(8,128)S(1)}, bf16[1024,256]{1,0:T(8,128)(2,1)}) custom-call(s32[1]{0:T(128)} %bitcast.6.meta, bf16[1024,256]{1,0:T(8,128)(2,1)S(1)} %get-tuple-element.80.q_ref, ...), custom_call_target="tpu_custom_call", output_to_operand_aliasing={{0}: (5, {}), {1}: (6, {}), {2}: (7, {}), {3}: (8, {})} | custom-call | flops 2147483648 | bytes 1048576 | tf_op jit(solution)/shard_map/pallas_call | solution.py:252
  120.9 1.4 %shard_map.89 = (bf16[256,256]{1,0:T(8,128)(2,1)}, bf16[256,256]{1,0:T(8,128)(2,1)}, f32[2,2]{1,0:T(2,128)}, f32[2,2]{1,0:T(2,128)}) custom-call(s32[3]{0:T(128)S(1)} %pad_add_fusion.meta, bf16[256,256]{1,0:T(8,128)(2,1)S(1)} %get-tuple-element.141.own, bf16[256,256]{1,0:T(8,128)(2,1)S(1)} %collective-permute-done.15.oth), custom_call_target="tpu_custom_call" | custom-call | bytes 1048576 | tf_op jit(solution)/shard_map/pallas_call | solution.py:252
  (34 shorter events, 1.2 us)
Async XLA Ops:
  0.7 12.9 %copy-start = (bf16[1024,256]{1,0:T(8,128)(2,1)S(1)}, bf16[1024,256]{1,0:T(8,128)(2,1)}, u32[]{:S(2)}) copy-start(bf16[1024,256]{1,0:T(8,128)(2,1)} %q_ref.1) | copy-start | bytes 1572868
  1.6 6.8 %collective-permute-start.1 = (bf16[128,256]{1,0:T(8,128)(2,1)S(1)}, bf16[128,256]{1,0:T(8,128)(2,1)S(1)}, u32[]{:S(2)}, u32[]{:S(2)}) collective-permute-start(bf16[128,256]{1,0:T(8,128)(2,1)S(1)} %get-tuple-element.148), channel_id=1, source_target_pairs={{0,4},{1,5},{2,6},{3,7},{4,0},{5,1},{6,2},{7,3},{8,12},{9,13},{10,... | collective-permute-start | bytes 196616 | tf_op jit(solution)/shard_map/ppermute | solution.py:270
  4.4 4.3 %collective-permute-start.2 = (bf16[128,256]{1,0:T(8,128)(2,1)S(1)}, bf16[128,256]{1,0:T(8,128)(2,1)S(1)}, u32[]{:S(2)}, u32[]{:S(2)}) collective-permute-start(bf16[128,256]{1,0:T(8,128)(2,1)S(1)} %get-tuple-element.148), channel_id=1, source_target_pairs={{0,6},{1,7},{2,4},{3,5},{4,2},{5,3},{6,0},{7,1},{8,14},{9,15},{10,... | collective-permute-start | bytes 196616 | tf_op jit(solution)/shard_map/ppermute | solution.py:270
  5.3 3.1 %collective-permute-start = (bf16[128,256]{1,0:T(8,128)(2,1)S(1)}, bf16[128,256]{1,0:T(8,128)(2,1)S(1)}, u32[]{:S(2)}, u32[]{:S(2)}) collective-permute-start(bf16[128,256]{1,0:T(8,128)(2,1)S(1)} %get-tuple-element.147), channel_id=1, source_target_pairs={{0,2},{1,3},{2,0},{3,1},{4,6},{5,7},{6,4},{7,5},{8,10},{9,11},{10,... | collective-permute-start | bytes 196616 | tf_op jit(solution)/shard_map/ppermute | solution.py:270
  5.4 0.7 copy-start.1
  8.8 3.4 %collective-permute-start.3 = (bf16[512,256]{1,0:T(8,128)(2,1)S(1)}, bf16[512,256]{1,0:T(8,128)(2,1)S(1)}, u32[]{:S(2)}, u32[]{:S(2)}) collective-permute-start(bf16[512,256]{1,0:T(8,128)(2,1)S(1)} %pad_maximum_fusion.3.e_ref.refs_0_), channel_id=1, source_target_pairs={{0,32},{32,0},{64,96},{96,64},{128,160},{160,128},{192,224},{224,1... | collective-permute-start | bytes 786440 | tf_op jit(solution)/shard_map/ppermute | solution.py:273
  10.9 17.4 %collective-permute-start.7 = (bf16[512,256]{1,0:T(8,128)(2,1)S(1)}, bf16[512,256]{1,0:T(8,128)(2,1)S(1)}, u32[]{:S(2)}, u32[]{:S(2)}) collective-permute-start(bf16[512,256]{1,0:T(8,128)(2,1)S(1)} %pad_maximum_fusion.3.e_ref.refs_0_), channel_id=1, source_target_pairs={{0,1},{1,0},{2,3},{3,2},{4,5},{5,4},{6,7},{7,6},{8,9},{9,8},{10,11... | collective-permute-start | bytes 786440 | tf_op jit(solution)/shard_map/ppermute | solution.py:270
  12.1 16.2 %collective-permute-start.5 = (bf16[512,256]{1,0:T(8,128)(2,1)S(1)}, bf16[512,256]{1,0:T(8,128)(2,1)S(1)}, u32[]{:S(2)}, u32[]{:S(2)}) collective-permute-start(bf16[512,256]{1,0:T(8,128)(2,1)S(1)} %pad_maximum_fusion.3.e_ref.refs_0_), channel_id=1, source_target_pairs={{0,64},{32,96},{64,128},{96,160},{128,192},{160,224},{192,0},{224,... | collective-permute-start | bytes 786440 | tf_op jit(solution)/shard_map/ppermute | solution.py:276
  12.1 16.2 %collective-permute-start.6 = (bf16[512,256]{1,0:T(8,128)(2,1)S(1)}, bf16[512,256]{1,0:T(8,128)(2,1)S(1)}, u32[]{:S(2)}, u32[]{:S(2)}) collective-permute-start(bf16[512,256]{1,0:T(8,128)(2,1)S(1)} %pad_maximum_fusion.3.e_ref.refs_0_), channel_id=1, source_target_pairs={{0,192},{32,224},{64,0},{96,32},{128,64},{160,96},{192,128},{224,1... | collective-permute-start | bytes 786440 | tf_op jit(solution)/shard_map/ppermute | solution.py:276
  28.4 2.5 %collective-permute-start.8 = (bf16[1024,256]{1,0:T(8,128)(2,1)S(1)}, bf16[1024,256]{1,0:T(8,128)(2,1)S(1)}, u32[]{:S(2)}, u32[]{:S(2)}) collective-permute-start(bf16[1024,256]{1,0:T(8,128)(2,1)S(1)} %pad_maximum_fusion), channel_id=1, source_target_pairs={{0,32},{32,0},{64,96},{96,64},{128,160},{160,128},{192,224},{224,1... | collective-permute-start | bytes 1572872 | tf_op jit(solution)/shard_map/ppermute | solution.py:273
  29.3 8.2 %collective-permute-start.10 = (bf16[512,256]{1,0:T(8,128)(2,1)S(1)}, bf16[512,256]{1,0:T(8,128)(2,1)S(1)}, u32[]{:S(2)}, u32[]{:S(2)}) collective-permute-start(bf16[512,256]{1,0:T(8,128)(2,1)S(1)} %collective-permute-done.7.e_ref.refs_1_), channel_id=1, source_target_pairs={{0,64},{32,96},{64,128},{96,160},{128,192},{160,224},{192,0},{224,... | collective-permute-start | bytes 786440 | tf_op jit(solution)/shard_map/ppermute | solution.py:276
  29.4 8.8 %collective-permute-start.11 = (bf16[512,256]{1,0:T(8,128)(2,1)S(1)}, bf16[512,256]{1,0:T(8,128)(2,1)S(1)}, u32[]{:S(2)}, u32[]{:S(2)}) collective-permute-start(bf16[512,256]{1,0:T(8,128)(2,1)S(1)} %collective-permute-done.7.e_ref.refs_1_), channel_id=1, source_target_pairs={{0,192},{32,224},{64,0},{96,32},{128,64},{160,96},{192,128},{224,1... | collective-permute-start | bytes 786440 | tf_op jit(solution)/shard_map/ppermute | solution.py:276
  38.2 22.9 %collective-permute-start.12 = (bf16[1024,256]{1,0:T(8,128)(2,1)S(1)}, bf16[1024,256]{1,0:T(8,128)(2,1)S(1)}, u32[]{:S(2)}, u32[]{:S(2)}) collective-permute-start(bf16[1024,256]{1,0:T(8,128)(2,1)S(1)} %pad_maximum_fusion.1), channel_id=1, source_target_pairs={{0,32},{32,0},{64,96},{96,64},{128,160},{160,128},{192,224},{224,1... | collective-permute-start | bytes 1572872 | tf_op jit(solution)/shard_map/ppermute | solution.py:273
  39.6 7.1 %collective-permute-start.13 = (bf16[512,256]{1,0:T(8,128)(2,1)S(1)}, bf16[512,256]{1,0:T(8,128)(2,1)S(1)}, u32[]{:S(2)}, u32[]{:S(2)}) collective-permute-start(bf16[512,256]{1,0:T(8,128)(2,1)S(1)} %collective-permute-done.7.e_ref.refs_1_), channel_id=1, source_target_pairs={{0,32},{32,0},{64,96},{96,64},{128,160},{160,128},{192,224},{224,1... | collective-permute-start | bytes 786440 | tf_op jit(solution)/shard_map/ppermute | solution.py:273
  39.7 48.6 %collective-permute-start.4 = (bf16[512,256]{1,0:T(8,128)(2,1)S(1)}, bf16[512,256]{1,0:T(8,128)(2,1)S(1)}, u32[]{:S(2)}, u32[]{:S(2)}) collective-permute-start(bf16[512,256]{1,0:T(8,128)(2,1)S(1)} %pad_maximum_fusion.3.e_ref.refs_0_), channel_id=1, source_target_pairs={{0,128},{32,160},{64,192},{96,224},{128,0},{160,32},{192,64},{224,... | collective-permute-start | bytes 786440 | tf_op jit(solution)/shard_map/ppermute | solution.py:276
  46.7 41.6 %collective-permute-start.9 = (bf16[512,256]{1,0:T(8,128)(2,1)S(1)}, bf16[512,256]{1,0:T(8,128)(2,1)S(1)}, u32[]{:S(2)}, u32[]{:S(2)}) collective-permute-start(bf16[512,256]{1,0:T(8,128)(2,1)S(1)} %collective-permute-done.7.e_ref.refs_1_), channel_id=1, source_target_pairs={{0,128},{32,160},{64,192},{96,224},{128,0},{160,32},{192,64},{224,... | collective-permute-start | bytes 786440 | tf_op jit(solution)/shard_map/ppermute | solution.py:276
  88.4 2.0 %collective-permute-start.14 = (bf16[1024,256]{1,0:T(8,128)(2,1)S(1)}, bf16[1024,256]{1,0:T(8,128)(2,1)S(1)}, u32[]{:S(2)}, u32[]{:S(2)}) collective-permute-start(bf16[1024,256]{1,0:T(8,128)(2,1)S(1)} %pad_maximum_fusion.2), channel_id=1, source_target_pairs={{0,32},{32,0},{64,96},{96,64},{128,160},{160,128},{192,224},{224,1... | collective-permute-start | bytes 1572872 | tf_op jit(solution)/shard_map/ppermute | solution.py:273
  91.3 29.6 %collective-permute-start.15 = (bf16[256,256]{1,0:T(8,128)(2,1)S(1)}, bf16[256,256]{1,0:T(8,128)(2,1)S(1)}, u32[]{:S(2)}, u32[]{:S(2)}) collective-permute-start(bf16[256,256]{1,0:T(8,128)(2,1)S(1)} %get-tuple-element.142), channel_id=1, source_target_pairs={{0,4},{1,5},{2,6},{3,7},{4,0},{5,1},{6,2},{7,3},{8,12},{9,13},{10,... | collective-permute-start | bytes 393224 | tf_op jit(solution)/shard_map/ppermute | solution.py:270

commit v3 on v2

--- a/solution.py
+++ b/solution.py
@@ -90,11 +90,61 @@
         bound_ref[:, 1:2] = jnp.full((8, 1), lowest)
 
 
-def near_kernel(z, meta, q_ref, e_ref, x_ref, *refs):
+def fill(meta, arrays, kv_ref, units):
+    for u, unit in enumerate(units):
+        for j, choices in enumerate(unit):
+            for use, (i, row) in enumerate(choices):
+                wanted = meta[0] > u
+                if len(choices) > 1:
+                    wanted = jnp.logical_and(wanted, meta[1] == use)
+
+                @pl.when(wanted)
+                def _():
+                    at = (2 * u + j) * SEG
+                    kv_ref[at : at + SEG] = arrays[i][row : row + SEG]
+
+
+def norm_of(kv_ref, count):
+    norms = [longest(kv_ref[at : at + 2 * SEG, :HD]) for at in range(0, kv_ref.shape[0], 2 * SEG)]
+    norm = jnp.where(count > 0, norms[0], 0.0)
+    for u in range(1, len(norms)):
+        norm = jnp.maximum(norm, jnp.where(count > u, norms[u], 0.0))
+    return norm
+
+
+def units_quick(q_ref, state, kv_ref, count):
+    tiles = q_ref.shape[0] // TN
+
+    def step(i):
+        keys = rows_at((i // tiles) * 2 * SEG, 2 * SEG)
+        for h in range(2):
+            fast(q_ref, state, h, (i % tiles) * TN, TN, kv_ref[keys, :HD], kv_ref[keys, HD:])
+
+    loop(0, count * tiles, step)
+
+
+def units_careful(q_ref, state, kv_ref, count):
+    few = q_ref.shape[0] // TS
+
+    def step(i):
+        keys = rows_at((i // few) * SEG, SEG)
+        for h in range(2):
+            slow(q_ref, state, h, (i % few) * TS, TS, kv_ref[keys, :HD], kv_ref[keys, HD:])
+
+    loop(0, 2 * count * few, step)
+
+
+def near_kernel(z, units, meta, q_ref, e_ref, x_ref, *refs):
+    count = 0
+    if units:
+        kv_ref, arrays = refs[-1], refs[: len(refs) - 10]
+        refs = refs[:-1]
+        count = meta[0]
+        fill(meta, arrays, kv_ref, units)
     state, page_ref = refs[-5:-1], refs[-1]
     acc_ref, shift_ref, total_ref, bound_ref = state
     rows = q_ref.shape[0]
-    core, dec = meta[0], meta[1]
+    core, dec = meta[2], meta[3]
     if z == 0:
         refs[0][...] = q_ref[...]
         acc_ref[...] = jnp.zeros_like(acc_ref)
@@ -134,6 +184,8 @@
                 fast(q_ref, state, h, i * TQ, TQ, x_ref[:, :HD], x_ref[:, HD:])
 
         loop(0, jnp.where(core == 1, rows // TQ, 0), extra)
+        if units:
+            units_quick(q_ref, state, kv_ref, count)
 
     def careful():
         lane = lax.broadcasted_iota(jnp.int32, (1, SEG), 1)
@@ -150,12 +202,17 @@
 
         loop(0, rows // TS, diagonal)
         loop(0, jnp.where(core == 1, rows // TS, 0), extra)
+        if units:
+            units_careful(q_ref, state, kv_ref, count)
 
     key_norm = jnp.maximum(longest(e_ref[:, :HD]), longest(x_ref[:, :HD]))
+    if units:
+        key_norm = jnp.maximum(key_norm, norm_of(kv_ref, count))
     guarded(state, key_norm, quick, careful)
 
 
-def next_kernel(last, meta, q_ref, own0, own1, there, *refs):
+def next_kernel(n, units, last, meta, q_ref, *refs):
+    arrays = refs[:n]
     if last:
         state, out_ref, kv_ref = refs[-6:-2], *refs[-2:]
     else:
@@ -163,36 +220,14 @@
     rows = q_ref.shape[0]
     count = meta[0]
 
-    for j, own in enumerate((own0, own1)):
-
-        @pl.when(count > j)
-        def _():
-            kv_ref[2 * j * SEG : (2 * j + 1) * SEG] = own[...]
-            kv_ref[(2 * j + 1) * SEG : (2 * j + 2) * SEG] = there[j * SEG : (j + 1) * SEG]
-
     @pl.when(count > 0)
     def _():
-        tiles = rows // TN
-
-        def step(i):
-            keys = rows_at((i // tiles) * 2 * SEG, 2 * SEG)
-            for h in range(2):
-                fast(q_ref, state, h, (i % tiles) * TN, TN, kv_ref[keys, :HD], kv_ref[keys, HD:])
-
-        few = rows // TS
-
-        def slow_step(i):
-            keys = rows_at((i // few) * SEG, SEG)
-            for h in range(2):
-                slow(q_ref, state, h, (i % few) * TS, TS, kv_ref[keys, :HD], kv_ref[keys, HD:])
-
-        norms = [longest(x[:, :HD]) for x in (own0, own1, there)]
-        key_norm = jnp.maximum(jnp.maximum(norms[0], norms[1]), norms[2])
+        fill(meta, arrays, kv_ref, units)
         guarded(
             state,
-            key_norm,
-            lambda: loop(0, count * tiles, step),
-            lambda: loop(0, 2 * count * few, slow_step),
+            norm_of(kv_ref, count),
+            lambda: units_quick(q_ref, state, kv_ref, count),
+            lambda: units_careful(q_ref, state, kv_ref, count),
         )
 
     if last:
@@ -206,9 +241,9 @@
 
 def pick_kernel(meta, *refs):
     pages, outs = refs[:-2], refs[-2:]
-    own, (e0, e1, ab0, ab1, cc) = pages[:8], pages[8:]
+    own, (e0, e1, c0, c1, ab0, ab1) = pages[:8], pages[8:]
     places = [(ref, 0) for ref in (*own, e0, e1)]
-    places += [(ab0, SEG), (ab1, SEG), (cc, 0), (cc, SEG), (ab0, 0), (ab1, 0)]
+    places += [(ab0, SEG), (ab1, SEG), (c0, 0), (c1, 0), (ab0, 0), (ab1, 0)]
     for d in range(2):
         for j in range(2):
             at = meta[2 * d + j]
@@ -248,14 +283,13 @@
 PARAMS = pltpu.CompilerParams(vmem_limit_bytes=10 * 2**20)
 
 
-def call(kernel, meta, arrays, outs, work=0, **more):
+def call(kernel, meta, arrays, outs, **more):
     return pl.pallas_call(
         kernel,
         in_specs=[SMEM] + [VMEM] * len(arrays),
         out_specs=[VMEM] * len(outs),
         out_shape=[jax.ShapeDtypeStruct(s, t) for s, t in outs],
         compiler_params=PARAMS,
-        cost_estimate=pl.CostEstimate(flops=4 * HD * work, transcendentals=work, bytes_accessed=2**20),
         **more,
     )(meta, *arrays)
 
@@ -301,71 +335,81 @@
         ((2 * tok, 1), jnp.float32),
         ((8, 2), jnp.float32),
     ]
-    place = jnp.stack([core, dec]).astype(i32)
-    near_by = jnp.where(y == 3, 2, jnp.where(y >= 1, 1, 0)).astype(i32).reshape(1)
-    far = jnp.where(y >= 2, 2, 0).astype(i32).reshape(1)
-    e0, at, flags, place, near_by, far = lax.optimization_barrier(
-        (e0, at, flags, place, near_by, far)
+    def meta_of(count, other):
+        return jnp.stack([count + 0 * y, other + 0 * y, core, dec]).astype(i32)
+
+    top = jnp.where(y == 3, 1, 0)
+    some = jnp.where(y >= 1, 1, 0)
+    place = meta_of(0, 0)
+    above = meta_of(top, top)
+    below = meta_of(some, top)
+    below_above = meta_of(some + top, top)
+    far = meta_of(jnp.where(y >= 2, 1, 0), 0)
+    e0, at, flags, place, above, below, below_above, far = lax.optimization_barrier(
+        (e0, at, flags, place, above, below, below_above, far)
     )
     e0_there = over_core(e0)
     e1 = over_dec(e0, 1)
-    e0_y, e0_there = lax.optimization_barrier((e0, e0_there))
-    a0, b0 = over_y(e0_y, 1), over_y(e0_y, 3)
-    score_count = 2 * tok * SEG
-
-    def near(z, q, e, x, state=()):
+    a0, b0 = over_y(e0, 1), over_y(e0, 3)
+    e0_far, e0_there = lax.optimization_barrier((e0, e0_there))
+    c0 = over_y(e0_far, 2)
+
+    def near(z, meta, q, e, x, arrays=(), units=(), state=()):
+        n = len(arrays)
+        kv = [pltpu.VMEM((2 * len(units) * SEG, 2 * HD), jnp.bfloat16)] if units else []
         return call(
-            functools.partial(near_kernel, z),
-            place,
-            [q, e, x, *state],
+            functools.partial(near_kernel, z, units),
+            meta,
+            [q, e, x, *arrays, *state],
             [((tok, 2 * HD), jnp.bfloat16)] * (z == 0) + state_types,
-            2 * score_count,
-            scratch_shapes=[pltpu.VMEM((SEG, 2 * HD), jnp.bfloat16)],
-            input_output_aliases={4 + i: i for i in range(len(state))},
+            scratch_shapes=[pltpu.VMEM((SEG, 2 * HD), jnp.bfloat16), *kv],
+            input_output_aliases={n + 4 + i: i for i in range(len(state))},
         )
 
-    def more(count, own0, own1, there, state, last=False):
+    def more(meta, arrays, units, state, last=False):
+        n = len(arrays)
         return call(
-            functools.partial(next_kernel, last),
-            count,
-            [q, own0, own1, there, *state],
+            functools.partial(next_kernel, n, units, last),
+            meta,
+            [q, *arrays, *state],
             state_types + [((tok, 2 * HD), jnp.bfloat16)] * last,
-            4 * score_count,
-            scratch_shapes=[pltpu.VMEM((4 * SEG, 2 * HD), jnp.bfloat16)],
-            input_output_aliases={5 + i: i for i in range(4)},
+            scratch_shapes=[pltpu.VMEM((2 * len(units) * SEG, 2 * HD), jnp.bfloat16)],
+            input_output_aliases={n + 2 + i: i for i in range(4)},
         )
 
     def both(first, second):
         return over_core(jnp.concatenate([first, second], axis=0))
 
-    q, *state = near(0, queries, e0, e0_there)
-    e0_far, state = lax.optimization_barrier((e0, state))
-    c0 = over_y(e0_far, 2)
-    a0, b0, e1, state = lax.optimization_barrier((a0, b0, e1, state))
+    pair = [((0, 0),), ((1, 0),)]
+    crossed = [((0, 0), (2, SEG)), ((2, 0),)]
+    q, *state = near(0, place, queries, e0, e0_there)
+    state = more(above, [a0, b0], [pair], state)
+    a0, b0, c0, e1, state = lax.optimization_barrier((a0, b0, c0, e1, state))
     ab0_there = both(a0, b0)
     a1, b1 = over_y(e1, 1), over_y(e1, 3)
-    e1_there = over_core(e1)
-    state = more(near_by, a0, b0, ab0_there, state)
-    e1_far, state = lax.optimization_barrier((e1, state))
-    c1 = over_y(e1_far, 2)
+    e1_there, c0_there = over_core(e1), over_core(c0)
+    e1_there, c0_there, state = lax.optimization_barrier((e1_there, c0_there, state))
+    state = near(1, below, q, e1, e1_there, [a0, b0, ab0_there], [crossed], state)
     a1, b1, state = lax.optimization_barrier((a1, b1, state))
     ab1_there = both(a1, b1)
-    state = near(1, q, e1, e1_there, state)
-    state = more(near_by, a1, b1, ab1_there, state)
-    c0, c1, state = lax.optimization_barrier((c0, c1, state))
-    c_there = both(c0, c1)
+    e1_far, a1 = lax.optimization_barrier((e1, a1))
+    c1 = over_y(e1_far, 2)
+    state = more(far, [c0, c0_there], [pair], state)
+    state = more(below_above, [a1, b1, ab1_there], [crossed, pair], state)
+    c1, state = lax.optimization_barrier((c1, state))
+    c1_there = over_core(c1)
 
     block = ((2 * PAGE, 2 * HD), jnp.bfloat16)
     at, state = lax.optimization_barrier((at, state))
     mine, to_head = call(
         pick_kernel,
         at,
-        [e0, e1, b0, b1, c0, c1, a0, a1, e0_there, e1_there, ab0_there, ab1_there, c_there],
+        [e0, e1, b0, b1, c0, c1, a0, a1, e0_there, e1_there, c0_there, c1_there, ab0_there, ab1_there],
         [block] * 2,
     )
     state, mine = lax.optimization_barrier((state, mine))
     oth = over_dec(to_head, 4)
-    *_, attended = more(far, c0, c1, c_there, state, True)
+    *_, attended = more(far, [c1, c1_there], [pair], state, True)
     cache_keys, cache_values, key_scales, value_scales = call(
         cache_kernel,
         flags,

time: 122 us -> 129 us (1.057)
  the two profiles are of different devices: /device:TPU:185 before, /device:TPU:17 now
where the time goes in v3:
time: 129 us
  Pallas kernels  89.8 us (70%)
  starting transfers between devices  32.3 us (25%)
  waiting for transfers between devices  4.06 us (3%)
    pallas_call x8, Pallas kernels, call(): pl.pallas_call(kernel, in_specs=[SMEM] + [VMEM] * len(arrays), out_specs=...  89.8 us
    ppermute x6, starting transfers between devices, over_y(): return lax.ppermute(x, 'blk', [(i, (i + 2 * d) % 8) for i in range(8)])  17.4 us
    ppermute x5, starting transfers between devices, over_dec(): return lax.ppermute(x, 'dec', [(i, i ^ m) for i in range(8)])  11.9 us
    ppermute x6, starting transfers between devices, over_core(): return lax.ppermute(x, 'blk', [(i, i ^ 1) for i in range(8)])  3.07 us
  transfers between devices with their start and end apart: 17, of which 3 were waited for; matrix products, arithmetic and copies ran while one was open for 1% of the time, Pallas kernels for 68%

profile of v3, /device:TPU:17, one launch (start us, length us, event | category | flops | bytes accessed | tf_op | source)
XLA Modules:
  0.0 129.0 jit_solution(11163641321246686867)
XLA Ops:
  0.7 0.8 fusion.8
  1.5 2.8 %collective-permute-start.1 = (bf16[128,256]{1,0:T(8,128)(2,1)S(1)}, bf16[128,256]{1,0:T(8,128)(2,1)S(1)}, u32[]{:S(2)}, u32[]{:S(2)}) collective-permute-start(bf16[128,256]{1,0:T(8,128)(2,1)S(1)} %get-tuple-element.156), channel_id=1, source_target_pairs={{0,4},{1,5},{2,6},{3,7},{4,0},{5,1},{6,2},{7,3},{8,12},{9,13},{10,... | collective-permute-start | bytes 196616 | tf_op jit(solution)/shard_map/ppermute | solution.py:304
  4.4 0.9 collective-permute-start.2
  5.5 0.2 compare_reduce_fusion
  5.7 0.2 fusion
  6.2 2.2 %collective-permute-done = bf16[128,256]{1,0:T(8,128)(2,1)S(1)} collective-permute-done((bf16[128,256]{1,0:T(8,128)(2,1)S(1)}, bf16[128,256]{1,0:T(8,128)(2,1)S(1)}, u32[]{:S(2)}, u32[]{:S(2)}) %collective-permute-start) | collective-permute-done | bytes 65568 | tf_op jit(solution)/shard_map/ppermute | solution.py:304
  8.3 0.3 collective-permute-done.2
  8.7 2.2 %collective-permute-start.3 = (bf16[512,256]{1,0:T(8,128)(2,1)S(1)}, bf16[512,256]{1,0:T(8,128)(2,1)S(1)}, u32[]{:S(2)}, u32[]{:S(2)}) collective-permute-start(bf16[512,256]{1,0:T(8,128)(2,1)S(1)} %pad_maximum_fusion.2.e_ref.refs_0_), channel_id=1, source_target_pairs={{0,32},{32,0},{64,96},{96,64},{128,160},{160,128},{192,224},{224,1... | collective-permute-start | bytes 786440 | tf_op jit(solution)/shard_map/ppermute | solution.py:307
  10.9 1.0 collective-permute-start.4
  11.9 0.5 collective-permute-start.5
  12.4 6.9 %collective-permute-start.7 = (bf16[512,256]{1,0:T(8,128)(2,1)S(1)}, bf16[512,256]{1,0:T(8,128)(2,1)S(1)}, u32[]{:S(2)}, u32[]{:S(2)}) collective-permute-start(bf16[512,256]{1,0:T(8,128)(2,1)S(1)} %pad_maximum_fusion.2.e_ref.refs_0_), channel_id=1, source_target_pairs={{0,1},{1,0},{2,3},{3,2},{4,5},{5,4},{6,7},{7,6},{8,9},{9,8},{10,11... | collective-permute-start | bytes 786440 | tf_op jit(solution)/shard_map/ppermute | solution.py:304
  19.3 1.3 %collective-permute-start.6 = (bf16[512,256]{1,0:T(8,128)(2,1)S(1)}, bf16[512,256]{1,0:T(8,128)(2,1)S(1)}, u32[]{:S(2)}, u32[]{:S(2)}) collective-permute-start(bf16[512,256]{1,0:T(8,128)(2,1)S(1)} %pad_maximum_fusion.2.e_ref.refs_0_), channel_id=1, source_target_pairs={{0,128},{32,160},{64,192},{96,224},{128,0},{160,32},{192,64},{224,... | collective-permute-start | bytes 786440 | tf_op jit(solution)/shard_map/ppermute | solution.py:310
  20.6 14.8 %shard_map.83 = (bf16[1024,256]{1,0:T(8,128)(2,1)S(1)}, f32[2048,128]{1,0:T(8,128)S(1)}, f32[2048,1]{1,0:T(8,128)S(1)}, f32[2048,1]{1,0:T(8,128)S(1)}, f32[8,2]{1,0:T(8,128)S(1)}) custom-call(s32[4]{0:T(128)S(1)} %get-tuple-element.81.meta, bf16[1024,256]{1,0:T(8,128)(2,1)S(1)} %copy-done, bf16[512,256]{1,0:T(8,128)(2,1)S(1)} %pad_maximum_fusion.2.e_ref.refs_0_, ...), custom_call_target="tpu_custom_call" | custom-call | tf_op jit(solution)/shard_map/pallas_call | solution.py:287
  35.4 0.6 shard_map.84
  36.1 0.5 collective-permute-start.10
  36.7 14.5 %collective-permute-start.8 = (bf16[512,256]{1,0:T(8,128)(2,1)S(1)}, bf16[512,256]{1,0:T(8,128)(2,1)S(1)}, u32[]{:S(2)}, u32[]{:S(2)}) collective-permute-start(bf16[512,256]{1,0:T(8,128)(2,1)S(1)} %collective-permute-done.7.e_ref.refs_1_), channel_id=1, source_target_pairs={{0,64},{32,96},{64,128},{96,160},{128,192},{160,224},{192,0},{224,... | collective-permute-start | bytes 786440 | tf_op jit(solution)/shard_map/ppermute | solution.py:310
  51.2 27.7 %shard_map.85 = (f32[2048,128]{1,0:T(8,128)S(1)}, f32[2048,1]{1,0:T(8,128)S(1)}, f32[2048,1]{1,0:T(8,128)S(1)}, f32[8,2]{1,0:T(8,128)S(1)}) custom-call(s32[4]{0:T(128)S(1)} %get-tuple-element.96.meta, bf16[1024,256]{1,0:T(8,128)(2,1)S(1)} %get-tuple-element.84.q_ref, ...), custom_call_target="tpu_custom_call", output_to_operand_aliasing={{0}: (7, {}), {1}: (8, {}), {2}: (9, {}), {3}: (10, {})} | custom-call | tf_op jit(solution)/shard_map/pallas_call | solution.py:287
  79.2 14.4 %shard_map.86 = (f32[2048,128]{1,0:T(8,128)S(1)}, f32[2048,1]{1,0:T(8,128)S(1)}, f32[2048,1]{1,0:T(8,128)S(1)}, f32[8,2]{1,0:T(8,128)S(1)}) custom-call(s32[4]{0:T(128)S(1)} %get-tuple-element.80.meta, bf16[1024,256]{1,0:T(8,128)(2,1)S(1)} %get-tuple-element.84.q_ref, ...), custom_call_target="tpu_custom_call", output_to_operand_aliasing={{0}: (4, {}), {1}: (5, {}), {2}: (6, {}), {3}: (7, {})} | custom-call | tf_op jit(solution)/shard_map/pallas_call | solution.py:287
  93.6 14.5 %shard_map.87 = (f32[2048,128]{1,0:T(8,128)S(1)}, f32[2048,1]{1,0:T(8,128)S(1)}, f32[2048,1]{1,0:T(8,128)S(1)}, f32[8,2]{1,0:T(8,128)S(1)}) custom-call(s32[4]{0:T(128)S(1)} %get-tuple-element.115.meta, bf16[1024,256]{1,0:T(8,128)(2,1)S(1)} %get-tuple-element.84.q_ref, ...), custom_call_target="tpu_custom_call", output_to_operand_aliasing={{0}: (5, {}), {1}: (6, {}), {2}: (7, {}), {3}: (8, {})} | custom-call | tf_op jit(solution)/shard_map/pallas_call | solution.py:287
  108.2 1.5 %collective-permute-done.15.refs_11_.refs_1_ = bf16[512,256]{1,0:T(8,128)(2,1)S(1)} collective-permute-done((bf16[512,256]{1,0:T(8,128)(2,1)S(1)}, bf16[512,256]{1,0:T(8,128)(2,1)S(1)}, u32[]{:S(2)}, u32[]{:S(2)}) %collective-permute-start.15) | collective-permute-done | bytes 262176 | tf_op jit(solution)/shard_map/ppermute | solution.py:307
  109.8 0.9 shard_map.88
  110.7 1.3 collective-permute-start.16
  112.0 15.5 %shard_map.89 = (f32[2048,128]{1,0:T(8,128)S(1)}, f32[2048,1]{1,0:T(8,128)S(1)}, f32[2048,1]{1,0:T(8,128)S(1)}, f32[8,2]{1,0:T(8,128)S(1)}, bf16[1024,256]{1,0:T(8,128)(2,1)}) custom-call(s32[4]{0:T(128)S(1)} %get-tuple-element.80.meta, ...), custom_call_target="tpu_custom_call", output_to_operand_aliasing={{0}: (4, {}), {1}: (5, {}), {2}: (6, {}), {3}: (7, {})} | custom-call | tf_op jit(solution)/shard_map/pallas_call | solution.py:287
  127.5 1.4 %shard_map.90 = (bf16[256,256]{1,0:T(8,128)(2,1)}, bf16[256,256]{1,0:T(8,128)(2,1)}, f32[2,2]{1,0:T(2,128)}, f32[2,2]{1,0:T(2,128)}) custom-call(s32[3]{0:T(128)S(1)} %pad_add_fusion.meta, bf16[256,256]{1,0:T(8,128)(2,1)S(1)} %get-tuple-element.149.own, bf16[256,256]{1,0:T(8,128)(2,1)S(1)} %collective-permute-done.16.oth), custom_call_target="tpu_custom_call" | custom-call | tf_op jit(solution)/shard_map/pallas_call | solution.py:287
  (38 shorter events, 1.2 us)
Async XLA Ops:
  0.7 4.8 %copy-start.1 = (s32[64]{0:T(128)S(1)}, s32[64]{0:T(128)}, u32[]{:S(2)}) copy-start(s32[64]{0:T(128)} %param.7) | copy-start | bytes 772
  1.5 19.1 %copy-start = (bf16[1024,256]{1,0:T(8,128)(2,1)S(1)}, bf16[1024,256]{1,0:T(8,128)(2,1)}, u32[]{:S(2)}) copy-start(bf16[1024,256]{1,0:T(8,128)(2,1)} %q_ref.1) | copy-start | bytes 1572868
  1.5 6.8 %collective-permute-start.1 = (bf16[128,256]{1,0:T(8,128)(2,1)S(1)}, bf16[128,256]{1,0:T(8,128)(2,1)S(1)}, u32[]{:S(2)}, u32[]{:S(2)}) collective-permute-start(bf16[128,256]{1,0:T(8,128)(2,1)S(1)} %get-tuple-element.156), channel_id=1, source_target_pairs={{0,4},{1,5},{2,6},{3,7},{4,0},{5,1},{6,2},{7,3},{8,12},{9,13},{10,... | collective-permute-start | bytes 196616 | tf_op jit(solution)/shard_map/ppermute | solution.py:304
  4.4 4.3 %collective-permute-start.2 = (bf16[128,256]{1,0:T(8,128)(2,1)S(1)}, bf16[128,256]{1,0:T(8,128)(2,1)S(1)}, u32[]{:S(2)}, u32[]{:S(2)}) collective-permute-start(bf16[128,256]{1,0:T(8,128)(2,1)S(1)} %get-tuple-element.156), channel_id=1, source_target_pairs={{0,6},{1,7},{2,4},{3,5},{4,2},{5,3},{6,0},{7,1},{8,14},{9,15},{10,... | collective-permute-start | bytes 196616 | tf_op jit(solution)/shard_map/ppermute | solution.py:304
  5.2 3.1 %collective-permute-start = (bf16[128,256]{1,0:T(8,128)(2,1)S(1)}, bf16[128,256]{1,0:T(8,128)(2,1)S(1)}, u32[]{:S(2)}, u32[]{:S(2)}) collective-permute-start(bf16[128,256]{1,0:T(8,128)(2,1)S(1)} %get-tuple-element.155), channel_id=1, source_target_pairs={{0,2},{1,3},{2,0},{3,1},{4,6},{5,7},{6,4},{7,5},{8,10},{9,11},{10,... | collective-permute-start | bytes 196616 | tf_op jit(solution)/shard_map/ppermute | solution.py:304
  8.7 10.6 %collective-permute-start.3 = (bf16[512,256]{1,0:T(8,128)(2,1)S(1)}, bf16[512,256]{1,0:T(8,128)(2,1)S(1)}, u32[]{:S(2)}, u32[]{:S(2)}) collective-permute-start(bf16[512,256]{1,0:T(8,128)(2,1)S(1)} %pad_maximum_fusion.2.e_ref.refs_0_), channel_id=1, source_target_pairs={{0,32},{32,0},{64,96},{96,64},{128,160},{160,128},{192,224},{224,1... | collective-permute-start | bytes 786440 | tf_op jit(solution)/shard_map/ppermute | solution.py:307
  10.9 24.5 %collective-permute-start.4 = (bf16[512,256]{1,0:T(8,128)(2,1)S(1)}, bf16[512,256]{1,0:T(8,128)(2,1)S(1)}, u32[]{:S(2)}, u32[]{:S(2)}) collective-permute-start(bf16[512,256]{1,0:T(8,128)(2,1)S(1)} %pad_maximum_fusion.2.e_ref.refs_0_), channel_id=1, source_target_pairs={{0,64},{32,96},{64,128},{96,160},{128,192},{160,224},{192,0},{224,... | collective-permute-start | bytes 786440 | tf_op jit(solution)/shard_map/ppermute | solution.py:310
  11.9 23.5 %collective-permute-start.5 = (bf16[512,256]{1,0:T(8,128)(2,1)S(1)}, bf16[512,256]{1,0:T(8,128)(2,1)S(1)}, u32[]{:S(2)}, u32[]{:S(2)}) collective-permute-start(bf16[512,256]{1,0:T(8,128)(2,1)S(1)} %pad_maximum_fusion.2.e_ref.refs_0_), channel_id=1, source_target_pairs={{0,192},{32,224},{64,0},{96,32},{128,64},{160,96},{192,128},{224,1... | collective-permute-start | bytes 786440 | tf_op jit(solution)/shard_map/ppermute | solution.py:310
  12.4 23.6 %collective-permute-start.7 = (bf16[512,256]{1,0:T(8,128)(2,1)S(1)}, bf16[512,256]{1,0:T(8,128)(2,1)S(1)}, u32[]{:S(2)}, u32[]{:S(2)}) collective-permute-start(bf16[512,256]{1,0:T(8,128)(2,1)S(1)} %pad_maximum_fusion.2.e_ref.refs_0_), channel_id=1, source_target_pairs={{0,1},{1,0},{2,3},{3,2},{4,5},{5,4},{6,7},{7,6},{8,9},{9,8},{10,11... | collective-permute-start | bytes 786440 | tf_op jit(solution)/shard_map/ppermute | solution.py:304
  19.3 16.7 %collective-permute-start.6 = (bf16[512,256]{1,0:T(8,128)(2,1)S(1)}, bf16[512,256]{1,0:T(8,128)(2,1)S(1)}, u32[]{:S(2)}, u32[]{:S(2)}) collective-permute-start(bf16[512,256]{1,0:T(8,128)(2,1)S(1)} %pad_maximum_fusion.2.e_ref.refs_0_), channel_id=1, source_target_pairs={{0,128},{32,160},{64,192},{96,224},{128,0},{160,32},{192,64},{224,... | collective-permute-start | bytes 786440 | tf_op jit(solution)/shard_map/ppermute | solution.py:310
  36.0 15.2 %collective-permute-start.12 = (bf16[1024,256]{1,0:T(8,128)(2,1)S(1)}, bf16[1024,256]{1,0:T(8,128)(2,1)S(1)}, u32[]{:S(2)}, u32[]{:S(2)}) collective-permute-start(bf16[1024,256]{1,0:T(8,128)(2,1)S(1)} %pad_maximum_fusion), channel_id=1, source_target_pairs={{0,32},{32,0},{64,96},{96,64},{128,160},{160,128},{192,224},{224,1... | collective-permute-start | bytes 1572872 | tf_op jit(solution)/shard_map/ppermute | solution.py:307
  36.1 15.1 %collective-permute-start.10 = (bf16[512,256]{1,0:T(8,128)(2,1)S(1)}, bf16[512,256]{1,0:T(8,128)(2,1)S(1)}, u32[]{:S(2)}, u32[]{:S(2)}) collective-permute-start(bf16[512,256]{1,0:T(8,128)(2,1)S(1)} %collective-permute-done.7.e_ref.refs_1_), channel_id=1, source_target_pairs={{0,32},{32,0},{64,96},{96,64},{128,160},{160,128},{192,224},{224,1... | collective-permute-start | bytes 786440 | tf_op jit(solution)/shard_map/ppermute | solution.py:307
  36.6 14.6 %collective-permute-start.11 = (bf16[512,256]{1,0:T(8,128)(2,1)S(1)}, bf16[512,256]{1,0:T(8,128)(2,1)S(1)}, u32[]{:S(2)}, u32[]{:S(2)}) collective-permute-start(bf16[512,256]{1,0:T(8,128)(2,1)S(1)} %collective-permute-done.6.refs_0_.refs_4_), channel_id=1, source_target_pairs={{0,32},{32,0},{64,96},{96,64},{128,160},{160,128},{192,224},{224,1... | collective-permute-start | bytes 786440 | tf_op jit(solution)/shard_map/ppermute | solution.py:307
  36.7 42.2 %collective-permute-start.8 = (bf16[512,256]{1,0:T(8,128)(2,1)S(1)}, bf16[512,256]{1,0:T(8,128)(2,1)S(1)}, u32[]{:S(2)}, u32[]{:S(2)}) collective-permute-start(bf16[512,256]{1,0:T(8,128)(2,1)S(1)} %collective-permute-done.7.e_ref.refs_1_), channel_id=1, source_target_pairs={{0,64},{32,96},{64,128},{96,160},{128,192},{160,224},{192,0},{224,... | collective-permute-start | bytes 786440 | tf_op jit(solution)/shard_map/ppermute | solution.py:310
  51.2 27.8 %collective-permute-start.9 = (bf16[512,256]{1,0:T(8,128)(2,1)S(1)}, bf16[512,256]{1,0:T(8,128)(2,1)S(1)}, u32[]{:S(2)}, u32[]{:S(2)}) collective-permute-start(bf16[512,256]{1,0:T(8,128)(2,1)S(1)} %collective-permute-done.7.e_ref.refs_1_), channel_id=1, source_target_pairs={{0,192},{32,224},{64,0},{96,32},{128,64},{160,96},{192,128},{224,1... | collective-permute-start | bytes 786440 | tf_op jit(solution)/shard_map/ppermute | solution.py:310
  79.0 14.6 %collective-permute-start.14 = (bf16[1024,256]{1,0:T(8,128)(2,1)S(1)}, bf16[1024,256]{1,0:T(8,128)(2,1)S(1)}, u32[]{:S(2)}, u32[]{:S(2)}) collective-permute-start(bf16[1024,256]{1,0:T(8,128)(2,1)S(1)} %pad_maximum_fusion.1), channel_id=1, source_target_pairs={{0,32},{32,0},{64,96},{96,64},{128,160},{160,128},{192,224},{224,1... | collective-permute-start | bytes 1572872 | tf_op jit(solution)/shard_map/ppermute | solution.py:307
  79.1 29.0 %collective-permute-start.13 = (bf16[512,256]{1,0:T(8,128)(2,1)S(1)}, bf16[512,256]{1,0:T(8,128)(2,1)S(1)}, u32[]{:S(2)}, u32[]{:S(2)}) collective-permute-start(bf16[512,256]{1,0:T(8,128)(2,1)S(1)} %collective-permute-done.7.e_ref.refs_1_), channel_id=1, source_target_pairs={{0,128},{32,160},{64,192},{96,224},{128,0},{160,32},{192,64},{224,... | collective-permute-start | bytes 786440 | tf_op jit(solution)/shard_map/ppermute | solution.py:310
  108.1 1.6 %collective-permute-start.15 = (bf16[512,256]{1,0:T(8,128)(2,1)S(1)}, bf16[512,256]{1,0:T(8,128)(2,1)S(1)}, u32[]{:S(2)}, u32[]{:S(2)}) collective-permute-start(bf16[512,256]{1,0:T(8,128)(2,1)S(1)} %collective-permute-done.13.refs_5_.refs_0_), channel_id=1, source_target_pairs={{0,32},{32,0},{64,96},{96,64},{128,160},{160,128},{192,224},{224,1... | collective-permute-start | bytes 786440 | tf_op jit(solution)/shard_map/ppermute | solution.py:307
  110.7 16.8 %collective-permute-start.16 = (bf16[256,256]{1,0:T(8,128)(2,1)S(1)}, bf16[256,256]{1,0:T(8,128)(2,1)S(1)}, u32[]{:S(2)}, u32[]{:S(2)}) collective-permute-start(bf16[256,256]{1,0:T(8,128)(2,1)S(1)} %get-tuple-element.150), channel_id=1, source_target_pairs={{0,4},{1,5},{2,6},{3,7},{4,0},{5,1},{6,2},{7,3},{8,12},{9,13},{10,... | collective-permute-start | bytes 393224 | tf_op jit(solution)/shard_map/ppermute | solution.py:304

commit v4 on v3

--- a/solution.py
+++ b/solution.py
@@ -112,13 +112,17 @@
     return norm
 
 
-def units_quick(q_ref, state, kv_ref, count):
-    tiles = q_ref.shape[0] // TN
+def units_quick(q_ref, state, kv_ref, count, finish=None):
+    tiles = q_ref.shape[0] // (2 * TN)
 
     def step(i):
         keys = rows_at((i // tiles) * 2 * SEG, 2 * SEG)
-        for h in range(2):
-            fast(q_ref, state, h, (i % tiles) * TN, TN, kv_ref[keys, :HD], kv_ref[keys, HD:])
+        for part in range(2):
+            row = (i % tiles) * 2 * TN + part * TN
+            for h in range(2):
+                fast(q_ref, state, h, row, TN, kv_ref[keys, :HD], kv_ref[keys, HD:])
+                if finish is not None:
+                    finish(h, row, TN)
 
     loop(0, count * tiles, step)
 
@@ -220,23 +224,35 @@
     rows = q_ref.shape[0]
     count = meta[0]
 
+    def finish(h, row, size):
+        r = rows_at(h * rows + row, size)
+        mean = state[0][r] * (1.0 / state[2][r])
+        out_ref[rows_at(row, size), h * HD : (h + 1) * HD] = mean.astype(jnp.bfloat16)
+
+    def finish_all():
+        def step(i):
+            for h in range(2):
+                finish(h, i * TN, TN)
+
+        loop(0, rows // TN, step)
+
+    def careful():
+        units_careful(q_ref, state, kv_ref, count)
+        if last:
+            finish_all()
+
     @pl.when(count > 0)
     def _():
         fill(meta, arrays, kv_ref, units)
         guarded(
             state,
             norm_of(kv_ref, count),
-            lambda: units_quick(q_ref, state, kv_ref, count),
-            lambda: units_careful(q_ref, state, kv_ref, count),
+            lambda: units_quick(q_ref, state, kv_ref, count, finish if last else None),
+            careful,
         )
 
     if last:
-        acc_ref, _, total_ref, _ = state
-        for h in range(2):
-            r = slice(h * rows, (h + 1) * rows)
-            out_ref[:, h * HD : (h + 1) * HD] = (acc_ref[r] * (1.0 / total_ref[r])).astype(
-                jnp.bfloat16
-            )
+        pl.when(count == 0)(finish_all)
 
 
 def pick_kernel(meta, *refs):
@@ -268,7 +284,7 @@
             for b, block in enumerate((own, oth)):
                 x = block[rows, kind * HD : (kind + 1) * HD].astype(jnp.float32)
                 x = jnp.where(filled, x, 0.0)
-                scale = jnp.max(jnp.abs(x)) + 1e-6
+                scale = jnp.max(jnp.abs(x), keepdims=True) + 1e-6
                 normed.append((x / scale).astype(jnp.bfloat16))
                 here = jnp.logical_and(row_at == j, col_at == (col if b == 0 else 1 - col))
                 scales[kind] = jnp.where(jnp.logical_and(here, filled), scale, scales[kind])
@@ -342,11 +358,11 @@
     some = jnp.where(y >= 1, 1, 0)
     place = meta_of(0, 0)
     above = meta_of(top, top)
-    below = meta_of(some, top)
     below_above = meta_of(some + top, top)
+    below_far = meta_of(some + jnp.where(y >= 2, 1, 0), top)
     far = meta_of(jnp.where(y >= 2, 1, 0), 0)
-    e0, at, flags, place, above, below, below_above, far = lax.optimization_barrier(
-        (e0, at, flags, place, above, below, below_above, far)
+    e0, at, flags, place, above, below_far, below_above, far = lax.optimization_barrier(
+        (e0, at, flags, place, above, below_far, below_above, far)
     )
     e0_there = over_core(e0)
     e1 = over_dec(e0, 1)
@@ -389,14 +405,24 @@
     a1, b1 = over_y(e1, 1), over_y(e1, 3)
     e1_there, c0_there = over_core(e1), over_core(c0)
     e1_there, c0_there, state = lax.optimization_barrier((e1_there, c0_there, state))
-    state = near(1, below, q, e1, e1_there, [a0, b0, ab0_there], [crossed], state)
+    distant = [((3, 0),), ((4, 0),)]
+    state = near(
+        1,
+        below_far,
+        q,
+        e1,
+        e1_there,
+        [a0, b0, ab0_there, c0, c0_there],
+        [crossed, distant],
+        state,
+    )
     a1, b1, state = lax.optimization_barrier((a1, b1, state))
     ab1_there = both(a1, b1)
-    e1_far, a1 = lax.optimization_barrier((e1, a1))
-    c1 = over_y(e1_far, 2)
-    state = more(far, [c0, c0_there], [pair], state)
+    half = SEG // 2
+    c1 = over_y(a1[:half], 1), over_y(b1[half:], 3)
     state = more(below_above, [a1, b1, ab1_there], [crossed, pair], state)
     c1, state = lax.optimization_barrier((c1, state))
+    c1 = jnp.concatenate(c1, axis=0)
     c1_there = over_core(c1)
 
     block = ((2 * PAGE, 2 * HD), jnp.bfloat16)

time: 129 us -> 131 us (1.016)
  starting transfers between devices: 32.3 us -> 34.5 us
    ppermute x6 -> x7, starting transfers between devices: 17.4 us -> 19.4 us  [over_y(): return lax.ppermute(x, 'blk', [(i, (i + 2 * d) % 8) for i in range(8)])]
    pallas_call x8 -> x7, Pallas kernels: 89.8 us -> 88.9 us  [call(): pl.pallas_call(kernel, in_specs=[SMEM] + [VMEM] * len(arrays), out_specs=...]
  transfers between devices with their start and end apart: 17 -> 18, of which waited for: 3 -> 3; matrix products, arithmetic and copies ran while one was open for 1% -> 1% of each run, Pallas kernels for 68% -> 66%
where the time goes in v4:
time: 131 us; the launch traced here: 130 us
  Pallas kernels  88.9 us (68%)
  starting transfers between devices  34.5 us (26%)
  waiting for transfers between devices  4.06 us (3%)
    pallas_call x7, Pallas kernels, call(): pl.pallas_call(kernel, in_specs=[SMEM] + [VMEM] * len(arrays), out_specs=...  88.9 us
    ppermute x7, starting transfers between devices, over_y(): return lax.ppermute(x, 'blk', [(i, (i + 2 * d) % 8) for i in range(8)])  19.4 us
    ppermute x5, starting transfers between devices, over_dec(): return lax.ppermute(x, 'dec', [(i, i ^ m) for i in range(8)])  11.9 us
    ppermute x6, starting transfers between devices, over_core(): return lax.ppermute(x, 'blk', [(i, i ^ 1) for i in range(8)])  3.29 us
  transfers between devices with their start and end apart: 18, of which 3 were waited for; matrix products, arithmetic and copies ran while one was open for 1% of the time, Pallas kernels for 66%

profile of v4, /device:TPU:17, one launch (start us, length us, event | category | flops | bytes accessed | tf_op | source)
XLA Modules:
  0.0 130.3 jit_solution(5217101462740909965)
XLA Ops:
  0.7 0.8 fusion.8
  1.5 2.8 %collective-permute-start.1 = (bf16[128,256]{1,0:T(8,128)(2,1)S(1)}, bf16[128,256]{1,0:T(8,128)(2,1)S(1)}, u32[]{:S(2)}, u32[]{:S(2)}) collective-permute-start(bf16[128,256]{1,0:T(8,128)(2,1)S(1)} %get-tuple-element.146), channel_id=1, source_target_pairs={{0,4},{1,5},{2,6},{3,7},{4,0},{5,1},{6,2},{7,3},{8,12},{9,13},{10,... | collective-permute-start | bytes 196616 | tf_op jit(solution)/shard_map/ppermute | solution.py:320
  4.4 0.9 collective-permute-start.2
  5.5 0.2 compare_reduce_fusion
  6.2 2.2 %collective-permute-done = bf16[128,256]{1,0:T(8,128)(2,1)S(1)} collective-permute-done((bf16[128,256]{1,0:T(8,128)(2,1)S(1)}, bf16[128,256]{1,0:T(8,128)(2,1)S(1)}, u32[]{:S(2)}, u32[]{:S(2)}) %collective-permute-start) | collective-permute-done | bytes 65568 | tf_op jit(solution)/shard_map/ppermute | solution.py:320
  8.3 0.3 collective-permute-done.2
  8.7 2.2 %collective-permute-start.3 = (bf16[512,256]{1,0:T(8,128)(2,1)S(1)}, bf16[512,256]{1,0:T(8,128)(2,1)S(1)}, u32[]{:S(2)}, u32[]{:S(2)}) collective-permute-start(bf16[512,256]{1,0:T(8,128)(2,1)S(1)} %pad_maximum_fusion.2.e_ref.refs_0_), channel_id=1, source_target_pairs={{0,32},{32,0},{64,96},{96,64},{128,160},{160,128},{192,224},{224,1... | collective-permute-start | bytes 786440 | tf_op jit(solution)/shard_map/ppermute | solution.py:323
  10.9 1.0 collective-permute-start.4
  11.9 0.5 collective-permute-start.5
  12.4 6.9 %collective-permute-start.7 = (bf16[512,256]{1,0:T(8,128)(2,1)S(1)}, bf16[512,256]{1,0:T(8,128)(2,1)S(1)}, u32[]{:S(2)}, u32[]{:S(2)}) collective-permute-start(bf16[512,256]{1,0:T(8,128)(2,1)S(1)} %pad_maximum_fusion.2.e_ref.refs_0_), channel_id=1, source_target_pairs={{0,1},{1,0},{2,3},{3,2},{4,5},{5,4},{6,7},{7,6},{8,9},{9,8},{10,11... | collective-permute-start | bytes 786440 | tf_op jit(solution)/shard_map/ppermute | solution.py:320
  19.3 1.3 %collective-permute-start.6 = (bf16[512,256]{1,0:T(8,128)(2,1)S(1)}, bf16[512,256]{1,0:T(8,128)(2,1)S(1)}, u32[]{:S(2)}, u32[]{:S(2)}) collective-permute-start(bf16[512,256]{1,0:T(8,128)(2,1)S(1)} %pad_maximum_fusion.2.e_ref.refs_0_), channel_id=1, source_target_pairs={{0,128},{32,160},{64,192},{96,224},{128,0},{160,32},{192,64},{224,... | collective-permute-start | bytes 786440 | tf_op jit(solution)/shard_map/ppermute | solution.py:326
  20.6 14.8 %shard_map.83 = (bf16[1024,256]{1,0:T(8,128)(2,1)S(1)}, f32[2048,128]{1,0:T(8,128)S(1)}, f32[2048,1]{1,0:T(8,128)S(1)}, f32[2048,1]{1,0:T(8,128)S(1)}, f32[8,2]{1,0:T(8,128)S(1)}) custom-call(s32[4]{0:T(128)S(1)} %get-tuple-element.76.meta, bf16[1024,256]{1,0:T(8,128)(2,1)S(1)} %copy-done, bf16[512,256]{1,0:T(8,128)(2,1)S(1)} %pad_maximum_fusion.2.e_ref.refs_0_, ...), custom_call_target="tpu_custom_call" | custom-call | tf_op jit(solution)/shard_map/pallas_call | solution.py:303
  35.4 0.6 shard_map.84
  36.1 0.5 collective-permute-start.10
  36.7 14.5 %collective-permute-start.8 = (bf16[512,256]{1,0:T(8,128)(2,1)S(1)}, bf16[512,256]{1,0:T(8,128)(2,1)S(1)}, u32[]{:S(2)}, u32[]{:S(2)}) collective-permute-start(bf16[512,256]{1,0:T(8,128)(2,1)S(1)} %collective-permute-done.7.e_ref.refs_1_), channel_id=1, source_target_pairs={{0,64},{32,96},{64,128},{96,160},{128,192},{160,224},{192,0},{224,... | collective-permute-start | bytes 786440 | tf_op jit(solution)/shard_map/ppermute | solution.py:326
  51.2 41.0 %shard_map.85 = (f32[2048,128]{1,0:T(8,128)S(1)}, f32[2048,1]{1,0:T(8,128)S(1)}, f32[2048,1]{1,0:T(8,128)S(1)}, f32[8,2]{1,0:T(8,128)S(1)}) custom-call(s32[4]{0:T(128)S(1)} %get-tuple-element.91.meta, bf16[1024,256]{1,0:T(8,128)(2,1)S(1)} %get-tuple-element.79.q_ref, ...), custom_call_target="tpu_custom_call", output_to_operand_aliasing={{0}: (9, {}), {1}: (10, {}), {2}: (11, {}), {3}: (12, {})} | custom-call | tf_op jit(solution)/shard_map/pallas_call | solution.py:303
  92.4 2.1 %collective-permute-start.13 = (bf16[256,256]{1,0:T(8,128)(2,1)S(1)}, bf16[256,256]{1,0:T(8,128)(2,1)S(1)}, u32[]{:S(2)}, u32[]{:S(2)}) collective-permute-start(bf16[256,256]{1,0:T(8,128)(2,1)S(1)} %slice.26), channel_id=1, source_target_pairs={{0,64},{32,96},{64,128},{96,160},{128,192},{160,224},{192,0},{224,... | collective-permute-start | bytes 393224 | tf_op jit(solution)/shard_map/ppermute | solution.py:326
  94.5 14.5 %shard_map.86 = (f32[2048,128]{1,0:T(8,128)S(1)}, f32[2048,1]{1,0:T(8,128)S(1)}, f32[2048,1]{1,0:T(8,128)S(1)}, f32[8,2]{1,0:T(8,128)S(1)}) custom-call(s32[4]{0:T(128)S(1)} %get-tuple-element.111.meta, bf16[1024,256]{1,0:T(8,128)(2,1)S(1)} %get-tuple-element.79.q_ref, ...), custom_call_target="tpu_custom_call", output_to_operand_aliasing={{0}: (5, {}), {1}: (6, {}), {2}: (7, {}), {3}: (8, {})} | custom-call | tf_op jit(solution)/shard_map/pallas_call | solution.py:303
  109.1 0.3 collective-permute-start.16
  109.4 1.5 %collective-permute-done.16.refs_11_.refs_1_ = bf16[512,256]{1,0:T(8,128)(2,1)S(1)} collective-permute-done((bf16[512,256]{1,0:T(8,128)(2,1)S(1)}, bf16[512,256]{1,0:T(8,128)(2,1)S(1)}, u32[]{:S(2)}, u32[]{:S(2)}) %collective-permute-start.16) | collective-permute-done | bytes 262176 | tf_op jit(solution)/shard_map/ppermute | solution.py:323
  110.9 0.9 shard_map.87
  111.9 1.3 collective-permute-start.17
  113.1 15.8 %shard_map.88 = (f32[2048,128]{1,0:T(8,128)S(1)}, f32[2048,1]{1,0:T(8,128)S(1)}, f32[2048,1]{1,0:T(8,128)S(1)}, f32[8,2]{1,0:T(8,128)S(1)}, bf16[1024,256]{1,0:T(8,128)(2,1)}) custom-call(s32[4]{0:T(128)S(1)} %get-tuple-element.75.meta, ...), custom_call_target="tpu_custom_call", output_to_operand_aliasing={{0}: (4, {}), {1}: (5, {}), {2}: (6, {}), {3}: (7, {})} | custom-call | tf_op jit(solution)/shard_map/pallas_call | solution.py:303
  128.9 1.4 %shard_map.89 = (bf16[256,256]{1,0:T(8,128)(2,1)}, bf16[256,256]{1,0:T(8,128)(2,1)}, f32[2,2]{1,0:T(2,128)}, f32[2,2]{1,0:T(2,128)}) custom-call(s32[3]{0:T(128)S(1)} %pad_add_fusion.meta, bf16[256,256]{1,0:T(8,128)(2,1)S(1)} %get-tuple-element.139.own, bf16[256,256]{1,0:T(8,128)(2,1)S(1)} %collective-permute-done.17.oth), custom_call_target="tpu_custom_call" | custom-call | tf_op jit(solution)/shard_map/pallas_call | solution.py:303
  (43 shorter events, 1.2 us)
Async XLA Ops:
  0.7 4.8 %copy-start.1 = (s32[64]{0:T(128)S(1)}, s32[64]{0:T(128)}, u32[]{:S(2)}) copy-start(s32[64]{0:T(128)} %param.7) | copy-start | bytes 772
  1.5 19.1 %copy-start = (bf16[1024,256]{1,0:T(8,128)(2,1)S(1)}, bf16[1024,256]{1,0:T(8,128)(2,1)}, u32[]{:S(2)}) copy-start(bf16[1024,256]{1,0:T(8,128)(2,1)} %q_ref.1) | copy-start | bytes 1572868
  1.5 6.8 %collective-permute-start.1 = (bf16[128,256]{1,0:T(8,128)(2,1)S(1)}, bf16[128,256]{1,0:T(8,128)(2,1)S(1)}, u32[]{:S(2)}, u32[]{:S(2)}) collective-permute-start(bf16[128,256]{1,0:T(8,128)(2,1)S(1)} %get-tuple-element.146), channel_id=1, source_target_pairs={{0,4},{1,5},{2,6},{3,7},{4,0},{5,1},{6,2},{7,3},{8,12},{9,13},{10,... | collective-permute-start | bytes 196616 | tf_op jit(solution)/shard_map/ppermute | solution.py:320
  4.4 4.3 %collective-permute-start.2 = (bf16[128,256]{1,0:T(8,128)(2,1)S(1)}, bf16[128,256]{1,0:T(8,128)(2,1)S(1)}, u32[]{:S(2)}, u32[]{:S(2)}) collective-permute-start(bf16[128,256]{1,0:T(8,128)(2,1)S(1)} %get-tuple-element.146), channel_id=1, source_target_pairs={{0,6},{1,7},{2,4},{3,5},{4,2},{5,3},{6,0},{7,1},{8,14},{9,15},{10,... | collective-permute-start | bytes 196616 | tf_op jit(solution)/shard_map/ppermute | solution.py:320
  5.2 3.1 %collective-permute-start = (bf16[128,256]{1,0:T(8,128)(2,1)S(1)}, bf16[128,256]{1,0:T(8,128)(2,1)S(1)}, u32[]{:S(2)}, u32[]{:S(2)}) collective-permute-start(bf16[128,256]{1,0:T(8,128)(2,1)S(1)} %get-tuple-element.145), channel_id=1, source_target_pairs={{0,2},{1,3},{2,0},{3,1},{4,6},{5,7},{6,4},{7,5},{8,10},{9,11},{10,... | collective-permute-start | bytes 196616 | tf_op jit(solution)/shard_map/ppermute | solution.py:320
  8.7 10.6 %collective-permute-start.3 = (bf16[512,256]{1,0:T(8,128)(2,1)S(1)}, bf16[512,256]{1,0:T(8,128)(2,1)S(1)}, u32[]{:S(2)}, u32[]{:S(2)}) collective-permute-start(bf16[512,256]{1,0:T(8,128)(2,1)S(1)} %pad_maximum_fusion.2.e_ref.refs_0_), channel_id=1, source_target_pairs={{0,32},{32,0},{64,96},{96,64},{128,160},{160,128},{192,224},{224,1... | collective-permute-start | bytes 786440 | tf_op jit(solution)/shard_map/ppermute | solution.py:323
  10.9 24.5 %collective-permute-start.4 = (bf16[512,256]{1,0:T(8,128)(2,1)S(1)}, bf16[512,256]{1,0:T(8,128)(2,1)S(1)}, u32[]{:S(2)}, u32[]{:S(2)}) collective-permute-start(bf16[512,256]{1,0:T(8,128)(2,1)S(1)} %pad_maximum_fusion.2.e_ref.refs_0_), channel_id=1, source_target_pairs={{0,64},{32,96},{64,128},{96,160},{128,192},{160,224},{192,0},{224,... | collective-permute-start | bytes 786440 | tf_op jit(solution)/shard_map/ppermute | solution.py:326
  11.9 23.5 %collective-permute-start.5 = (bf16[512,256]{1,0:T(8,128)(2,1)S(1)}, bf16[512,256]{1,0:T(8,128)(2,1)S(1)}, u32[]{:S(2)}, u32[]{:S(2)}) collective-permute-start(bf16[512,256]{1,0:T(8,128)(2,1)S(1)} %pad_maximum_fusion.2.e_ref.refs_0_), channel_id=1, source_target_pairs={{0,192},{32,224},{64,0},{96,32},{128,64},{160,96},{192,128},{224,1... | collective-permute-start | bytes 786440 | tf_op jit(solution)/shard_map/ppermute | solution.py:326
  12.4 23.6 %collective-permute-start.7 = (bf16[512,256]{1,0:T(8,128)(2,1)S(1)}, bf16[512,256]{1,0:T(8,128)(2,1)S(1)}, u32[]{:S(2)}, u32[]{:S(2)}) collective-permute-start(bf16[512,256]{1,0:T(8,128)(2,1)S(1)} %pad_maximum_fusion.2.e_ref.refs_0_), channel_id=1, source_target_pairs={{0,1},{1,0},{2,3},{3,2},{4,5},{5,4},{6,7},{7,6},{8,9},{9,8},{10,11... | collective-permute-start | bytes 786440 | tf_op jit(solution)/shard_map/ppermute | solution.py:320
  19.3 16.7 %collective-permute-start.6 = (bf16[512,256]{1,0:T(8,128)(2,1)S(1)}, bf16[512,256]{1,0:T(8,128)(2,1)S(1)}, u32[]{:S(2)}, u32[]{:S(2)}) collective-permute-start(bf16[512,256]{1,0:T(8,128)(2,1)S(1)} %pad_maximum_fusion.2.e_ref.refs_0_), channel_id=1, source_target_pairs={{0,128},{32,160},{64,192},{96,224},{128,0},{160,32},{192,64},{224,... | collective-permute-start | bytes 786440 | tf_op jit(solution)/shard_map/ppermute | solution.py:326
  36.0 15.2 %collective-permute-start.12 = (bf16[1024,256]{1,0:T(8,128)(2,1)S(1)}, bf16[1024,256]{1,0:T(8,128)(2,1)S(1)}, u32[]{:S(2)}, u32[]{:S(2)}) collective-permute-start(bf16[1024,256]{1,0:T(8,128)(2,1)S(1)} %pad_maximum_fusion), channel_id=1, source_target_pairs={{0,32},{32,0},{64,96},{96,64},{128,160},{160,128},{192,224},{224,1... | collective-permute-start | bytes 1572872 | tf_op jit(solution)/shard_map/ppermute | solution.py:323
  36.1 15.1 %collective-permute-start.10 = (bf16[512,256]{1,0:T(8,128)(2,1)S(1)}, bf16[512,256]{1,0:T(8,128)(2,1)S(1)}, u32[]{:S(2)}, u32[]{:S(2)}) collective-permute-start(bf16[512,256]{1,0:T(8,128)(2,1)S(1)} %collective-permute-done.7.e_ref.refs_1_), channel_id=1, source_target_pairs={{0,32},{32,0},{64,96},{96,64},{128,160},{160,128},{192,224},{224,1... | collective-permute-start | bytes 786440 | tf_op jit(solution)/shard_map/ppermute | solution.py:323
  36.6 14.6 %collective-permute-start.11 = (bf16[512,256]{1,0:T(8,128)(2,1)S(1)}, bf16[512,256]{1,0:T(8,128)(2,1)S(1)}, u32[]{:S(2)}, u32[]{:S(2)}) collective-permute-start(bf16[512,256]{1,0:T(8,128)(2,1)S(1)} %collective-permute-done.6.refs_3_.refs_4_), channel_id=1, source_target_pairs={{0,32},{32,0},{64,96},{96,64},{128,160},{160,128},{192,224},{224,1... | collective-permute-start | bytes 786440 | tf_op jit(solution)/shard_map/ppermute | solution.py:323
  36.7 55.5 %collective-permute-start.8 = (bf16[512,256]{1,0:T(8,128)(2,1)S(1)}, bf16[512,256]{1,0:T(8,128)(2,1)S(1)}, u32[]{:S(2)}, u32[]{:S(2)}) collective-permute-start(bf16[512,256]{1,0:T(8,128)(2,1)S(1)} %collective-permute-done.7.e_ref.refs_1_), channel_id=1, source_target_pairs={{0,64},{32,96},{64,128},{96,160},{128,192},{160,224},{192,0},{224,... | collective-permute-start | bytes 786440 | tf_op jit(solution)/shard_map/ppermute | solution.py:326
  51.2 41.0 %collective-permute-start.9 = (bf16[512,256]{1,0:T(8,128)(2,1)S(1)}, bf16[512,256]{1,0:T(8,128)(2,1)S(1)}, u32[]{:S(2)}, u32[]{:S(2)}) collective-permute-start(bf16[512,256]{1,0:T(8,128)(2,1)S(1)} %collective-permute-done.7.e_ref.refs_1_), channel_id=1, source_target_pairs={{0,192},{32,224},{64,0},{96,32},{128,64},{160,96},{192,128},{224,1... | collective-permute-start | bytes 786440 | tf_op jit(solution)/shard_map/ppermute | solution.py:326
  92.3 2.2 %collective-permute-start.15 = (bf16[1024,256]{1,0:T(8,128)(2,1)S(1)}, bf16[1024,256]{1,0:T(8,128)(2,1)S(1)}, u32[]{:S(2)}, u32[]{:S(2)}) collective-permute-start(bf16[1024,256]{1,0:T(8,128)(2,1)S(1)} %pad_maximum_fusion.1), channel_id=1, source_target_pairs={{0,32},{32,0},{64,96},{96,64},{128,160},{160,128},{192,224},{224,1... | collective-permute-start | bytes 1572872 | tf_op jit(solution)/shard_map/ppermute | solution.py:323
  92.4 16.6 %collective-permute-start.13 = (bf16[256,256]{1,0:T(8,128)(2,1)S(1)}, bf16[256,256]{1,0:T(8,128)(2,1)S(1)}, u32[]{:S(2)}, u32[]{:S(2)}) collective-permute-start(bf16[256,256]{1,0:T(8,128)(2,1)S(1)} %slice.26), channel_id=1, source_target_pairs={{0,64},{32,96},{64,128},{96,160},{128,192},{160,224},{192,0},{224,... | collective-permute-start | bytes 393224 | tf_op jit(solution)/shard_map/ppermute | solution.py:326
  94.5 14.5 %collective-permute-start.14 = (bf16[256,256]{1,0:T(8,128)(2,1)S(1)}, bf16[256,256]{1,0:T(8,128)(2,1)S(1)}, u32[]{:S(2)}, u32[]{:S(2)}) collective-permute-start(bf16[256,256]{1,0:T(8,128)(2,1)S(1)} %slice.27), channel_id=1, source_target_pairs={{0,192},{32,224},{64,0},{96,32},{128,64},{160,96},{192,128},{224,1... | collective-permute-start | bytes 393224 | tf_op jit(solution)/shard_map/ppermute | solution.py:326
  109.1 1.8 %collective-permute-start.16 = (bf16[512,256]{1,0:T(8,128)(2,1)S(1)}, bf16[512,256]{1,0:T(8,128)(2,1)S(1)}, u32[]{:S(2)}, u32[]{:S(2)}) collective-permute-start(bf16[512,256]{1,0:T(8,128)(2,1)S(1)} %constant_dynamic-update-slice_fusion.refs_5_.refs_0_), channel_id=1, source_target_pairs={{0,32},{32,0},{64,96},{96,64},{128,160},{160,128},{192,224},{224,1... | collective-permute-start | bytes 786440 | tf_op jit(solution)/shard_map/ppermute | solution.py:323
  111.9 17.0 %collective-permute-start.17 = (bf16[256,256]{1,0:T(8,128)(2,1)S(1)}, bf16[256,256]{1,0:T(8,128)(2,1)S(1)}, u32[]{:S(2)}, u32[]{:S(2)}) collective-permute-start(bf16[256,256]{1,0:T(8,128)(2,1)S(1)} %get-tuple-element.140), channel_id=1, source_target_pairs={{0,4},{1,5},{2,6},{3,7},{4,0},{5,1},{6,2},{7,3},{8,12},{9,13},{10,... | collective-permute-start | bytes 393224 | tf_op jit(solution)/shard_map/ppermute | solution.py:320

commit v5 on v4

--- a/solution.py
+++ b/solution.py
@@ -113,12 +113,12 @@
 
 
 def units_quick(q_ref, state, kv_ref, count, finish=None):
-    tiles = q_ref.shape[0] // (2 * TN)
+    tiles = q_ref.shape[0] // (4 * TN)
 
     def step(i):
         keys = rows_at((i // tiles) * 2 * SEG, 2 * SEG)
-        for part in range(2):
-            row = (i % tiles) * 2 * TN + part * TN
+        for part in range(4):
+            row = (i % tiles) * 4 * TN + part * TN
             for h in range(2):
                 fast(q_ref, state, h, row, TN, kv_ref[keys, :HD], kv_ref[keys, HD:])
                 if finish is not None:

time: 131 us -> 131 us (level)
  transfers between devices with their start and end apart: 18 -> 18, of which waited for: 3 -> 3; matrix products, arithmetic and copies ran while one was open for 1% -> 1% of each run, Pallas kernels for 66% -> 67%
where the time goes in v5:
time: 131 us
  Pallas kernels  89.6 us (68%)
  starting transfers between devices  34.3 us (26%)
  waiting for transfers between devices  4.06 us (3%)
    pallas_call x7, Pallas kernels, call(): pl.pallas_call(kernel, in_specs=[SMEM] + [VMEM] * len(arrays), out_specs=...  89.6 us
    ppermute x7, starting transfers between devices, over_y(): return lax.ppermute(x, 'blk', [(i, (i + 2 * d) % 8) for i in range(8)])  19.4 us
    ppermute x5, starting transfers between devices, over_dec(): return lax.ppermute(x, 'dec', [(i, i ^ m) for i in range(8)])  11.9 us
    ppermute x6, starting transfers between devices, over_core(): return lax.ppermute(x, 'blk', [(i, i ^ 1) for i in range(8)])  3.07 us
  transfers between devices with their start and end apart: 18, of which 3 were waited for; matrix products, arithmetic and copies ran while one was open for 1% of the time, Pallas kernels for 67%

profile of v5, /device:TPU:17, one launch (start us, length us, event | category | flops | bytes accessed | tf_op | source)
XLA Modules:
  0.0 130.8 jit_solution(4063849189521633134)
XLA Ops:
  0.7 0.8 fusion.8
  1.5 2.8 %collective-permute-start.1 = (bf16[128,256]{1,0:T(8,128)(2,1)S(1)}, bf16[128,256]{1,0:T(8,128)(2,1)S(1)}, u32[]{:S(2)}, u32[]{:S(2)}) collective-permute-start(bf16[128,256]{1,0:T(8,128)(2,1)S(1)} %get-tuple-element.146), channel_id=1, source_target_pairs={{0,4},{1,5},{2,6},{3,7},{4,0},{5,1},{6,2},{7,3},{8,12},{9,13},{10,... | collective-permute-start | bytes 196616 | tf_op jit(solution)/shard_map/ppermute | solution.py:320
  4.4 0.9 collective-permute-start.2
  5.5 0.2 compare_reduce_fusion
  5.7 0.2 fusion
  6.2 2.2 %collective-permute-done = bf16[128,256]{1,0:T(8,128)(2,1)S(1)} collective-permute-done((bf16[128,256]{1,0:T(8,128)(2,1)S(1)}, bf16[128,256]{1,0:T(8,128)(2,1)S(1)}, u32[]{:S(2)}, u32[]{:S(2)}) %collective-permute-start) | collective-permute-done | bytes 65568 | tf_op jit(solution)/shard_map/ppermute | solution.py:320
  8.3 0.3 collective-permute-done.2
  8.7 2.2 %collective-permute-start.3 = (bf16[512,256]{1,0:T(8,128)(2,1)S(1)}, bf16[512,256]{1,0:T(8,128)(2,1)S(1)}, u32[]{:S(2)}, u32[]{:S(2)}) collective-permute-start(bf16[512,256]{1,0:T(8,128)(2,1)S(1)} %pad_maximum_fusion.2.e_ref.refs_0_), channel_id=1, source_target_pairs={{0,32},{32,0},{64,96},{96,64},{128,160},{160,128},{192,224},{224,1... | collective-permute-start | bytes 786440 | tf_op jit(solution)/shard_map/ppermute | solution.py:323
  10.9 1.0 collective-permute-start.4
  11.9 0.5 collective-permute-start.5
  12.4 6.9 %collective-permute-start.7 = (bf16[512,256]{1,0:T(8,128)(2,1)S(1)}, bf16[512,256]{1,0:T(8,128)(2,1)S(1)}, u32[]{:S(2)}, u32[]{:S(2)}) collective-permute-start(bf16[512,256]{1,0:T(8,128)(2,1)S(1)} %pad_maximum_fusion.2.e_ref.refs_0_), channel_id=1, source_target_pairs={{0,1},{1,0},{2,3},{3,2},{4,5},{5,4},{6,7},{7,6},{8,9},{9,8},{10,11... | collective-permute-start | bytes 786440 | tf_op jit(solution)/shard_map/ppermute | solution.py:320
  19.3 1.3 %collective-permute-start.6 = (bf16[512,256]{1,0:T(8,128)(2,1)S(1)}, bf16[512,256]{1,0:T(8,128)(2,1)S(1)}, u32[]{:S(2)}, u32[]{:S(2)}) collective-permute-start(bf16[512,256]{1,0:T(8,128)(2,1)S(1)} %pad_maximum_fusion.2.e_ref.refs_0_), channel_id=1, source_target_pairs={{0,128},{32,160},{64,192},{96,224},{128,0},{160,32},{192,64},{224,... | collective-permute-start | bytes 786440 | tf_op jit(solution)/shard_map/ppermute | solution.py:326
  20.6 14.8 %shard_map.83 = (bf16[1024,256]{1,0:T(8,128)(2,1)S(1)}, f32[2048,128]{1,0:T(8,128)S(1)}, f32[2048,1]{1,0:T(8,128)S(1)}, f32[2048,1]{1,0:T(8,128)S(1)}, f32[8,2]{1,0:T(8,128)S(1)}) custom-call(s32[4]{0:T(128)S(1)} %get-tuple-element.76.meta, bf16[1024,256]{1,0:T(8,128)(2,1)S(1)} %copy-done, bf16[512,256]{1,0:T(8,128)(2,1)S(1)} %pad_maximum_fusion.2.e_ref.refs_0_, ...), custom_call_target="tpu_custom_call" | custom-call | tf_op jit(solution)/shard_map/pallas_call | solution.py:303
  35.4 0.7 shard_map.84
  36.3 0.5 collective-permute-start.10
  36.9 14.5 %collective-permute-start.8 = (bf16[512,256]{1,0:T(8,128)(2,1)S(1)}, bf16[512,256]{1,0:T(8,128)(2,1)S(1)}, u32[]{:S(2)}, u32[]{:S(2)}) collective-permute-start(bf16[512,256]{1,0:T(8,128)(2,1)S(1)} %collective-permute-done.7.e_ref.refs_1_), channel_id=1, source_target_pairs={{0,64},{32,96},{64,128},{96,160},{128,192},{160,224},{192,0},{224,... | collective-permute-start | bytes 786440 | tf_op jit(solution)/shard_map/ppermute | solution.py:326
  51.4 41.0 %shard_map.85 = (f32[2048,128]{1,0:T(8,128)S(1)}, f32[2048,1]{1,0:T(8,128)S(1)}, f32[2048,1]{1,0:T(8,128)S(1)}, f32[8,2]{1,0:T(8,128)S(1)}) custom-call(s32[4]{0:T(128)S(1)} %get-tuple-element.91.meta, bf16[1024,256]{1,0:T(8,128)(2,1)S(1)} %get-tuple-element.79.q_ref, ...), custom_call_target="tpu_custom_call", output_to_operand_aliasing={{0}: (9, {}), {1}: (10, {}), {2}: (11, {}), {3}: (12, {})} | custom-call | tf_op jit(solution)/shard_map/pallas_call | solution.py:303
  92.6 2.1 %collective-permute-start.13 = (bf16[256,256]{1,0:T(8,128)(2,1)S(1)}, bf16[256,256]{1,0:T(8,128)(2,1)S(1)}, u32[]{:S(2)}, u32[]{:S(2)}) collective-permute-start(bf16[256,256]{1,0:T(8,128)(2,1)S(1)} %slice.26), channel_id=1, source_target_pairs={{0,64},{32,96},{64,128},{96,160},{128,192},{160,224},{192,0},{224,... | collective-permute-start | bytes 393224 | tf_op jit(solution)/shard_map/ppermute | solution.py:326
  94.7 15.0 %shard_map.86 = (f32[2048,128]{1,0:T(8,128)S(1)}, f32[2048,1]{1,0:T(8,128)S(1)}, f32[2048,1]{1,0:T(8,128)S(1)}, f32[8,2]{1,0:T(8,128)S(1)}) custom-call(s32[4]{0:T(128)S(1)} %get-tuple-element.111.meta, bf16[1024,256]{1,0:T(8,128)(2,1)S(1)} %get-tuple-element.79.q_ref, ...), custom_call_target="tpu_custom_call", output_to_operand_aliasing={{0}: (5, {}), {1}: (6, {}), {2}: (7, {}), {3}: (8, {})} | custom-call | tf_op jit(solution)/shard_map/pallas_call | solution.py:303
  109.9 1.5 %collective-permute-done.16.refs_11_.refs_1_ = bf16[512,256]{1,0:T(8,128)(2,1)S(1)} collective-permute-done((bf16[512,256]{1,0:T(8,128)(2,1)S(1)}, bf16[512,256]{1,0:T(8,128)(2,1)S(1)}, u32[]{:S(2)}, u32[]{:S(2)}) %collective-permute-start.16) | collective-permute-done | bytes 262176 | tf_op jit(solution)/shard_map/ppermute | solution.py:323
  111.4 0.9 shard_map.87
  112.3 1.3 collective-permute-start.17
  113.6 15.7 %shard_map.88 = (f32[2048,128]{1,0:T(8,128)S(1)}, f32[2048,1]{1,0:T(8,128)S(1)}, f32[2048,1]{1,0:T(8,128)S(1)}, f32[8,2]{1,0:T(8,128)S(1)}, bf16[1024,256]{1,0:T(8,128)(2,1)}) custom-call(s32[4]{0:T(128)S(1)} %get-tuple-element.75.meta, ...), custom_call_target="tpu_custom_call", output_to_operand_aliasing={{0}: (4, {}), {1}: (5, {}), {2}: (6, {}), {3}: (7, {})} | custom-call | tf_op jit(solution)/shard_map/pallas_call | solution.py:303
  129.3 1.4 %shard_map.89 = (bf16[256,256]{1,0:T(8,128)(2,1)}, bf16[256,256]{1,0:T(8,128)(2,1)}, f32[2,2]{1,0:T(2,128)}, f32[2,2]{1,0:T(2,128)}) custom-call(s32[3]{0:T(128)S(1)} %pad_add_fusion.meta, bf16[256,256]{1,0:T(8,128)(2,1)S(1)} %get-tuple-element.139.own, bf16[256,256]{1,0:T(8,128)(2,1)S(1)} %collective-permute-done.17.oth), custom_call_target="tpu_custom_call" | custom-call | tf_op jit(solution)/shard_map/pallas_call | solution.py:303
  (43 shorter events, 1.1 us)
Async XLA Ops:
  0.7 4.8 %copy-start.1 = (s32[64]{0:T(128)S(1)}, s32[64]{0:T(128)}, u32[]{:S(2)}) copy-start(s32[64]{0:T(128)} %param.7) | copy-start | bytes 772
  1.5 19.1 %copy-start = (bf16[1024,256]{1,0:T(8,128)(2,1)S(1)}, bf16[1024,256]{1,0:T(8,128)(2,1)}, u32[]{:S(2)}) copy-start(bf16[1024,256]{1,0:T(8,128)(2,1)} %q_ref.1) | copy-start | bytes 1572868
  1.5 6.8 %collective-permute-start.1 = (bf16[128,256]{1,0:T(8,128)(2,1)S(1)}, bf16[128,256]{1,0:T(8,128)(2,1)S(1)}, u32[]{:S(2)}, u32[]{:S(2)}) collective-permute-start(bf16[128,256]{1,0:T(8,128)(2,1)S(1)} %get-tuple-element.146), channel_id=1, source_target_pairs={{0,4},{1,5},{2,6},{3,7},{4,0},{5,1},{6,2},{7,3},{8,12},{9,13},{10,... | collective-permute-start | bytes 196616 | tf_op jit(solution)/shard_map/ppermute | solution.py:320
  4.4 4.3 %collective-permute-start.2 = (bf16[128,256]{1,0:T(8,128)(2,1)S(1)}, bf16[128,256]{1,0:T(8,128)(2,1)S(1)}, u32[]{:S(2)}, u32[]{:S(2)}) collective-permute-start(bf16[128,256]{1,0:T(8,128)(2,1)S(1)} %get-tuple-element.146), channel_id=1, source_target_pairs={{0,6},{1,7},{2,4},{3,5},{4,2},{5,3},{6,0},{7,1},{8,14},{9,15},{10,... | collective-permute-start | bytes 196616 | tf_op jit(solution)/shard_map/ppermute | solution.py:320
  5.2 3.1 %collective-permute-start = (bf16[128,256]{1,0:T(8,128)(2,1)S(1)}, bf16[128,256]{1,0:T(8,128)(2,1)S(1)}, u32[]{:S(2)}, u32[]{:S(2)}) collective-permute-start(bf16[128,256]{1,0:T(8,128)(2,1)S(1)} %get-tuple-element.145), channel_id=1, source_target_pairs={{0,2},{1,3},{2,0},{3,1},{4,6},{5,7},{6,4},{7,5},{8,10},{9,11},{10,... | collective-permute-start | bytes 196616 | tf_op jit(solution)/shard_map/ppermute | solution.py:320
  8.7 10.6 %collective-permute-start.3 = (bf16[512,256]{1,0:T(8,128)(2,1)S(1)}, bf16[512,256]{1,0:T(8,128)(2,1)S(1)}, u32[]{:S(2)}, u32[]{:S(2)}) collective-permute-start(bf16[512,256]{1,0:T(8,128)(2,1)S(1)} %pad_maximum_fusion.2.e_ref.refs_0_), channel_id=1, source_target_pairs={{0,32},{32,0},{64,96},{96,64},{128,160},{160,128},{192,224},{224,1... | collective-permute-start | bytes 786440 | tf_op jit(solution)/shard_map/ppermute | solution.py:323
  10.9 24.5 %collective-permute-start.4 = (bf16[512,256]{1,0:T(8,128)(2,1)S(1)}, bf16[512,256]{1,0:T(8,128)(2,1)S(1)}, u32[]{:S(2)}, u32[]{:S(2)}) collective-permute-start(bf16[512,256]{1,0:T(8,128)(2,1)S(1)} %pad_maximum_fusion.2.e_ref.refs_0_), channel_id=1, source_target_pairs={{0,64},{32,96},{64,128},{96,160},{128,192},{160,224},{192,0},{224,... | collective-permute-start | bytes 786440 | tf_op jit(solution)/shard_map/ppermute | solution.py:326
  11.9 23.5 %collective-permute-start.5 = (bf16[512,256]{1,0:T(8,128)(2,1)S(1)}, bf16[512,256]{1,0:T(8,128)(2,1)S(1)}, u32[]{:S(2)}, u32[]{:S(2)}) collective-permute-start(bf16[512,256]{1,0:T(8,128)(2,1)S(1)} %pad_maximum_fusion.2.e_ref.refs_0_), channel_id=1, source_target_pairs={{0,192},{32,224},{64,0},{96,32},{128,64},{160,96},{192,128},{224,1... | collective-permute-start | bytes 786440 | tf_op jit(solution)/shard_map/ppermute | solution.py:326
  12.4 23.8 %collective-permute-start.7 = (bf16[512,256]{1,0:T(8,128)(2,1)S(1)}, bf16[512,256]{1,0:T(8,128)(2,1)S(1)}, u32[]{:S(2)}, u32[]{:S(2)}) collective-permute-start(bf16[512,256]{1,0:T(8,128)(2,1)S(1)} %pad_maximum_fusion.2.e_ref.refs_0_), channel_id=1, source_target_pairs={{0,1},{1,0},{2,3},{3,2},{4,5},{5,4},{6,7},{7,6},{8,9},{9,8},{10,11... | collective-permute-start | bytes 786440 | tf_op jit(solution)/shard_map/ppermute | solution.py:320
  19.3 16.9 %collective-permute-start.6 = (bf16[512,256]{1,0:T(8,128)(2,1)S(1)}, bf16[512,256]{1,0:T(8,128)(2,1)S(1)}, u32[]{:S(2)}, u32[]{:S(2)}) collective-permute-start(bf16[512,256]{1,0:T(8,128)(2,1)S(1)} %pad_maximum_fusion.2.e_ref.refs_0_), channel_id=1, source_target_pairs={{0,128},{32,160},{64,192},{96,224},{128,0},{160,32},{192,64},{224,... | collective-permute-start | bytes 786440 | tf_op jit(solution)/shard_map/ppermute | solution.py:326
  36.2 15.2 %collective-permute-start.12 = (bf16[1024,256]{1,0:T(8,128)(2,1)S(1)}, bf16[1024,256]{1,0:T(8,128)(2,1)S(1)}, u32[]{:S(2)}, u32[]{:S(2)}) collective-permute-start(bf16[1024,256]{1,0:T(8,128)(2,1)S(1)} %pad_maximum_fusion), channel_id=1, source_target_pairs={{0,32},{32,0},{64,96},{96,64},{128,160},{160,128},{192,224},{224,1... | collective-permute-start | bytes 1572872 | tf_op jit(solution)/shard_map/ppermute | solution.py:323
  36.3 15.1 %collective-permute-start.10 = (bf16[512,256]{1,0:T(8,128)(2,1)S(1)}, bf16[512,256]{1,0:T(8,128)(2,1)S(1)}, u32[]{:S(2)}, u32[]{:S(2)}) collective-permute-start(bf16[512,256]{1,0:T(8,128)(2,1)S(1)} %collective-permute-done.7.e_ref.refs_1_), channel_id=1, source_target_pairs={{0,32},{32,0},{64,96},{96,64},{128,160},{160,128},{192,224},{224,1... | collective-permute-start | bytes 786440 | tf_op jit(solution)/shard_map/ppermute | solution.py:323
  36.8 14.6 %collective-permute-start.11 = (bf16[512,256]{1,0:T(8,128)(2,1)S(1)}, bf16[512,256]{1,0:T(8,128)(2,1)S(1)}, u32[]{:S(2)}, u32[]{:S(2)}) collective-permute-start(bf16[512,256]{1,0:T(8,128)(2,1)S(1)} %collective-permute-done.6.refs_3_.refs_4_), channel_id=1, source_target_pairs={{0,32},{32,0},{64,96},{96,64},{128,160},{160,128},{192,224},{224,1... | collective-permute-start | bytes 786440 | tf_op jit(solution)/shard_map/ppermute | solution.py:323
  36.9 55.5 %collective-permute-start.8 = (bf16[512,256]{1,0:T(8,128)(2,1)S(1)}, bf16[512,256]{1,0:T(8,128)(2,1)S(1)}, u32[]{:S(2)}, u32[]{:S(2)}) collective-permute-start(bf16[512,256]{1,0:T(8,128)(2,1)S(1)} %collective-permute-done.7.e_ref.refs_1_), channel_id=1, source_target_pairs={{0,64},{32,96},{64,128},{96,160},{128,192},{160,224},{192,0},{224,... | collective-permute-start | bytes 786440 | tf_op jit(solution)/shard_map/ppermute | solution.py:326
  51.4 41.0 %collective-permute-start.9 = (bf16[512,256]{1,0:T(8,128)(2,1)S(1)}, bf16[512,256]{1,0:T(8,128)(2,1)S(1)}, u32[]{:S(2)}, u32[]{:S(2)}) collective-permute-start(bf16[512,256]{1,0:T(8,128)(2,1)S(1)} %collective-permute-done.7.e_ref.refs_1_), channel_id=1, source_target_pairs={{0,192},{32,224},{64,0},{96,32},{128,64},{160,96},{192,128},{224,1... | collective-permute-start | bytes 786440 | tf_op jit(solution)/shard_map/ppermute | solution.py:326
  92.5 2.2 %collective-permute-start.15 = (bf16[1024,256]{1,0:T(8,128)(2,1)S(1)}, bf16[1024,256]{1,0:T(8,128)(2,1)S(1)}, u32[]{:S(2)}, u32[]{:S(2)}) collective-permute-start(bf16[1024,256]{1,0:T(8,128)(2,1)S(1)} %pad_maximum_fusion.1), channel_id=1, source_target_pairs={{0,32},{32,0},{64,96},{96,64},{128,160},{160,128},{192,224},{224,1... | collective-permute-start | bytes 1572872 | tf_op jit(solution)/shard_map/ppermute | solution.py:323
  92.6 17.1 %collective-permute-start.13 = (bf16[256,256]{1,0:T(8,128)(2,1)S(1)}, bf16[256,256]{1,0:T(8,128)(2,1)S(1)}, u32[]{:S(2)}, u32[]{:S(2)}) collective-permute-start(bf16[256,256]{1,0:T(8,128)(2,1)S(1)} %slice.26), channel_id=1, source_target_pairs={{0,64},{32,96},{64,128},{96,160},{128,192},{160,224},{192,0},{224,... | collective-permute-start | bytes 393224 | tf_op jit(solution)/shard_map/ppermute | solution.py:326
  94.7 15.0 %collective-permute-start.14 = (bf16[256,256]{1,0:T(8,128)(2,1)S(1)}, bf16[256,256]{1,0:T(8,128)(2,1)S(1)}, u32[]{:S(2)}, u32[]{:S(2)}) collective-permute-start(bf16[256,256]{1,0:T(8,128)(2,1)S(1)} %slice.27), channel_id=1, source_target_pairs={{0,192},{32,224},{64,0},{96,32},{128,64},{160,96},{192,128},{224,1... | collective-permute-start | bytes 393224 | tf_op jit(solution)/shard_map/ppermute | solution.py:326
  109.8 1.6 %collective-permute-start.16 = (bf16[512,256]{1,0:T(8,128)(2,1)S(1)}, bf16[512,256]{1,0:T(8,128)(2,1)S(1)}, u32[]{:S(2)}, u32[]{:S(2)}) collective-permute-start(bf16[512,256]{1,0:T(8,128)(2,1)S(1)} %constant_dynamic-update-slice_fusion.refs_5_.refs_0_), channel_id=1, source_target_pairs={{0,32},{32,0},{64,96},{96,64},{128,160},{160,128},{192,224},{224,1... | collective-permute-start | bytes 786440 | tf_op jit(solution)/shard_map/ppermute | solution.py:323
  112.3 17.0 %collective-permute-start.17 = (bf16[256,256]{1,0:T(8,128)(2,1)S(1)}, bf16[256,256]{1,0:T(8,128)(2,1)S(1)}, u32[]{:S(2)}, u32[]{:S(2)}) collective-permute-start(bf16[256,256]{1,0:T(8,128)(2,1)S(1)} %get-tuple-element.140), channel_id=1, source_target_pairs={{0,4},{1,5},{2,6},{3,7},{4,0},{5,1},{6,2},{7,3},{8,12},{9,13},{10,... | collective-permute-start | bytes 393224 | tf_op jit(solution)/shard_map/ppermute | solution.py:320

commit v6 on v5

--- a/solution.py
+++ b/solution.py
@@ -260,15 +260,22 @@
     own, (e0, e1, c0, c1, ab0, ab1) = pages[:8], pages[8:]
     places = [(ref, 0) for ref in (*own, e0, e1)]
     places += [(ab0, SEG), (ab1, SEG), (c0, 0), (c1, 0), (ab0, 0), (ab1, 0)]
+    def copy(out, j, at):
+        for group in range(0, len(places), 4):
+
+            @pl.when(at // 16 == group // 4)
+            def _():
+                for b in range(group, group + 4):
+                    ref, start = places[b]
+
+                    @pl.when(at // 4 == b)
+                    def _():
+                        rows = rows_at(start + (at % 4) * PAGE, PAGE)
+                        out[j * PAGE : (j + 1) * PAGE] = ref[rows]
+
     for d in range(2):
         for j in range(2):
-            at = meta[2 * d + j]
-            for b, (ref, start) in enumerate(places):
-
-                @pl.when(at // 4 == b)
-                def _():
-                    rows = rows_at(start + (at % 4) * PAGE, PAGE)
-                    outs[d][j * PAGE : (j + 1) * PAGE] = ref[rows]
+            copy(outs[d], j, meta[2 * d + j])
 
 
 def cache_kernel(meta, own, oth, ck, cv, ks, vs):

time: 131 us -> 131 us (level)
  no operation moved by 1% of the time
where the time goes in v6:
time: 131 us
  Pallas kernels  89.4 us (68%)
  starting transfers between devices  34.3 us (26%)
  waiting for transfers between devices  4.06 us (3%)
    pallas_call x7, Pallas kernels, call(): pl.pallas_call(kernel, in_specs=[SMEM] + [VMEM] * len(arrays), out_specs=...  89.4 us
    ppermute x7, starting transfers between devices, over_y(): return lax.ppermute(x, 'blk', [(i, (i + 2 * d) % 8) for i in range(8)])  19.4 us
    ppermute x5, starting transfers between devices, over_dec(): return lax.ppermute(x, 'dec', [(i, i ^ m) for i in range(8)])  11.9 us
    ppermute x6, starting transfers between devices, over_core(): return lax.ppermute(x, 'blk', [(i, i ^ 1) for i in range(8)])  3.07 us
  transfers between devices with their start and end apart: 18, of which 3 were waited for; matrix products, arithmetic and copies ran while one was open for 1% of the time, Pallas kernels for 67%

profile of v6, /device:TPU:17, one launch (start us, length us, event | category | flops | bytes accessed | tf_op | source)
XLA Modules:
  0.0 130.6 jit_solution(1829151146513959941)
XLA Ops:
  0.7 0.8 fusion.8
  1.5 2.8 %collective-permute-start.1 = (bf16[128,256]{1,0:T(8,128)(2,1)S(1)}, bf16[128,256]{1,0:T(8,128)(2,1)S(1)}, u32[]{:S(2)}, u32[]{:S(2)}) collective-permute-start(bf16[128,256]{1,0:T(8,128)(2,1)S(1)} %get-tuple-element.146), channel_id=1, source_target_pairs={{0,4},{1,5},{2,6},{3,7},{4,0},{5,1},{6,2},{7,3},{8,12},{9,13},{10,... | collective-permute-start | bytes 196616 | tf_op jit(solution)/shard_map/ppermute | solution.py:327
  4.4 0.9 collective-permute-start.2
  5.5 0.2 compare_reduce_fusion
  5.7 0.2 fusion
  6.2 2.2 %collective-permute-done = bf16[128,256]{1,0:T(8,128)(2,1)S(1)} collective-permute-done((bf16[128,256]{1,0:T(8,128)(2,1)S(1)}, bf16[128,256]{1,0:T(8,128)(2,1)S(1)}, u32[]{:S(2)}, u32[]{:S(2)}) %collective-permute-start) | collective-permute-done | bytes 65568 | tf_op jit(solution)/shard_map/ppermute | solution.py:327
  8.3 0.3 collective-permute-done.2
  8.7 2.2 %collective-permute-start.3 = (bf16[512,256]{1,0:T(8,128)(2,1)S(1)}, bf16[512,256]{1,0:T(8,128)(2,1)S(1)}, u32[]{:S(2)}, u32[]{:S(2)}) collective-permute-start(bf16[512,256]{1,0:T(8,128)(2,1)S(1)} %pad_maximum_fusion.2.e_ref.refs_0_), channel_id=1, source_target_pairs={{0,32},{32,0},{64,96},{96,64},{128,160},{160,128},{192,224},{224,1... | collective-permute-start | bytes 786440 | tf_op jit(solution)/shard_map/ppermute | solution.py:330
  10.9 1.0 collective-permute-start.4
  11.9 0.5 collective-permute-start.5
  12.4 6.9 %collective-permute-start.7 = (bf16[512,256]{1,0:T(8,128)(2,1)S(1)}, bf16[512,256]{1,0:T(8,128)(2,1)S(1)}, u32[]{:S(2)}, u32[]{:S(2)}) collective-permute-start(bf16[512,256]{1,0:T(8,128)(2,1)S(1)} %pad_maximum_fusion.2.e_ref.refs_0_), channel_id=1, source_target_pairs={{0,1},{1,0},{2,3},{3,2},{4,5},{5,4},{6,7},{7,6},{8,9},{9,8},{10,11... | collective-permute-start | bytes 786440 | tf_op jit(solution)/shard_map/ppermute | solution.py:327
  19.3 1.3 %collective-permute-start.6 = (bf16[512,256]{1,0:T(8,128)(2,1)S(1)}, bf16[512,256]{1,0:T(8,128)(2,1)S(1)}, u32[]{:S(2)}, u32[]{:S(2)}) collective-permute-start(bf16[512,256]{1,0:T(8,128)(2,1)S(1)} %pad_maximum_fusion.2.e_ref.refs_0_), channel_id=1, source_target_pairs={{0,128},{32,160},{64,192},{96,224},{128,0},{160,32},{192,64},{224,... | collective-permute-start | bytes 786440 | tf_op jit(solution)/shard_map/ppermute | solution.py:333
  20.6 14.8 %shard_map.83 = (bf16[1024,256]{1,0:T(8,128)(2,1)S(1)}, f32[2048,128]{1,0:T(8,128)S(1)}, f32[2048,1]{1,0:T(8,128)S(1)}, f32[2048,1]{1,0:T(8,128)S(1)}, f32[8,2]{1,0:T(8,128)S(1)}) custom-call(s32[4]{0:T(128)S(1)} %get-tuple-element.76.meta, bf16[1024,256]{1,0:T(8,128)(2,1)S(1)} %copy-done, bf16[512,256]{1,0:T(8,128)(2,1)S(1)} %pad_maximum_fusion.2.e_ref.refs_0_, ...), custom_call_target="tpu_custom_call" | custom-call | tf_op jit(solution)/shard_map/pallas_call | solution.py:310
  35.4 0.7 shard_map.84
  36.3 0.5 collective-permute-start.10
  36.9 14.5 %collective-permute-start.8 = (bf16[512,256]{1,0:T(8,128)(2,1)S(1)}, bf16[512,256]{1,0:T(8,128)(2,1)S(1)}, u32[]{:S(2)}, u32[]{:S(2)}) collective-permute-start(bf16[512,256]{1,0:T(8,128)(2,1)S(1)} %collective-permute-done.7.e_ref.refs_1_), channel_id=1, source_target_pairs={{0,64},{32,96},{64,128},{96,160},{128,192},{160,224},{192,0},{224,... | collective-permute-start | bytes 786440 | tf_op jit(solution)/shard_map/ppermute | solution.py:333
  51.4 41.0 %shard_map.85 = (f32[2048,128]{1,0:T(8,128)S(1)}, f32[2048,1]{1,0:T(8,128)S(1)}, f32[2048,1]{1,0:T(8,128)S(1)}, f32[8,2]{1,0:T(8,128)S(1)}) custom-call(s32[4]{0:T(128)S(1)} %get-tuple-element.91.meta, bf16[1024,256]{1,0:T(8,128)(2,1)S(1)} %get-tuple-element.79.q_ref, ...), custom_call_target="tpu_custom_call", output_to_operand_aliasing={{0}: (9, {}), {1}: (10, {}), {2}: (11, {}), {3}: (12, {})} | custom-call | tf_op jit(solution)/shard_map/pallas_call | solution.py:310
  92.6 2.1 %collective-permute-start.13 = (bf16[256,256]{1,0:T(8,128)(2,1)S(1)}, bf16[256,256]{1,0:T(8,128)(2,1)S(1)}, u32[]{:S(2)}, u32[]{:S(2)}) collective-permute-start(bf16[256,256]{1,0:T(8,128)(2,1)S(1)} %slice.26), channel_id=1, source_target_pairs={{0,64},{32,96},{64,128},{96,160},{128,192},{160,224},{192,0},{224,... | collective-permute-start | bytes 393224 | tf_op jit(solution)/shard_map/ppermute | solution.py:333
  94.7 15.0 %shard_map.86 = (f32[2048,128]{1,0:T(8,128)S(1)}, f32[2048,1]{1,0:T(8,128)S(1)}, f32[2048,1]{1,0:T(8,128)S(1)}, f32[8,2]{1,0:T(8,128)S(1)}) custom-call(s32[4]{0:T(128)S(1)} %get-tuple-element.111.meta, bf16[1024,256]{1,0:T(8,128)(2,1)S(1)} %get-tuple-element.79.q_ref, ...), custom_call_target="tpu_custom_call", output_to_operand_aliasing={{0}: (5, {}), {1}: (6, {}), {2}: (7, {}), {3}: (8, {})} | custom-call | tf_op jit(solution)/shard_map/pallas_call | solution.py:310
  109.9 1.5 %collective-permute-done.16.refs_11_.refs_1_ = bf16[512,256]{1,0:T(8,128)(2,1)S(1)} collective-permute-done((bf16[512,256]{1,0:T(8,128)(2,1)S(1)}, bf16[512,256]{1,0:T(8,128)(2,1)S(1)}, u32[]{:S(2)}, u32[]{:S(2)}) %collective-permute-start.16) | collective-permute-done | bytes 262176 | tf_op jit(solution)/shard_map/ppermute | solution.py:330
  111.4 0.7 shard_map.87
  112.1 1.3 collective-permute-start.17
  113.4 15.8 %shard_map.88 = (f32[2048,128]{1,0:T(8,128)S(1)}, f32[2048,1]{1,0:T(8,128)S(1)}, f32[2048,1]{1,0:T(8,128)S(1)}, f32[8,2]{1,0:T(8,128)S(1)}, bf16[1024,256]{1,0:T(8,128)(2,1)}) custom-call(s32[4]{0:T(128)S(1)} %get-tuple-element.75.meta, ...), custom_call_target="tpu_custom_call", output_to_operand_aliasing={{0}: (4, {}), {1}: (5, {}), {2}: (6, {}), {3}: (7, {})} | custom-call | tf_op jit(solution)/shard_map/pallas_call | solution.py:310
  129.1 1.4 %shard_map.89 = (bf16[256,256]{1,0:T(8,128)(2,1)}, bf16[256,256]{1,0:T(8,128)(2,1)}, f32[2,2]{1,0:T(2,128)}, f32[2,2]{1,0:T(2,128)}) custom-call(s32[3]{0:T(128)S(1)} %pad_add_fusion.meta, bf16[256,256]{1,0:T(8,128)(2,1)S(1)} %get-tuple-element.139.own, bf16[256,256]{1,0:T(8,128)(2,1)S(1)} %collective-permute-done.17.oth), custom_call_target="tpu_custom_call" | custom-call | tf_op jit(solution)/shard_map/pallas_call | solution.py:310
  (43 shorter events, 1.1 us)
Async XLA Ops:
  0.7 4.8 %copy-start.1 = (s32[64]{0:T(128)S(1)}, s32[64]{0:T(128)}, u32[]{:S(2)}) copy-start(s32[64]{0:T(128)} %param.7) | copy-start | bytes 772
  1.5 19.1 %copy-start = (bf16[1024,256]{1,0:T(8,128)(2,1)S(1)}, bf16[1024,256]{1,0:T(8,128)(2,1)}, u32[]{:S(2)}) copy-start(bf16[1024,256]{1,0:T(8,128)(2,1)} %q_ref.1) | copy-start | bytes 1572868
  1.5 6.8 %collective-permute-start.1 = (bf16[128,256]{1,0:T(8,128)(2,1)S(1)}, bf16[128,256]{1,0:T(8,128)(2,1)S(1)}, u32[]{:S(2)}, u32[]{:S(2)}) collective-permute-start(bf16[128,256]{1,0:T(8,128)(2,1)S(1)} %get-tuple-element.146), channel_id=1, source_target_pairs={{0,4},{1,5},{2,6},{3,7},{4,0},{5,1},{6,2},{7,3},{8,12},{9,13},{10,... | collective-permute-start | bytes 196616 | tf_op jit(solution)/shard_map/ppermute | solution.py:327
  4.4 4.3 %collective-permute-start.2 = (bf16[128,256]{1,0:T(8,128)(2,1)S(1)}, bf16[128,256]{1,0:T(8,128)(2,1)S(1)}, u32[]{:S(2)}, u32[]{:S(2)}) collective-permute-start(bf16[128,256]{1,0:T(8,128)(2,1)S(1)} %get-tuple-element.146), channel_id=1, source_target_pairs={{0,6},{1,7},{2,4},{3,5},{4,2},{5,3},{6,0},{7,1},{8,14},{9,15},{10,... | collective-permute-start | bytes 196616 | tf_op jit(solution)/shard_map/ppermute | solution.py:327
  5.2 3.1 %collective-permute-start = (bf16[128,256]{1,0:T(8,128)(2,1)S(1)}, bf16[128,256]{1,0:T(8,128)(2,1)S(1)}, u32[]{:S(2)}, u32[]{:S(2)}) collective-permute-start(bf16[128,256]{1,0:T(8,128)(2,1)S(1)} %get-tuple-element.145), channel_id=1, source_target_pairs={{0,2},{1,3},{2,0},{3,1},{4,6},{5,7},{6,4},{7,5},{8,10},{9,11},{10,... | collective-permute-start | bytes 196616 | tf_op jit(solution)/shard_map/ppermute | solution.py:327
  8.7 10.6 %collective-permute-start.3 = (bf16[512,256]{1,0:T(8,128)(2,1)S(1)}, bf16[512,256]{1,0:T(8,128)(2,1)S(1)}, u32[]{:S(2)}, u32[]{:S(2)}) collective-permute-start(bf16[512,256]{1,0:T(8,128)(2,1)S(1)} %pad_maximum_fusion.2.e_ref.refs_0_), channel_id=1, source_target_pairs={{0,32},{32,0},{64,96},{96,64},{128,160},{160,128},{192,224},{224,1... | collective-permute-start | bytes 786440 | tf_op jit(solution)/shard_map/ppermute | solution.py:330
  10.9 24.5 %collective-permute-start.4 = (bf16[512,256]{1,0:T(8,128)(2,1)S(1)}, bf16[512,256]{1,0:T(8,128)(2,1)S(1)}, u32[]{:S(2)}, u32[]{:S(2)}) collective-permute-start(bf16[512,256]{1,0:T(8,128)(2,1)S(1)} %pad_maximum_fusion.2.e_ref.refs_0_), channel_id=1, source_target_pairs={{0,64},{32,96},{64,128},{96,160},{128,192},{160,224},{192,0},{224,... | collective-permute-start | bytes 786440 | tf_op jit(solution)/shard_map/ppermute | solution.py:333
  11.9 23.5 %collective-permute-start.5 = (bf16[512,256]{1,0:T(8,128)(2,1)S(1)}, bf16[512,256]{1,0:T(8,128)(2,1)S(1)}, u32[]{:S(2)}, u32[]{:S(2)}) collective-permute-start(bf16[512,256]{1,0:T(8,128)(2,1)S(1)} %pad_maximum_fusion.2.e_ref.refs_0_), channel_id=1, source_target_pairs={{0,192},{32,224},{64,0},{96,32},{128,64},{160,96},{192,128},{224,1... | collective-permute-start | bytes 786440 | tf_op jit(solution)/shard_map/ppermute | solution.py:333
  12.4 23.8 %collective-permute-start.7 = (bf16[512,256]{1,0:T(8,128)(2,1)S(1)}, bf16[512,256]{1,0:T(8,128)(2,1)S(1)}, u32[]{:S(2)}, u32[]{:S(2)}) collective-permute-start(bf16[512,256]{1,0:T(8,128)(2,1)S(1)} %pad_maximum_fusion.2.e_ref.refs_0_), channel_id=1, source_target_pairs={{0,1},{1,0},{2,3},{3,2},{4,5},{5,4},{6,7},{7,6},{8,9},{9,8},{10,11... | collective-permute-start | bytes 786440 | tf_op jit(solution)/shard_map/ppermute | solution.py:327
  19.3 16.9 %collective-permute-start.6 = (bf16[512,256]{1,0:T(8,128)(2,1)S(1)}, bf16[512,256]{1,0:T(8,128)(2,1)S(1)}, u32[]{:S(2)}, u32[]{:S(2)}) collective-permute-start(bf16[512,256]{1,0:T(8,128)(2,1)S(1)} %pad_maximum_fusion.2.e_ref.refs_0_), channel_id=1, source_target_pairs={{0,128},{32,160},{64,192},{96,224},{128,0},{160,32},{192,64},{224,... | collective-permute-start | bytes 786440 | tf_op jit(solution)/shard_map/ppermute | solution.py:333
  36.2 15.2 %collective-permute-start.12 = (bf16[1024,256]{1,0:T(8,128)(2,1)S(1)}, bf16[1024,256]{1,0:T(8,128)(2,1)S(1)}, u32[]{:S(2)}, u32[]{:S(2)}) collective-permute-start(bf16[1024,256]{1,0:T(8,128)(2,1)S(1)} %pad_maximum_fusion), channel_id=1, source_target_pairs={{0,32},{32,0},{64,96},{96,64},{128,160},{160,128},{192,224},{224,1... | collective-permute-start | bytes 1572872 | tf_op jit(solution)/shard_map/ppermute | solution.py:330
  36.3 15.1 %collective-permute-start.10 = (bf16[512,256]{1,0:T(8,128)(2,1)S(1)}, bf16[512,256]{1,0:T(8,128)(2,1)S(1)}, u32[]{:S(2)}, u32[]{:S(2)}) collective-permute-start(bf16[512,256]{1,0:T(8,128)(2,1)S(1)} %collective-permute-done.7.e_ref.refs_1_), channel_id=1, source_target_pairs={{0,32},{32,0},{64,96},{96,64},{128,160},{160,128},{192,224},{224,1... | collective-permute-start | bytes 786440 | tf_op jit(solution)/shard_map/ppermute | solution.py:330
  36.8 14.6 %collective-permute-start.11 = (bf16[512,256]{1,0:T(8,128)(2,1)S(1)}, bf16[512,256]{1,0:T(8,128)(2,1)S(1)}, u32[]{:S(2)}, u32[]{:S(2)}) collective-permute-start(bf16[512,256]{1,0:T(8,128)(2,1)S(1)} %collective-permute-done.6.refs_3_.refs_4_), channel_id=1, source_target_pairs={{0,32},{32,0},{64,96},{96,64},{128,160},{160,128},{192,224},{224,1... | collective-permute-start | bytes 786440 | tf_op jit(solution)/shard_map/ppermute | solution.py:330
  36.9 55.5 %collective-permute-start.8 = (bf16[512,256]{1,0:T(8,128)(2,1)S(1)}, bf16[512,256]{1,0:T(8,128)(2,1)S(1)}, u32[]{:S(2)}, u32[]{:S(2)}) collective-permute-start(bf16[512,256]{1,0:T(8,128)(2,1)S(1)} %collective-permute-done.7.e_ref.refs_1_), channel_id=1, source_target_pairs={{0,64},{32,96},{64,128},{96,160},{128,192},{160,224},{192,0},{224,... | collective-permute-start | bytes 786440 | tf_op jit(solution)/shard_map/ppermute | solution.py:333
  51.4 41.0 %collective-permute-start.9 = (bf16[512,256]{1,0:T(8,128)(2,1)S(1)}, bf16[512,256]{1,0:T(8,128)(2,1)S(1)}, u32[]{:S(2)}, u32[]{:S(2)}) collective-permute-start(bf16[512,256]{1,0:T(8,128)(2,1)S(1)} %collective-permute-done.7.e_ref.refs_1_), channel_id=1, source_target_pairs={{0,192},{32,224},{64,0},{96,32},{128,64},{160,96},{192,128},{224,1... | collective-permute-start | bytes 786440 | tf_op jit(solution)/shard_map/ppermute | solution.py:333
  92.5 2.2 %collective-permute-start.15 = (bf16[1024,256]{1,0:T(8,128)(2,1)S(1)}, bf16[1024,256]{1,0:T(8,128)(2,1)S(1)}, u32[]{:S(2)}, u32[]{:S(2)}) collective-permute-start(bf16[1024,256]{1,0:T(8,128)(2,1)S(1)} %pad_maximum_fusion.1), channel_id=1, source_target_pairs={{0,32},{32,0},{64,96},{96,64},{128,160},{160,128},{192,224},{224,1... | collective-permute-start | bytes 1572872 | tf_op jit(solution)/shard_map/ppermute | solution.py:330
  92.6 17.1 %collective-permute-start.13 = (bf16[256,256]{1,0:T(8,128)(2,1)S(1)}, bf16[256,256]{1,0:T(8,128)(2,1)S(1)}, u32[]{:S(2)}, u32[]{:S(2)}) collective-permute-start(bf16[256,256]{1,0:T(8,128)(2,1)S(1)} %slice.26), channel_id=1, source_target_pairs={{0,64},{32,96},{64,128},{96,160},{128,192},{160,224},{192,0},{224,... | collective-permute-start | bytes 393224 | tf_op jit(solution)/shard_map/ppermute | solution.py:333
  94.7 15.0 %collective-permute-start.14 = (bf16[256,256]{1,0:T(8,128)(2,1)S(1)}, bf16[256,256]{1,0:T(8,128)(2,1)S(1)}, u32[]{:S(2)}, u32[]{:S(2)}) collective-permute-start(bf16[256,256]{1,0:T(8,128)(2,1)S(1)} %slice.27), channel_id=1, source_target_pairs={{0,192},{32,224},{64,0},{96,32},{128,64},{160,96},{192,128},{224,1... | collective-permute-start | bytes 393224 | tf_op jit(solution)/shard_map/ppermute | solution.py:333
  109.8 1.6 %collective-permute-start.16 = (bf16[512,256]{1,0:T(8,128)(2,1)S(1)}, bf16[512,256]{1,0:T(8,128)(2,1)S(1)}, u32[]{:S(2)}, u32[]{:S(2)}) collective-permute-start(bf16[512,256]{1,0:T(8,128)(2,1)S(1)} %constant_dynamic-update-slice_fusion.refs_5_.refs_0_), channel_id=1, source_target_pairs={{0,32},{32,0},{64,96},{96,64},{128,160},{160,128},{192,224},{224,1... | collective-permute-start | bytes 786440 | tf_op jit(solution)/shard_map/ppermute | solution.py:330
  112.1 17.0 %collective-permute-start.17 = (bf16[256,256]{1,0:T(8,128)(2,1)S(1)}, bf16[256,256]{1,0:T(8,128)(2,1)S(1)}, u32[]{:S(2)}, u32[]{:S(2)}) collective-permute-start(bf16[256,256]{1,0:T(8,128)(2,1)S(1)} %get-tuple-element.140), channel_id=1, source_target_pairs={{0,4},{1,5},{2,6},{3,7},{4,0},{5,1},{6,2},{7,3},{8,12},{9,13},{10,... | collective-permute-start | bytes 393224 | tf_op jit(solution)/shard_map/ppermute | solution.py:327

commit v7 on v6

--- a/solution.py
+++ b/solution.py
@@ -23,9 +23,8 @@
 
 
 def longest(x):
-    x = x.astype(jnp.float32)
     squares = jnp.dot(
-        (x * x).astype(jnp.bfloat16),
+        x * x,
         jnp.ones((HD, HD), jnp.bfloat16),
         preferred_element_type=jnp.float32,
     )

time: 131 us -> 131 us (level)
  no operation moved by 1% of the time
where the time goes in v7:
time: 131 us
  Pallas kernels  89.5 us (68%)
  starting transfers between devices  34.3 us (26%)
  waiting for transfers between devices  4.06 us (3%)
    pallas_call x7, Pallas kernels, call(): pl.pallas_call(kernel, in_specs=[SMEM] + [VMEM] * len(arrays), out_specs=...  89.5 us
    ppermute x7, starting transfers between devices, over_y(): return lax.ppermute(x, 'blk', [(i, (i + 2 * d) % 8) for i in range(8)])  19.4 us
    ppermute x5, starting transfers between devices, over_dec(): return lax.ppermute(x, 'dec', [(i, i ^ m) for i in range(8)])  11.9 us
    ppermute x6, starting transfers between devices, over_core(): return lax.ppermute(x, 'blk', [(i, i ^ 1) for i in range(8)])  3.07 us
  transfers between devices with their start and end apart: 18, of which 3 were waited for; matrix products, arithmetic and copies ran while one was open for 1% of the time, Pallas kernels for 67%

profile of v7, /device:TPU:17, one launch (start us, length us, event | category | flops | bytes accessed | tf_op | source)
XLA Modules:
  0.0 130.7 jit_solution(9110928677282725808)
XLA Ops:
  0.7 0.8 fusion.8
  1.5 2.8 %collective-permute-start.1 = (bf16[128,256]{1,0:T(8,128)(2,1)S(1)}, bf16[128,256]{1,0:T(8,128)(2,1)S(1)}, u32[]{:S(2)}, u32[]{:S(2)}) collective-permute-start(bf16[128,256]{1,0:T(8,128)(2,1)S(1)} %get-tuple-element.146), channel_id=1, source_target_pairs={{0,4},{1,5},{2,6},{3,7},{4,0},{5,1},{6,2},{7,3},{8,12},{9,13},{10,... | collective-permute-start | bytes 196616 | tf_op jit(solution)/shard_map/ppermute | solution.py:326
  4.4 0.9 collective-permute-start.2
  5.5 0.2 compare_reduce_fusion
  5.7 0.2 fusion
  6.2 2.2 %collective-permute-done = bf16[128,256]{1,0:T(8,128)(2,1)S(1)} collective-permute-done((bf16[128,256]{1,0:T(8,128)(2,1)S(1)}, bf16[128,256]{1,0:T(8,128)(2,1)S(1)}, u32[]{:S(2)}, u32[]{:S(2)}) %collective-permute-start) | collective-permute-done | bytes 65568 | tf_op jit(solution)/shard_map/ppermute | solution.py:326
  8.3 0.3 collective-permute-done.2
  8.7 2.2 %collective-permute-start.3 = (bf16[512,256]{1,0:T(8,128)(2,1)S(1)}, bf16[512,256]{1,0:T(8,128)(2,1)S(1)}, u32[]{:S(2)}, u32[]{:S(2)}) collective-permute-start(bf16[512,256]{1,0:T(8,128)(2,1)S(1)} %pad_maximum_fusion.2.e_ref.refs_0_), channel_id=1, source_target_pairs={{0,32},{32,0},{64,96},{96,64},{128,160},{160,128},{192,224},{224,1... | collective-permute-start | bytes 786440 | tf_op jit(solution)/shard_map/ppermute | solution.py:329
  10.9 1.0 collective-permute-start.4
  11.9 0.5 collective-permute-start.5
  12.4 6.9 %collective-permute-start.7 = (bf16[512,256]{1,0:T(8,128)(2,1)S(1)}, bf16[512,256]{1,0:T(8,128)(2,1)S(1)}, u32[]{:S(2)}, u32[]{:S(2)}) collective-permute-start(bf16[512,256]{1,0:T(8,128)(2,1)S(1)} %pad_maximum_fusion.2.e_ref.refs_0_), channel_id=1, source_target_pairs={{0,1},{1,0},{2,3},{3,2},{4,5},{5,4},{6,7},{7,6},{8,9},{9,8},{10,11... | collective-permute-start | bytes 786440 | tf_op jit(solution)/shard_map/ppermute | solution.py:326
  19.3 1.3 %collective-permute-start.6 = (bf16[512,256]{1,0:T(8,128)(2,1)S(1)}, bf16[512,256]{1,0:T(8,128)(2,1)S(1)}, u32[]{:S(2)}, u32[]{:S(2)}) collective-permute-start(bf16[512,256]{1,0:T(8,128)(2,1)S(1)} %pad_maximum_fusion.2.e_ref.refs_0_), channel_id=1, source_target_pairs={{0,128},{32,160},{64,192},{96,224},{128,0},{160,32},{192,64},{224,... | collective-permute-start | bytes 786440 | tf_op jit(solution)/shard_map/ppermute | solution.py:332
  20.6 14.8 %shard_map.83 = (bf16[1024,256]{1,0:T(8,128)(2,1)S(1)}, f32[2048,128]{1,0:T(8,128)S(1)}, f32[2048,1]{1,0:T(8,128)S(1)}, f32[2048,1]{1,0:T(8,128)S(1)}, f32[8,2]{1,0:T(8,128)S(1)}) custom-call(s32[4]{0:T(128)S(1)} %get-tuple-element.76.meta, bf16[1024,256]{1,0:T(8,128)(2,1)S(1)} %copy-done, bf16[512,256]{1,0:T(8,128)(2,1)S(1)} %pad_maximum_fusion.2.e_ref.refs_0_, ...), custom_call_target="tpu_custom_call" | custom-call | tf_op jit(solution)/shard_map/pallas_call | solution.py:309
  35.4 0.7 shard_map.84
  36.3 0.5 collective-permute-start.10
  36.9 14.5 %collective-permute-start.8 = (bf16[512,256]{1,0:T(8,128)(2,1)S(1)}, bf16[512,256]{1,0:T(8,128)(2,1)S(1)}, u32[]{:S(2)}, u32[]{:S(2)}) collective-permute-start(bf16[512,256]{1,0:T(8,128)(2,1)S(1)} %collective-permute-done.7.e_ref.refs_1_), channel_id=1, source_target_pairs={{0,64},{32,96},{64,128},{96,160},{128,192},{160,224},{192,0},{224,... | collective-permute-start | bytes 786440 | tf_op jit(solution)/shard_map/ppermute | solution.py:332
  51.4 41.1 %shard_map.85 = (f32[2048,128]{1,0:T(8,128)S(1)}, f32[2048,1]{1,0:T(8,128)S(1)}, f32[2048,1]{1,0:T(8,128)S(1)}, f32[8,2]{1,0:T(8,128)S(1)}) custom-call(s32[4]{0:T(128)S(1)} %get-tuple-element.91.meta, bf16[1024,256]{1,0:T(8,128)(2,1)S(1)} %get-tuple-element.79.q_ref, ...), custom_call_target="tpu_custom_call", output_to_operand_aliasing={{0}: (9, {}), {1}: (10, {}), {2}: (11, {}), {3}: (12, {})} | custom-call | tf_op jit(solution)/shard_map/pallas_call | solution.py:309
  92.7 2.1 %collective-permute-start.13 = (bf16[256,256]{1,0:T(8,128)(2,1)S(1)}, bf16[256,256]{1,0:T(8,128)(2,1)S(1)}, u32[]{:S(2)}, u32[]{:S(2)}) collective-permute-start(bf16[256,256]{1,0:T(8,128)(2,1)S(1)} %slice.26), channel_id=1, source_target_pairs={{0,64},{32,96},{64,128},{96,160},{128,192},{160,224},{192,0},{224,... | collective-permute-start | bytes 393224 | tf_op jit(solution)/shard_map/ppermute | solution.py:332
  94.8 15.1 %shard_map.86 = (f32[2048,128]{1,0:T(8,128)S(1)}, f32[2048,1]{1,0:T(8,128)S(1)}, f32[2048,1]{1,0:T(8,128)S(1)}, f32[8,2]{1,0:T(8,128)S(1)}) custom-call(s32[4]{0:T(128)S(1)} %get-tuple-element.111.meta, bf16[1024,256]{1,0:T(8,128)(2,1)S(1)} %get-tuple-element.79.q_ref, ...), custom_call_target="tpu_custom_call", output_to_operand_aliasing={{0}: (5, {}), {1}: (6, {}), {2}: (7, {}), {3}: (8, {})} | custom-call | tf_op jit(solution)/shard_map/pallas_call | solution.py:309
  110.0 1.5 %collective-permute-done.16.refs_11_.refs_1_ = bf16[512,256]{1,0:T(8,128)(2,1)S(1)} collective-permute-done((bf16[512,256]{1,0:T(8,128)(2,1)S(1)}, bf16[512,256]{1,0:T(8,128)(2,1)S(1)}, u32[]{:S(2)}, u32[]{:S(2)}) %collective-permute-start.16) | collective-permute-done | bytes 262176 | tf_op jit(solution)/shard_map/ppermute | solution.py:329
  111.6 0.7 shard_map.87
  112.3 1.3 collective-permute-start.17
  113.5 15.7 %shard_map.88 = (f32[2048,128]{1,0:T(8,128)S(1)}, f32[2048,1]{1,0:T(8,128)S(1)}, f32[2048,1]{1,0:T(8,128)S(1)}, f32[8,2]{1,0:T(8,128)S(1)}, bf16[1024,256]{1,0:T(8,128)(2,1)}) custom-call(s32[4]{0:T(128)S(1)} %get-tuple-element.75.meta, ...), custom_call_target="tpu_custom_call", output_to_operand_aliasing={{0}: (4, {}), {1}: (5, {}), {2}: (6, {}), {3}: (7, {})} | custom-call | tf_op jit(solution)/shard_map/pallas_call | solution.py:309
  129.3 1.4 %shard_map.89 = (bf16[256,256]{1,0:T(8,128)(2,1)}, bf16[256,256]{1,0:T(8,128)(2,1)}, f32[2,2]{1,0:T(2,128)}, f32[2,2]{1,0:T(2,128)}) custom-call(s32[3]{0:T(128)S(1)} %pad_add_fusion.meta, bf16[256,256]{1,0:T(8,128)(2,1)S(1)} %get-tuple-element.139.own, bf16[256,256]{1,0:T(8,128)(2,1)S(1)} %collective-permute-done.17.oth), custom_call_target="tpu_custom_call" | custom-call | tf_op jit(solution)/shard_map/pallas_call | solution.py:309
  (43 shorter events, 1.1 us)
Async XLA Ops:
  0.7 4.8 %copy-start.1 = (s32[64]{0:T(128)S(1)}, s32[64]{0:T(128)}, u32[]{:S(2)}) copy-start(s32[64]{0:T(128)} %param.7) | copy-start | bytes 772
  1.5 19.1 %copy-start = (bf16[1024,256]{1,0:T(8,128)(2,1)S(1)}, bf16[1024,256]{1,0:T(8,128)(2,1)}, u32[]{:S(2)}) copy-start(bf16[1024,256]{1,0:T(8,128)(2,1)} %q_ref.1) | copy-start | bytes 1572868
  1.5 6.8 %collective-permute-start.1 = (bf16[128,256]{1,0:T(8,128)(2,1)S(1)}, bf16[128,256]{1,0:T(8,128)(2,1)S(1)}, u32[]{:S(2)}, u32[]{:S(2)}) collective-permute-start(bf16[128,256]{1,0:T(8,128)(2,1)S(1)} %get-tuple-element.146), channel_id=1, source_target_pairs={{0,4},{1,5},{2,6},{3,7},{4,0},{5,1},{6,2},{7,3},{8,12},{9,13},{10,... | collective-permute-start | bytes 196616 | tf_op jit(solution)/shard_map/ppermute | solution.py:326
  4.4 4.3 %collective-permute-start.2 = (bf16[128,256]{1,0:T(8,128)(2,1)S(1)}, bf16[128,256]{1,0:T(8,128)(2,1)S(1)}, u32[]{:S(2)}, u32[]{:S(2)}) collective-permute-start(bf16[128,256]{1,0:T(8,128)(2,1)S(1)} %get-tuple-element.146), channel_id=1, source_target_pairs={{0,6},{1,7},{2,4},{3,5},{4,2},{5,3},{6,0},{7,1},{8,14},{9,15},{10,... | collective-permute-start | bytes 196616 | tf_op jit(solution)/shard_map/ppermute | solution.py:326
  5.2 3.1 %collective-permute-start = (bf16[128,256]{1,0:T(8,128)(2,1)S(1)}, bf16[128,256]{1,0:T(8,128)(2,1)S(1)}, u32[]{:S(2)}, u32[]{:S(2)}) collective-permute-start(bf16[128,256]{1,0:T(8,128)(2,1)S(1)} %get-tuple-element.145), channel_id=1, source_target_pairs={{0,2},{1,3},{2,0},{3,1},{4,6},{5,7},{6,4},{7,5},{8,10},{9,11},{10,... | collective-permute-start | bytes 196616 | tf_op jit(solution)/shard_map/ppermute | solution.py:326
  8.7 10.6 %collective-permute-start.3 = (bf16[512,256]{1,0:T(8,128)(2,1)S(1)}, bf16[512,256]{1,0:T(8,128)(2,1)S(1)}, u32[]{:S(2)}, u32[]{:S(2)}) collective-permute-start(bf16[512,256]{1,0:T(8,128)(2,1)S(1)} %pad_maximum_fusion.2.e_ref.refs_0_), channel_id=1, source_target_pairs={{0,32},{32,0},{64,96},{96,64},{128,160},{160,128},{192,224},{224,1... | collective-permute-start | bytes 786440 | tf_op jit(solution)/shard_map/ppermute | solution.py:329
  10.9 24.5 %collective-permute-start.4 = (bf16[512,256]{1,0:T(8,128)(2,1)S(1)}, bf16[512,256]{1,0:T(8,128)(2,1)S(1)}, u32[]{:S(2)}, u32[]{:S(2)}) collective-permute-start(bf16[512,256]{1,0:T(8,128)(2,1)S(1)} %pad_maximum_fusion.2.e_ref.refs_0_), channel_id=1, source_target_pairs={{0,64},{32,96},{64,128},{96,160},{128,192},{160,224},{192,0},{224,... | collective-permute-start | bytes 786440 | tf_op jit(solution)/shard_map/ppermute | solution.py:332
  11.9 23.5 %collective-permute-start.5 = (bf16[512,256]{1,0:T(8,128)(2,1)S(1)}, bf16[512,256]{1,0:T(8,128)(2,1)S(1)}, u32[]{:S(2)}, u32[]{:S(2)}) collective-permute-start(bf16[512,256]{1,0:T(8,128)(2,1)S(1)} %pad_maximum_fusion.2.e_ref.refs_0_), channel_id=1, source_target_pairs={{0,192},{32,224},{64,0},{96,32},{128,64},{160,96},{192,128},{224,1... | collective-permute-start | bytes 786440 | tf_op jit(solution)/shard_map/ppermute | solution.py:332
  12.4 23.8 %collective-permute-start.7 = (bf16[512,256]{1,0:T(8,128)(2,1)S(1)}, bf16[512,256]{1,0:T(8,128)(2,1)S(1)}, u32[]{:S(2)}, u32[]{:S(2)}) collective-permute-start(bf16[512,256]{1,0:T(8,128)(2,1)S(1)} %pad_maximum_fusion.2.e_ref.refs_0_), channel_id=1, source_target_pairs={{0,1},{1,0},{2,3},{3,2},{4,5},{5,4},{6,7},{7,6},{8,9},{9,8},{10,11... | collective-permute-start | bytes 786440 | tf_op jit(solution)/shard_map/ppermute | solution.py:326
  19.3 16.9 %collective-permute-start.6 = (bf16[512,256]{1,0:T(8,128)(2,1)S(1)}, bf16[512,256]{1,0:T(8,128)(2,1)S(1)}, u32[]{:S(2)}, u32[]{:S(2)}) collective-permute-start(bf16[512,256]{1,0:T(8,128)(2,1)S(1)} %pad_maximum_fusion.2.e_ref.refs_0_), channel_id=1, source_target_pairs={{0,128},{32,160},{64,192},{96,224},{128,0},{160,32},{192,64},{224,... | collective-permute-start | bytes 786440 | tf_op jit(solution)/shard_map/ppermute | solution.py:332
  36.2 15.2 %collective-permute-start.12 = (bf16[1024,256]{1,0:T(8,128)(2,1)S(1)}, bf16[1024,256]{1,0:T(8,128)(2,1)S(1)}, u32[]{:S(2)}, u32[]{:S(2)}) collective-permute-start(bf16[1024,256]{1,0:T(8,128)(2,1)S(1)} %pad_maximum_fusion), channel_id=1, source_target_pairs={{0,32},{32,0},{64,96},{96,64},{128,160},{160,128},{192,224},{224,1... | collective-permute-start | bytes 1572872 | tf_op jit(solution)/shard_map/ppermute | solution.py:329
  36.3 15.1 %collective-permute-start.10 = (bf16[512,256]{1,0:T(8,128)(2,1)S(1)}, bf16[512,256]{1,0:T(8,128)(2,1)S(1)}, u32[]{:S(2)}, u32[]{:S(2)}) collective-permute-start(bf16[512,256]{1,0:T(8,128)(2,1)S(1)} %collective-permute-done.7.e_ref.refs_1_), channel_id=1, source_target_pairs={{0,32},{32,0},{64,96},{96,64},{128,160},{160,128},{192,224},{224,1... | collective-permute-start | bytes 786440 | tf_op jit(solution)/shard_map/ppermute | solution.py:329
  36.8 14.6 %collective-permute-start.11 = (bf16[512,256]{1,0:T(8,128)(2,1)S(1)}, bf16[512,256]{1,0:T(8,128)(2,1)S(1)}, u32[]{:S(2)}, u32[]{:S(2)}) collective-permute-start(bf16[512,256]{1,0:T(8,128)(2,1)S(1)} %collective-permute-done.6.refs_3_.refs_4_), channel_id=1, source_target_pairs={{0,32},{32,0},{64,96},{96,64},{128,160},{160,128},{192,224},{224,1... | collective-permute-start | bytes 786440 | tf_op jit(solution)/shard_map/ppermute | solution.py:329
  36.9 55.6 %collective-permute-start.8 = (bf16[512,256]{1,0:T(8,128)(2,1)S(1)}, bf16[512,256]{1,0:T(8,128)(2,1)S(1)}, u32[]{:S(2)}, u32[]{:S(2)}) collective-permute-start(bf16[512,256]{1,0:T(8,128)(2,1)S(1)} %collective-permute-done.7.e_ref.refs_1_), channel_id=1, source_target_pairs={{0,64},{32,96},{64,128},{96,160},{128,192},{160,224},{192,0},{224,... | collective-permute-start | bytes 786440 | tf_op jit(solution)/shard_map/ppermute | solution.py:332
  51.4 41.1 %collective-permute-start.9 = (bf16[512,256]{1,0:T(8,128)(2,1)S(1)}, bf16[512,256]{1,0:T(8,128)(2,1)S(1)}, u32[]{:S(2)}, u32[]{:S(2)}) collective-permute-start(bf16[512,256]{1,0:T(8,128)(2,1)S(1)} %collective-permute-done.7.e_ref.refs_1_), channel_id=1, source_target_pairs={{0,192},{32,224},{64,0},{96,32},{128,64},{160,96},{192,128},{224,1... | collective-permute-start | bytes 786440 | tf_op jit(solution)/shard_map/ppermute | solution.py:332
  92.6 2.2 %collective-permute-start.15 = (bf16[1024,256]{1,0:T(8,128)(2,1)S(1)}, bf16[1024,256]{1,0:T(8,128)(2,1)S(1)}, u32[]{:S(2)}, u32[]{:S(2)}) collective-permute-start(bf16[1024,256]{1,0:T(8,128)(2,1)S(1)} %pad_maximum_fusion.1), channel_id=1, source_target_pairs={{0,32},{32,0},{64,96},{96,64},{128,160},{160,128},{192,224},{224,1... | collective-permute-start | bytes 1572872 | tf_op jit(solution)/shard_map/ppermute | solution.py:329
  92.7 17.2 %collective-permute-start.13 = (bf16[256,256]{1,0:T(8,128)(2,1)S(1)}, bf16[256,256]{1,0:T(8,128)(2,1)S(1)}, u32[]{:S(2)}, u32[]{:S(2)}) collective-permute-start(bf16[256,256]{1,0:T(8,128)(2,1)S(1)} %slice.26), channel_id=1, source_target_pairs={{0,64},{32,96},{64,128},{96,160},{128,192},{160,224},{192,0},{224,... | collective-permute-start | bytes 393224 | tf_op jit(solution)/shard_map/ppermute | solution.py:332
  94.8 15.1 %collective-permute-start.14 = (bf16[256,256]{1,0:T(8,128)(2,1)S(1)}, bf16[256,256]{1,0:T(8,128)(2,1)S(1)}, u32[]{:S(2)}, u32[]{:S(2)}) collective-permute-start(bf16[256,256]{1,0:T(8,128)(2,1)S(1)} %slice.27), channel_id=1, source_target_pairs={{0,192},{32,224},{64,0},{96,32},{128,64},{160,96},{192,128},{224,1... | collective-permute-start | bytes 393224 | tf_op jit(solution)/shard_map/ppermute | solution.py:332
  109.9 1.6 %collective-permute-start.16 = (bf16[512,256]{1,0:T(8,128)(2,1)S(1)}, bf16[512,256]{1,0:T(8,128)(2,1)S(1)}, u32[]{:S(2)}, u32[]{:S(2)}) collective-permute-start(bf16[512,256]{1,0:T(8,128)(2,1)S(1)} %constant_dynamic-update-slice_fusion.refs_5_.refs_0_), channel_id=1, source_target_pairs={{0,32},{32,0},{64,96},{96,64},{128,160},{160,128},{192,224},{224,1... | collective-permute-start | bytes 786440 | tf_op jit(solution)/shard_map/ppermute | solution.py:329
  112.3 17.0 %collective-permute-start.17 = (bf16[256,256]{1,0:T(8,128)(2,1)S(1)}, bf16[256,256]{1,0:T(8,128)(2,1)S(1)}, u32[]{:S(2)}, u32[]{:S(2)}) collective-permute-start(bf16[256,256]{1,0:T(8,128)(2,1)S(1)} %get-tuple-element.140), channel_id=1, source_target_pairs={{0,4},{1,5},{2,6},{3,7},{4,0},{5,1},{6,2},{7,3},{8,12},{9,13},{10,... | collective-permute-start | bytes 393224 | tf_op jit(solution)/shard_map/ppermute | solution.py:326

commit v8 on v7

--- a/solution.py
+++ b/solution.py
@@ -182,11 +182,12 @@
                     allowed,
                 )
 
-        def extra(i):
-            for h in range(2):
-                fast(q_ref, state, h, i * TQ, TQ, x_ref[:, :HD], x_ref[:, HD:])
-
-        loop(0, jnp.where(core == 1, rows // TQ, 0), extra)
+        @pl.when(core == 1)
+        def _():
+            for row in range(0, rows, TQ):
+                for h in range(2):
+                    fast(q_ref, state, h, row, TQ, x_ref[:, :HD], x_ref[:, HD:])
+
         if units:
             units_quick(q_ref, state, kv_ref, count)
 

time: 131 us -> 131 us (level)
  no operation moved by 1% of the time
where the time goes in v8:
time: 131 us; the launch traced here: 130 us
  Pallas kernels  89 us (68%)
  starting transfers between devices  34.6 us (26%)
  waiting for transfers between devices  4.06 us (3%)
    pallas_call x7, Pallas kernels, call(): pl.pallas_call(kernel, in_specs=[SMEM] + [VMEM] * len(arrays), out_specs=...  89 us
    ppermute x7, starting transfers between devices, over_y(): return lax.ppermute(x, 'blk', [(i, (i + 2 * d) % 8) for i in range(8)])  19.6 us
    ppermute x5, starting transfers between devices, over_dec(): return lax.ppermute(x, 'dec', [(i, i ^ m) for i in range(8)])  11.9 us
    ppermute x6, starting transfers between devices, over_core(): return lax.ppermute(x, 'blk', [(i, i ^ 1) for i in range(8)])  3.07 us
  transfers between devices with their start and end apart: 18, of which 3 were waited for; matrix products, arithmetic and copies ran while one was open for 1% of the time, Pallas kernels for 67%

profile of v8, /device:TPU:17, one launch (start us, length us, event | category | flops | bytes accessed | tf_op | source)
XLA Modules:
  0.0 130.5 jit_solution(15577537402370212096)
XLA Ops:
  0.7 0.8 fusion.8
  1.5 2.8 %collective-permute-start.1 = (bf16[128,256]{1,0:T(8,128)(2,1)S(1)}, bf16[128,256]{1,0:T(8,128)(2,1)S(1)}, u32[]{:S(2)}, u32[]{:S(2)}) collective-permute-start(bf16[128,256]{1,0:T(8,128)(2,1)S(1)} %get-tuple-element.146), channel_id=1, source_target_pairs={{0,4},{1,5},{2,6},{3,7},{4,0},{5,1},{6,2},{7,3},{8,12},{9,13},{10,... | collective-permute-start | bytes 196616 | tf_op jit(solution)/shard_map/ppermute | solution.py:327
  4.4 0.9 collective-permute-start.2
  5.5 0.2 compare_reduce_fusion
  5.7 0.2 fusion
  6.2 2.2 %collective-permute-done = bf16[128,256]{1,0:T(8,128)(2,1)S(1)} collective-permute-done((bf16[128,256]{1,0:T(8,128)(2,1)S(1)}, bf16[128,256]{1,0:T(8,128)(2,1)S(1)}, u32[]{:S(2)}, u32[]{:S(2)}) %collective-permute-start) | collective-permute-done | bytes 65568 | tf_op jit(solution)/shard_map/ppermute | solution.py:327
  8.3 0.3 collective-permute-done.2
  8.7 2.2 %collective-permute-start.3 = (bf16[512,256]{1,0:T(8,128)(2,1)S(1)}, bf16[512,256]{1,0:T(8,128)(2,1)S(1)}, u32[]{:S(2)}, u32[]{:S(2)}) collective-permute-start(bf16[512,256]{1,0:T(8,128)(2,1)S(1)} %pad_maximum_fusion.2.e_ref.refs_0_), channel_id=1, source_target_pairs={{0,32},{32,0},{64,96},{96,64},{128,160},{160,128},{192,224},{224,1... | collective-permute-start | bytes 786440 | tf_op jit(solution)/shard_map/ppermute | solution.py:330
  10.9 1.0 collective-permute-start.4
  11.9 0.5 collective-permute-start.5
  12.4 6.9 %collective-permute-start.7 = (bf16[512,256]{1,0:T(8,128)(2,1)S(1)}, bf16[512,256]{1,0:T(8,128)(2,1)S(1)}, u32[]{:S(2)}, u32[]{:S(2)}) collective-permute-start(bf16[512,256]{1,0:T(8,128)(2,1)S(1)} %pad_maximum_fusion.2.e_ref.refs_0_), channel_id=1, source_target_pairs={{0,1},{1,0},{2,3},{3,2},{4,5},{5,4},{6,7},{7,6},{8,9},{9,8},{10,11... | collective-permute-start | bytes 786440 | tf_op jit(solution)/shard_map/ppermute | solution.py:327
  19.3 1.3 %collective-permute-start.6 = (bf16[512,256]{1,0:T(8,128)(2,1)S(1)}, bf16[512,256]{1,0:T(8,128)(2,1)S(1)}, u32[]{:S(2)}, u32[]{:S(2)}) collective-permute-start(bf16[512,256]{1,0:T(8,128)(2,1)S(1)} %pad_maximum_fusion.2.e_ref.refs_0_), channel_id=1, source_target_pairs={{0,128},{32,160},{64,192},{96,224},{128,0},{160,32},{192,64},{224,... | collective-permute-start | bytes 786440 | tf_op jit(solution)/shard_map/ppermute | solution.py:333
  20.6 14.8 %shard_map.83 = (bf16[1024,256]{1,0:T(8,128)(2,1)S(1)}, f32[2048,128]{1,0:T(8,128)S(1)}, f32[2048,1]{1,0:T(8,128)S(1)}, f32[2048,1]{1,0:T(8,128)S(1)}, f32[8,2]{1,0:T(8,128)S(1)}) custom-call(s32[4]{0:T(128)S(1)} %get-tuple-element.76.meta, bf16[1024,256]{1,0:T(8,128)(2,1)S(1)} %copy-done, bf16[512,256]{1,0:T(8,128)(2,1)S(1)} %pad_maximum_fusion.2.e_ref.refs_0_, ...), custom_call_target="tpu_custom_call" | custom-call | tf_op jit(solution)/shard_map/pallas_call | solution.py:310
  35.4 0.8 shard_map.84
  36.4 0.5 collective-permute-start.10
  37.0 14.7 %collective-permute-start.8 = (bf16[512,256]{1,0:T(8,128)(2,1)S(1)}, bf16[512,256]{1,0:T(8,128)(2,1)S(1)}, u32[]{:S(2)}, u32[]{:S(2)}) collective-permute-start(bf16[512,256]{1,0:T(8,128)(2,1)S(1)} %collective-permute-done.7.e_ref.refs_1_), channel_id=1, source_target_pairs={{0,64},{32,96},{64,128},{96,160},{128,192},{160,224},{192,0},{224,... | collective-permute-start | bytes 786440 | tf_op jit(solution)/shard_map/ppermute | solution.py:333
  51.7 41.1 %shard_map.85 = (f32[2048,128]{1,0:T(8,128)S(1)}, f32[2048,1]{1,0:T(8,128)S(1)}, f32[2048,1]{1,0:T(8,128)S(1)}, f32[8,2]{1,0:T(8,128)S(1)}) custom-call(s32[4]{0:T(128)S(1)} %get-tuple-element.91.meta, bf16[1024,256]{1,0:T(8,128)(2,1)S(1)} %get-tuple-element.79.q_ref, ...), custom_call_target="tpu_custom_call", output_to_operand_aliasing={{0}: (9, {}), {1}: (10, {}), {2}: (11, {}), {3}: (12, {})} | custom-call | tf_op jit(solution)/shard_map/pallas_call | solution.py:310
  93.0 2.1 %collective-permute-start.13 = (bf16[256,256]{1,0:T(8,128)(2,1)S(1)}, bf16[256,256]{1,0:T(8,128)(2,1)S(1)}, u32[]{:S(2)}, u32[]{:S(2)}) collective-permute-start(bf16[256,256]{1,0:T(8,128)(2,1)S(1)} %slice.26), channel_id=1, source_target_pairs={{0,64},{32,96},{64,128},{96,160},{128,192},{160,224},{192,0},{224,... | collective-permute-start | bytes 393224 | tf_op jit(solution)/shard_map/ppermute | solution.py:333
  95.1 14.5 %shard_map.86 = (f32[2048,128]{1,0:T(8,128)S(1)}, f32[2048,1]{1,0:T(8,128)S(1)}, f32[2048,1]{1,0:T(8,128)S(1)}, f32[8,2]{1,0:T(8,128)S(1)}) custom-call(s32[4]{0:T(128)S(1)} %get-tuple-element.111.meta, bf16[1024,256]{1,0:T(8,128)(2,1)S(1)} %get-tuple-element.79.q_ref, ...), custom_call_target="tpu_custom_call", output_to_operand_aliasing={{0}: (5, {}), {1}: (6, {}), {2}: (7, {}), {3}: (8, {})} | custom-call | tf_op jit(solution)/shard_map/pallas_call | solution.py:310
  109.8 1.5 %collective-permute-done.16.refs_11_.refs_1_ = bf16[512,256]{1,0:T(8,128)(2,1)S(1)} collective-permute-done((bf16[512,256]{1,0:T(8,128)(2,1)S(1)}, bf16[512,256]{1,0:T(8,128)(2,1)S(1)}, u32[]{:S(2)}, u32[]{:S(2)}) %collective-permute-start.16) | collective-permute-done | bytes 262176 | tf_op jit(solution)/shard_map/ppermute | solution.py:330
  111.3 0.7 shard_map.87
  112.0 1.3 collective-permute-start.17
  113.3 15.7 %shard_map.88 = (f32[2048,128]{1,0:T(8,128)S(1)}, f32[2048,1]{1,0:T(8,128)S(1)}, f32[2048,1]{1,0:T(8,128)S(1)}, f32[8,2]{1,0:T(8,128)S(1)}, bf16[1024,256]{1,0:T(8,128)(2,1)}) custom-call(s32[4]{0:T(128)S(1)} %get-tuple-element.75.meta, ...), custom_call_target="tpu_custom_call", output_to_operand_aliasing={{0}: (4, {}), {1}: (5, {}), {2}: (6, {}), {3}: (7, {})} | custom-call | tf_op jit(solution)/shard_map/pallas_call | solution.py:310
  129.0 1.4 %shard_map.89 = (bf16[256,256]{1,0:T(8,128)(2,1)}, bf16[256,256]{1,0:T(8,128)(2,1)}, f32[2,2]{1,0:T(2,128)}, f32[2,2]{1,0:T(2,128)}) custom-call(s32[3]{0:T(128)S(1)} %pad_add_fusion.meta, bf16[256,256]{1,0:T(8,128)(2,1)S(1)} %get-tuple-element.139.own, bf16[256,256]{1,0:T(8,128)(2,1)S(1)} %collective-permute-done.17.oth), custom_call_target="tpu_custom_call" | custom-call | tf_op jit(solution)/shard_map/pallas_call | solution.py:310
  (43 shorter events, 1.1 us)
Async XLA Ops:
  0.7 4.8 %copy-start.1 = (s32[64]{0:T(128)S(1)}, s32[64]{0:T(128)}, u32[]{:S(2)}) copy-start(s32[64]{0:T(128)} %param.7) | copy-start | bytes 772
  1.5 19.1 %copy-start = (bf16[1024,256]{1,0:T(8,128)(2,1)S(1)}, bf16[1024,256]{1,0:T(8,128)(2,1)}, u32[]{:S(2)}) copy-start(bf16[1024,256]{1,0:T(8,128)(2,1)} %q_ref.1) | copy-start | bytes 1572868
  1.5 6.8 %collective-permute-start.1 = (bf16[128,256]{1,0:T(8,128)(2,1)S(1)}, bf16[128,256]{1,0:T(8,128)(2,1)S(1)}, u32[]{:S(2)}, u32[]{:S(2)}) collective-permute-start(bf16[128,256]{1,0:T(8,128)(2,1)S(1)} %get-tuple-element.146), channel_id=1, source_target_pairs={{0,4},{1,5},{2,6},{3,7},{4,0},{5,1},{6,2},{7,3},{8,12},{9,13},{10,... | collective-permute-start | bytes 196616 | tf_op jit(solution)/shard_map/ppermute | solution.py:327
  4.4 4.3 %collective-permute-start.2 = (bf16[128,256]{1,0:T(8,128)(2,1)S(1)}, bf16[128,256]{1,0:T(8,128)(2,1)S(1)}, u32[]{:S(2)}, u32[]{:S(2)}) collective-permute-start(bf16[128,256]{1,0:T(8,128)(2,1)S(1)} %get-tuple-element.146), channel_id=1, source_target_pairs={{0,6},{1,7},{2,4},{3,5},{4,2},{5,3},{6,0},{7,1},{8,14},{9,15},{10,... | collective-permute-start | bytes 196616 | tf_op jit(solution)/shard_map/ppermute | solution.py:327
  5.2 3.1 %collective-permute-start = (bf16[128,256]{1,0:T(8,128)(2,1)S(1)}, bf16[128,256]{1,0:T(8,128)(2,1)S(1)}, u32[]{:S(2)}, u32[]{:S(2)}) collective-permute-start(bf16[128,256]{1,0:T(8,128)(2,1)S(1)} %get-tuple-element.145), channel_id=1, source_target_pairs={{0,2},{1,3},{2,0},{3,1},{4,6},{5,7},{6,4},{7,5},{8,10},{9,11},{10,... | collective-permute-start | bytes 196616 | tf_op jit(solution)/shard_map/ppermute | solution.py:327
  8.7 10.6 %collective-permute-start.3 = (bf16[512,256]{1,0:T(8,128)(2,1)S(1)}, bf16[512,256]{1,0:T(8,128)(2,1)S(1)}, u32[]{:S(2)}, u32[]{:S(2)}) collective-permute-start(bf16[512,256]{1,0:T(8,128)(2,1)S(1)} %pad_maximum_fusion.2.e_ref.refs_0_), channel_id=1, source_target_pairs={{0,32},{32,0},{64,96},{96,64},{128,160},{160,128},{192,224},{224,1... | collective-permute-start | bytes 786440 | tf_op jit(solution)/shard_map/ppermute | solution.py:330
  10.9 24.5 %collective-permute-start.4 = (bf16[512,256]{1,0:T(8,128)(2,1)S(1)}, bf16[512,256]{1,0:T(8,128)(2,1)S(1)}, u32[]{:S(2)}, u32[]{:S(2)}) collective-permute-start(bf16[512,256]{1,0:T(8,128)(2,1)S(1)} %pad_maximum_fusion.2.e_ref.refs_0_), channel_id=1, source_target_pairs={{0,64},{32,96},{64,128},{96,160},{128,192},{160,224},{192,0},{224,... | collective-permute-start | bytes 786440 | tf_op jit(solution)/shard_map/ppermute | solution.py:333
  11.9 23.5 %collective-permute-start.5 = (bf16[512,256]{1,0:T(8,128)(2,1)S(1)}, bf16[512,256]{1,0:T(8,128)(2,1)S(1)}, u32[]{:S(2)}, u32[]{:S(2)}) collective-permute-start(bf16[512,256]{1,0:T(8,128)(2,1)S(1)} %pad_maximum_fusion.2.e_ref.refs_0_), channel_id=1, source_target_pairs={{0,192},{32,224},{64,0},{96,32},{128,64},{160,96},{192,128},{224,1... | collective-permute-start | bytes 786440 | tf_op jit(solution)/shard_map/ppermute | solution.py:333
  12.4 23.8 %collective-permute-start.7 = (bf16[512,256]{1,0:T(8,128)(2,1)S(1)}, bf16[512,256]{1,0:T(8,128)(2,1)S(1)}, u32[]{:S(2)}, u32[]{:S(2)}) collective-permute-start(bf16[512,256]{1,0:T(8,128)(2,1)S(1)} %pad_maximum_fusion.2.e_ref.refs_0_), channel_id=1, source_target_pairs={{0,1},{1,0},{2,3},{3,2},{4,5},{5,4},{6,7},{7,6},{8,9},{9,8},{10,11... | collective-permute-start | bytes 786440 | tf_op jit(solution)/shard_map/ppermute | solution.py:327
  19.3 16.9 %collective-permute-start.6 = (bf16[512,256]{1,0:T(8,128)(2,1)S(1)}, bf16[512,256]{1,0:T(8,128)(2,1)S(1)}, u32[]{:S(2)}, u32[]{:S(2)}) collective-permute-start(bf16[512,256]{1,0:T(8,128)(2,1)S(1)} %pad_maximum_fusion.2.e_ref.refs_0_), channel_id=1, source_target_pairs={{0,128},{32,160},{64,192},{96,224},{128,0},{160,32},{192,64},{224,... | collective-permute-start | bytes 786440 | tf_op jit(solution)/shard_map/ppermute | solution.py:333
  36.3 15.5 %collective-permute-start.12 = (bf16[1024,256]{1,0:T(8,128)(2,1)S(1)}, bf16[1024,256]{1,0:T(8,128)(2,1)S(1)}, u32[]{:S(2)}, u32[]{:S(2)}) collective-permute-start(bf16[1024,256]{1,0:T(8,128)(2,1)S(1)} %pad_maximum_fusion), channel_id=1, source_target_pairs={{0,32},{32,0},{64,96},{96,64},{128,160},{160,128},{192,224},{224,1... | collective-permute-start | bytes 1572872 | tf_op jit(solution)/shard_map/ppermute | solution.py:330
  36.4 15.3 %collective-permute-start.10 = (bf16[512,256]{1,0:T(8,128)(2,1)S(1)}, bf16[512,256]{1,0:T(8,128)(2,1)S(1)}, u32[]{:S(2)}, u32[]{:S(2)}) collective-permute-start(bf16[512,256]{1,0:T(8,128)(2,1)S(1)} %collective-permute-done.7.e_ref.refs_1_), channel_id=1, source_target_pairs={{0,32},{32,0},{64,96},{96,64},{128,160},{160,128},{192,224},{224,1... | collective-permute-start | bytes 786440 | tf_op jit(solution)/shard_map/ppermute | solution.py:330
  36.9 14.9 %collective-permute-start.11 = (bf16[512,256]{1,0:T(8,128)(2,1)S(1)}, bf16[512,256]{1,0:T(8,128)(2,1)S(1)}, u32[]{:S(2)}, u32[]{:S(2)}) collective-permute-start(bf16[512,256]{1,0:T(8,128)(2,1)S(1)} %collective-permute-done.6.refs_3_.refs_4_), channel_id=1, source_target_pairs={{0,32},{32,0},{64,96},{96,64},{128,160},{160,128},{192,224},{224,1... | collective-permute-start | bytes 786440 | tf_op jit(solution)/shard_map/ppermute | solution.py:330
  37.0 55.8 %collective-permute-start.8 = (bf16[512,256]{1,0:T(8,128)(2,1)S(1)}, bf16[512,256]{1,0:T(8,128)(2,1)S(1)}, u32[]{:S(2)}, u32[]{:S(2)}) collective-permute-start(bf16[512,256]{1,0:T(8,128)(2,1)S(1)} %collective-permute-done.7.e_ref.refs_1_), channel_id=1, source_target_pairs={{0,64},{32,96},{64,128},{96,160},{128,192},{160,224},{192,0},{224,... | collective-permute-start | bytes 786440 | tf_op jit(solution)/shard_map/ppermute | solution.py:333
  51.7 41.1 %collective-permute-start.9 = (bf16[512,256]{1,0:T(8,128)(2,1)S(1)}, bf16[512,256]{1,0:T(8,128)(2,1)S(1)}, u32[]{:S(2)}, u32[]{:S(2)}) collective-permute-start(bf16[512,256]{1,0:T(8,128)(2,1)S(1)} %collective-permute-done.7.e_ref.refs_1_), channel_id=1, source_target_pairs={{0,192},{32,224},{64,0},{96,32},{128,64},{160,96},{192,128},{224,1... | collective-permute-start | bytes 786440 | tf_op jit(solution)/shard_map/ppermute | solution.py:333
  92.9 2.2 %collective-permute-start.15 = (bf16[1024,256]{1,0:T(8,128)(2,1)S(1)}, bf16[1024,256]{1,0:T(8,128)(2,1)S(1)}, u32[]{:S(2)}, u32[]{:S(2)}) collective-permute-start(bf16[1024,256]{1,0:T(8,128)(2,1)S(1)} %pad_maximum_fusion.1), channel_id=1, source_target_pairs={{0,32},{32,0},{64,96},{96,64},{128,160},{160,128},{192,224},{224,1... | collective-permute-start | bytes 1572872 | tf_op jit(solution)/shard_map/ppermute | solution.py:330
  93.0 16.6 %collective-permute-start.13 = (bf16[256,256]{1,0:T(8,128)(2,1)S(1)}, bf16[256,256]{1,0:T(8,128)(2,1)S(1)}, u32[]{:S(2)}, u32[]{:S(2)}) collective-permute-start(bf16[256,256]{1,0:T(8,128)(2,1)S(1)} %slice.26), channel_id=1, source_target_pairs={{0,64},{32,96},{64,128},{96,160},{128,192},{160,224},{192,0},{224,... | collective-permute-start | bytes 393224 | tf_op jit(solution)/shard_map/ppermute | solution.py:333
  95.1 14.5 %collective-permute-start.14 = (bf16[256,256]{1,0:T(8,128)(2,1)S(1)}, bf16[256,256]{1,0:T(8,128)(2,1)S(1)}, u32[]{:S(2)}, u32[]{:S(2)}) collective-permute-start(bf16[256,256]{1,0:T(8,128)(2,1)S(1)} %slice.27), channel_id=1, source_target_pairs={{0,192},{32,224},{64,0},{96,32},{128,64},{160,96},{192,128},{224,1... | collective-permute-start | bytes 393224 | tf_op jit(solution)/shard_map/ppermute | solution.py:333
  109.7 1.6 %collective-permute-start.16 = (bf16[512,256]{1,0:T(8,128)(2,1)S(1)}, bf16[512,256]{1,0:T(8,128)(2,1)S(1)}, u32[]{:S(2)}, u32[]{:S(2)}) collective-permute-start(bf16[512,256]{1,0:T(8,128)(2,1)S(1)} %constant_dynamic-update-slice_fusion.refs_5_.refs_0_), channel_id=1, source_target_pairs={{0,32},{32,0},{64,96},{96,64},{128,160},{160,128},{192,224},{224,1... | collective-permute-start | bytes 786440 | tf_op jit(solution)/shard_map/ppermute | solution.py:330
  112.0 17.0 %collective-permute-start.17 = (bf16[256,256]{1,0:T(8,128)(2,1)S(1)}, bf16[256,256]{1,0:T(8,128)(2,1)S(1)}, u32[]{:S(2)}, u32[]{:S(2)}) collective-permute-start(bf16[256,256]{1,0:T(8,128)(2,1)S(1)} %get-tuple-element.140), channel_id=1, source_target_pairs={{0,4},{1,5},{2,6},{3,7},{4,0},{5,1},{6,2},{7,3},{8,12},{9,13},{10,... | collective-permute-start | bytes 393224 | tf_op jit(solution)/shard_map/ppermute | solution.py:327
